TPU v7x, 32 devices: a whole 2x2x4 slice. The times are simulated.
32 devices in a mesh: groups: 2 (over y), sec: 4 (over z), grid: 4 (over x, core).
Axes of the slice: x: 2, y: 2, z: 4, core: 2. Of those that a mesh axis runs over, the one named last changes fastest.
Arguments:
- modes: bfloat16 [8, 4096, 1024], P(('groups', 'sec'), 'grid'), parts along dimension 0
- exit_modes: bfloat16 [8192, 1024], P(('groups', 'grid')), parts along dimension 0
- pattern: int32 [8, 8, 2], P(('groups', 'sec')), parts along dimension 0, may hold values 0 or 1
- attenuation: float32 [8, 1024], P(('groups', 'sec')), parts along dimension 0, may hold values from 0.96 to 1
- reflection: float32 [8, 1024], P(('groups', 'sec')), parts along dimension 0, may hold values from -0.15 to 0.15
Outputs:
- cascade: float32 [6, 8, 128, 128], P('groups', 'grid', 'sec'), parts along dimension 0
There are 2 independent parts, one for each index of `groups`. A program takes and returns all parts, laid end to end along the dimension named above; each array names one. Nothing has to cross between parts.
All inputs are finite; a program needn't handle non-finite values. No bound on the sum of `pattern` on one device may be relied on, other than what follows from the above.
Results may differ from a plain program's by a relative error of at most 0.0003.
Values may be sent and summed in bfloat16 or wider, within the bound.
No kernel may reach another device: no remote copies, remote signals or barrier semaphores. Data moves between devices by JAX's collectives and lax.ppermute only.
A program may use at most 64 MiB of HBM per device.

v0:
```python
import jax
import jax.numpy as jnp
from jax import lax
from jax.sharding import PartitionSpec as P


def passed_along(block, axis, distance):
    devices = range(lax.axis_size(axis))
    route = [(i - distance, i) for i in devices if i - distance in devices]
    return lax.ppermute(block, axis, route)


def from_partner(value, axis, stride):
    return lax.ppermute(value, axis, [(i, i ^ 1 << stride) for i in range(lax.axis_size(axis))])


def batch_mul(left_side, right_side):
    product = jnp.einsum("kij,kjl->kil", left_side, right_side, precision=lax.Precision.HIGHEST)
    return lax.optimization_barrier(product)


def flipped(matrix):
    return jnp.swapaxes(matrix, 1, 2)


def star_product(first, second):
    trans_a, front_a, back_a = (first[0], first[1], first[2])
    trans_b, front_b, back_b = (second[0], second[1], second[2])
    bounce = batch_mul(back_a, front_b)
    bounce_sq = batch_mul(bounce, bounce)
    inner = trans_a + batch_mul(bounce, trans_a)
    inner = inner + batch_mul(bounce_sq, inner)
    trans_new = batch_mul(trans_b, inner)
    front_new = front_a + batch_mul(flipped(trans_a), batch_mul(front_b, inner))
    reverse_b = flipped(trans_b)
    behind = reverse_b + batch_mul(flipped(bounce), reverse_b)
    behind = behind + batch_mul(flipped(bounce_sq), behind)
    back_new = back_b + batch_mul(trans_b, batch_mul(back_a, behind))
    return jnp.stack([trans_new, front_new, back_new])


def tile_mask(flags, width):
    tiles = jnp.arange(width) // (width // 2)
    upper = (tiles[:, None] < tiles[None, :]).astype(jnp.float32)
    lower = (tiles[:, None] > tiles[None, :]).astype(jnp.float32)
    flag_up = flags[:, 0].astype(jnp.float32)[:, None, None]
    flag_low = flags[:, 1].astype(jnp.float32)[:, None, None]
    return 1.0 - upper - lower + upper * flag_up + lower * flag_low


def unit_matrices(intersection, decay_now, mirror):
    passing = jnp.sqrt(1.0 - mirror * mirror)
    trans_unit = passing[:, :, None] * intersection * decay_now[:, None, :]
    ident = jnp.eye(intersection.shape[1], dtype=jnp.float32)
    front_unit = ident[None] * (decay_now * decay_now * mirror)[:, :, None]
    back_unit = -ident[None] * mirror[:, :, None]
    return jnp.stack([trans_unit, front_unit, back_unit])


def intersection_terms(this_fields, next_fields, flags, classes, width):
    fields_a = jnp.swapaxes(this_fields.reshape(this_fields.shape[0], classes, width), 0, 1)
    fields_b = jnp.swapaxes(next_fields.reshape(next_fields.shape[0], classes, width), 0, 1)
    summed = jnp.einsum("kgm,kgn->kmn", fields_a, fields_b, preferred_element_type=jnp.float32)
    summed = lax.optimization_barrier(summed)
    return summed * tile_mask(flags, width)


def body(modes, exit_modes, pattern, attenuation, reflection):
    sec_count = lax.axis_size("sec")
    sec_index = lax.axis_index("sec")
    grid_count = lax.axis_size("grid")
    grid_index = lax.axis_index("grid")
    local_count = modes.shape[0]
    classes = pattern.shape[1]
    width = modes.shape[2] // classes
    class_share = classes // grid_count
    arriving = passed_along(modes[0], "sec", -1)
    partials = []
    following = jnp.where(sec_index == sec_count - 1, exit_modes, arriving)
    partials.append(
        intersection_terms(
            modes[local_count - 1], following, pattern[local_count - 1], classes, width
        )
    )
    stacked = jnp.stack(partials)
    decay_all = attenuation.reshape(local_count, classes, width)
    mirror_all = reflection.reshape(local_count, classes, width)
    intersections = lax.psum(stacked, "grid")
    merged = unit_matrices(intersections[0], decay_all[0], mirror_all[0])
    level_count = sec_count.bit_length() - 1
    for level_index in range(level_count):
        partner = from_partner(merged, "sec", level_index)
        upper_half = jnp.right_shift(sec_index, level_index) & 1 == 1
        merged = star_product(
            jnp.where(upper_half, partner, merged), jnp.where(upper_half, merged, partner)
        )
    row_count = width // sec_count
    merged = lax.dynamic_slice_in_dim(merged, sec_index * row_count, row_count, 2)
    return lax.dynamic_slice_in_dim(merged, grid_index * class_share, class_share, 1)


def solution(mesh):
    in_specs = (
        P(("groups", "sec"), "grid", None),
        P(("groups", "grid"), None),
        P(("groups", "sec"), None, None),
        P(("groups", "sec"), None),
        P(("groups", "sec"), None),
    )
    out_specs = P("groups", "grid", "sec", None)
    return jax.shard_map(body, mesh=mesh, in_specs=in_specs, out_specs=out_specs, check_vma=False)
```

profile of v0, /device:TPU:0, one launch (start us, length us, event | category | flops | bytes accessed | tf_op | source)
XLA Modules:
  0.0 280.8 jit_solution(2406137203251884640)
XLA Ops:
  7.9 3.6 %copy.56 = bf16[128,8,8,128]{3,2,1,0:T(8,128)(2,1)} copy(bf16[128,8,8,128]{3,1,2,0:T(8,128)(2,1)} %bitcast.148) | data formatting | bytes 4194304
  11.7 45.7 %collective-permute-done = bf16[1024,1024]{1,0:T(8,128)(2,1)} collective-permute-done((bf16[1024,1024]{1,0:T(8,128)(2,1)}, bf16[1024,1024]{1,0:T(8,128)(2,1)}, u32[]{:S(2)}, u32[]{:S(2)}) %collective-permute-start) | collective-permute-done | bytes 2097184 | tf_op jit(solution)/shard_map/ppermute | solution.py:10
  59.2 2.6 copy.55
  61.8 3.1 %fusion.3 = f32[8,128,128]{1,2,0:T(8,128)S(1)} fusion(bf16[8,1024,128]{1,2,0:T(8,128)(2,1)} %bitcast.150, bf16[1024,8,128]{2,1,0:T(8,128)(2,1)} %bitcast.149), kind=kOutput, calls=%fused_computation.9 | convolution fusion | flops 268435456 | bytes 4718592 | tf_op jit(solution)/shard_map/kgm,kgn->kmn/dot_general | solution.py:63
  66.1 33.6 %all-reduce.2.cloned.1.call-done = f32[1,8,128,128]{2,3,1,0:T(8,128)} async-done(((f32[1,8,128,128]{2,3,1,0:T(8,128)}), f32[1,8,128,128]{2,3,1,0:T(8,128)}) %all-reduce.2.cloned.1.call-update) | async-done | bytes 524304 | tf_op jit(solution)/shard_map/psum | solution.py:88
  103.2 33.6 %collective-permute-done.1 = f32[3,8,128,128]{2,3,1,0:T(8,128)} collective-permute-done((f32[3,8,128,128]{2,3,1,0:T(8,128)S(1)}, f32[3,8,128,128]{2,3,1,0:T(8,128)}, u32[]{:S(2)}, u32[]{:S(2)}) %collective-permute-start.1) | collective-permute-done | bytes 1572896 | tf_op jit(solution)/shard_map/ppermute | solution.py:14
  136.8 2.1 broadcast_select_fusion.2
  139.9 2.0 fusion.36
  143.4 2.0 copy.11
  145.4 3.2 %fusion.62 = f32[8,128,128]{2,1,0:T(8,128)} fusion(f32[8,128,128]{2,1,0:T(8,128)} %fusion.64, f32[8,128,128]{1,2,0:T(8,128)} %copy.11, f32[3,8,128,128]{2,3,1,0:T(8,128)S(1)} %get-tuple-element.8), kind=kOutput, calls=%fused_computation.93 | convolution fusion | flops 201457664 | bytes 2097152 | tf_op jit(solution)/shard_map/kij,kjl->kil/dot_general | solution.py:18
  148.7 2.1 copy.13
  150.7 3.1 %fusion.24 = f32[8,128,128]{2,1,0:T(8,128)} fusion(f32[3,8,128,128]{2,3,1,0:T(8,128)S(1)} %get-tuple-element.7, f32[8,128,128]{1,2,0:T(8,128)} %copy.13, f32[8,128,128]{1,2,0:T(8,128)} %copy.11, f32[3,8,128,128]{2,3,1,0:T(8,128)S(1)} %get-tuple-element.8), kind=kOutput, calls=%fused_computation.44 | convolution fusion | flops 201588736 | bytes 2621440 | tf_op jit(solution)/shard_map/kij,kjl->kil/dot_general | solution.py:18
  157.5 2.0 copy.16
  159.5 2.5 fusion.34
  162.0 2.0 copy.17
  168.1 2.0 fusion.22
  172.3 2.7 collective-permute-start.2
  175.0 66.3 %collective-permute-done.2 = f32[3,8,128,128]{2,3,1,0:T(8,128)} collective-permute-done((f32[3,8,128,128]{2,3,1,0:T(8,128)S(1)}, f32[3,8,128,128]{2,3,1,0:T(8,128)}, u32[]{:S(2)}, u32[]{:S(2)}) %collective-permute-start.2) | collective-permute-done | bytes 1572896 | tf_op jit(solution)/shard_map/ppermute | solution.py:14
  241.3 2.1 broadcast_select_fusion.3
  249.7 2.1 copy.25
  251.8 3.2 %fusion.58 = f32[8,128,128]{2,1,0:T(8,128)} fusion(f32[8,128,128]{2,1,0:T(8,128)} %fusion.65, f32[8,128,128]{1,2,0:T(8,128)} %copy.25, f32[3,8,128,128]{2,3,1,0:T(8,128)S(1)} %get-tuple-element.5), kind=kOutput, calls=%fused_computation.92 | convolution fusion | flops 201457664 | bytes 2097152 | tf_op jit(solution)/shard_map/kij,kjl->kil/dot_general | solution.py:18
  255.0 2.1 copy.27
  257.1 3.1 %fusion.33 = f32[8,128,128]{2,1,0:T(8,128)} fusion(f32[3,8,128,128]{2,3,1,0:T(8,128)S(1)} %get-tuple-element.6, f32[8,128,128]{1,2,0:T(8,128)} %copy.27, f32[8,128,128]{1,2,0:T(8,128)} %copy.25, f32[3,8,128,128]{2,3,1,0:T(8,128)S(1)} %get-tuple-element.5), kind=kOutput, calls=%fused_computation.55 | convolution fusion | flops 201588736 | bytes 2621440 | tf_op jit(solution)/shard_map/kij,kjl->kil/dot_general | solution.py:18
  265.9 2.1 copy.35
  (85 shorter events, 38.2 us)
Async XLA Ops:
  6.5 93.2 %all-reduce.2.cloned.1.call-start = ((), (), s32[]{:S(2)}) async-start(), calls=%async_computation | async-start | bytes 1048576 | tf_op jit(solution)/shard_map/psum | solution.py:88
  6.5 50.9 %collective-permute-start = (bf16[1024,1024]{1,0:T(8,128)(2,1)}, bf16[1024,1024]{1,0:T(8,128)(2,1)}, u32[]{:S(2)}, u32[]{:S(2)}) collective-permute-start(bf16[1024,1024]{1,0:T(8,128)(2,1)} %bitcast.147), channel_id=1, source_target_pairs={{4,0},{8,4},{12,8},{5,1},{9,5},{13,9},{6,2},{10,6},{14,10},{7,3},{... | collective-permute-start | bytes 6291464 | tf_op jit(solution)/shard_map/ppermute | solution.py:10
  7.8 3.6 %copy-start.21 = (s32[1,8,2]{1,2,0:T(2,128)S(1)}, s32[1,8,2]{1,2,0:T(2,128)}, u32[]{:S(2)}) copy-start(s32[1,8,2]{1,2,0:T(2,128)} %param.7) | copy-start | bytes 196
  7.8 3.6 %copy-start.19 = (f32[1,1024]{1,0:T(1,128)S(1)}, f32[1,1024]{1,0:T(1,128)}, u32[]{:S(2)}) copy-start(f32[1,1024]{1,0:T(1,128)} %param.9) | copy-start | bytes 12292
  7.9 3.6 %copy-start.20 = (f32[1,1024]{1,0:T(1,128)S(1)}, f32[1,1024]{1,0:T(1,128)}, u32[]{:S(2)}) copy-start(f32[1,1024]{1,0:T(1,128)} %param.8) | copy-start | bytes 12292
  66.1 35.0 %copy-start.8 = (f32[1,8,128,128]{2,3,1,0:T(8,128)}, f32[1,8,128,128]{2,3,1,0:T(8,128)S(1)}, u32[]{:S(2)}) copy-start(f32[1,8,128,128]{2,3,1,0:T(8,128)S(1)} %get-tuple-element.15) | copy-start | bytes 1572868
  66.1 35.0 %copy-start.9 = (f32[1,8,128,128]{2,3,1,0:T(8,128)}, f32[1,8,128,128]{2,3,1,0:T(8,128)S(1)}, u32[]{:S(2)}) copy-start(f32[1,8,128,128]{2,3,1,0:T(8,128)S(1)} %get-tuple-element.16) | copy-start | bytes 1572868
  101.7 35.1 %collective-permute-start.1 = (f32[3,8,128,128]{2,3,1,0:T(8,128)S(1)}, f32[3,8,128,128]{2,3,1,0:T(8,128)}, u32[]{:S(2)}, u32[]{:S(2)}) collective-permute-start(f32[3,8,128,128]{2,3,1,0:T(8,128)S(1)} %pad_maximum_fusion), channel_id=1, source_target_pairs={{0,4},{4,0},{8,12},{12,8},{1,5},{5,1},{9,13},{13,9},{2,6},{6,2},{1... | collective-permute-start | bytes 4718600 | tf_op jit(solution)/shard_map/ppermute | solution.py:14
  139.9 2.0 copy-start
  150.7 3.1 %copy-start.2 = (f32[8,128,128]{1,2,0:T(8,128)S(1)}, f32[8,128,128]{1,2,0:T(8,128)}, u32[]{:S(2)}) copy-start(f32[8,128,128]{1,2,0:T(8,128)} %copy.11) | copy-start | bytes 1572868
  150.7 3.1 %copy-start.4 = (f32[8,128,128]{1,2,0:T(8,128)S(1)}, f32[8,128,128]{1,2,0:T(8,128)}, u32[]{:S(2)}) copy-start(f32[8,128,128]{1,2,0:T(8,128)} %copy.13) | copy-start | bytes 1572868
  153.8 1.8 copy-start.1
  164.1 2.0 copy-start.11
  164.1 2.0 copy-start.14
  170.1 1.4 copy-start.6
  170.1 1.4 copy-start.12
  172.3 69.0 %collective-permute-start.2 = (f32[3,8,128,128]{2,3,1,0:T(8,128)S(1)}, f32[3,8,128,128]{2,3,1,0:T(8,128)}, u32[]{:S(2)}, u32[]{:S(2)}) collective-permute-start(f32[3,8,128,128]{2,3,1,0:T(8,128)S(1)} %pad_maximum_fusion.1), channel_id=1, source_target_pairs={{0,8},{4,12},{8,0},{12,4},{1,9},{5,13},{9,1},{13,5},{2,10},{6,14},... | collective-permute-start | bytes 4718600 | tf_op jit(solution)/shard_map/ppermute | solution.py:14
  257.1 3.1 %copy-start.3 = (f32[8,128,128]{1,2,0:T(8,128)S(1)}, f32[8,128,128]{1,2,0:T(8,128)}, u32[]{:S(2)}) copy-start(f32[8,128,128]{1,2,0:T(8,128)} %copy.25) | copy-start | bytes 1572868
  257.1 3.1 %copy-start.5 = (f32[8,128,128]{1,2,0:T(8,128)S(1)}, f32[8,128,128]{1,2,0:T(8,128)}, u32[]{:S(2)}) copy-start(f32[8,128,128]{1,2,0:T(8,128)} %copy.27) | copy-start | bytes 1572868
  260.2 1.8 copy-start.10
  260.2 1.8 copy-start.15
  267.9 2.0 copy-start.16
  270.6 2.2 copy-start.18
  271.6 1.4 copy-start.17
  (2 other events, 1.6 us)
Sparse Core Ops, SparseCore 0:
  66.1 33.5 all-reduce.1
where the time goes:
time: 282 us; the launch traced here: 281 us
  waiting for transfers between devices  179 us (63%)
  matrix products  43.1 us (15%)
  local copies, waits for them, and re-layouts  25.1 us (9%)
  other arithmetic  14.2 us (5%)
  between operations  13.8 us (5%)
  starting transfers between devices  5.45 us (2%)
    ppermute x2, waiting for transfers between devices, from_partner(): lax.ppermute(value, axis, [(i, i ^ 1 << stride) for i in range(lax.axis_s...  99.9 us
    ppermute x1, waiting for transfers between devices, passed_along(): return lax.ppermute(block, axis, route)  45.7 us
    dot_general x22, matrix products, batch_mul(): jnp.einsum('kij,kjl->kil', left_side, right_side, precision=lax.Precision...  39.9 us
    psum x1, waiting for transfers between devices, body(): intersections = lax.psum(stacked, 'grid')  33.6 us
    optimization_barrier x10, local copies, waits for them, and re-layouts, batch_mul(): return lax.optimization_barrier(product)  16.9 us
  transfers between devices with their start and end apart: 4, of which 4 were waited for; matrix products, arithmetic and copies ran while one was open for 1% of the time, Pallas kernels for 0%

commit v1 on v0

v1 whole, which is shorter than its diff:
```python
import functools

import jax
import jax.numpy as jnp
from jax import lax
from jax.experimental import pallas as pl
from jax.experimental.pallas import tpu as pltpu
from jax.sharding import PartitionSpec as P

BLOCK = 4
AXES = ("sec", "grid")


def halves(matrix):
    high = matrix.astype(jnp.bfloat16)
    return high, (matrix - high.astype(jnp.float32)).astype(jnp.bfloat16)


def mul(left, right, flip=False):
    dims = (((1,), (1 if flip else 0,)), ((), ()))

    def dot(a, b):
        return lax.dot_general(a, b, dims, preferred_element_type=jnp.float32)

    return dot(left[0], right[0]) + (dot(left[0], right[1]) + dot(left[1], right[0]))


def star_body(meta, *refs, orders, rows):
    terms, last, aux = refs[:BLOCK], refs[BLOCK], refs[BLOCK + 1 : 2 * BLOCK + 1]
    out, tbuf, abuf, rbuf = refs[2 * BLOCK + 1 :]
    for slot in range(BLOCK):
        tbuf[meta[slot]] = terms[slot][...]
        abuf[meta[BLOCK + slot]] = aux[slot][...]
    tbuf[BLOCK - 1] = last[...]
    width = out.shape[-1]
    picked = pl.ds(pl.multiple_of(meta[2 * BLOCK], 8), rows)
    row = lax.broadcasted_iota(jnp.int32, (width, width), 0)
    col = lax.broadcasted_iota(jnp.int32, (width, width), 1)
    part_row = lax.broadcasted_iota(jnp.int32, (rows, width), 0) + meta[2 * BLOCK]
    part_col = lax.broadcasted_iota(jnp.int32, (rows, width), 1)
    upper = jnp.logical_and(row < width // 2, col >= width // 2)
    lower = jnp.logical_and(row >= width // 2, col < width // 2)

    def diag(vector):
        return jnp.where(row == col, vector, 0.0)

    def part_diag(vector):
        return jnp.where(part_row == part_col, vector, 0.0)

    for order in range(orders):
        trans, front, back = [], [], []
        for sec in range(BLOCK):
            decay = abuf[sec, order, 0:1, :]
            mirror = abuf[sec, order, 1:2, :]
            mask = jnp.where(
                upper, abuf[sec, order, 2:3, :], jnp.where(lower, abuf[sec, order, 3:4, :], 1.0)
            )
            passing = jnp.broadcast_to(jnp.sqrt(1.0 - mirror * mirror), (width, width)).T
            trans.append(passing * (tbuf[sec, order] * mask) * decay)
            front.append(decay * decay * mirror)
            back.append(-mirror)
        bounce_a = back[0] * front[1]
        bounce_b = back[2] * front[3]
        gain_a = (1.0 + bounce_a * bounce_a) * (1.0 + bounce_a)
        gain_b = (1.0 + bounce_b * bounce_b) * (1.0 + bounce_b)
        flip_0 = trans[0].T
        flip_2 = trans[2].T
        rbuf[0] = flip_0
        rbuf[1] = trans[3]
        flip_0_part = rbuf[0, picked, :]
        trans_3_part = rbuf[1, picked, :]
        s0, s1, s2, s3 = [halves(t) for t in trans]
        trans_a = halves(mul(halves(trans[1] * gain_a), s0))
        back_a = halves(diag(back[1]) + mul(halves(trans[1] * (back[0] * gain_a)), s1, True))
        front_b = halves(diag(front[2]) + mul(halves(flip_2 * (front[3] * gain_b)), s2))
        trans_b = halves(mul(halves(trans[3] * gain_b), s2))
        flip_a_part = halves(mul(halves(flip_0_part * gain_a), s1, True))
        trans_b_part = mul(halves(trans_3_part * gain_b), s2)
        front_a_part = part_diag(front[0]) + mul(halves(flip_0_part * (front[1] * gain_a)), s0)
        back_b_part = part_diag(back[3]) + mul(halves(trans_3_part * (back[2] * gain_b)), s3, True)
        bounce = halves(mul(back_a, front_b))
        ahead = jnp.concatenate([trans_b_part, mul(flip_a_part, front_b)], axis=0)
        behind = mul(halves(trans_b_part), back_a)
        ahead = ahead + mul(halves(mul(halves(ahead), bounce)), bounce)
        behind = behind + mul(halves(mul(halves(behind), bounce, True)), bounce, True)
        ahead = ahead + mul(halves(ahead), bounce)
        behind = behind + mul(halves(behind), bounce, True)
        ahead = mul(halves(ahead), trans_a)
        out[0, order] = ahead[:rows]
        out[1, order] = front_a_part + ahead[rows:]
        out[2, order] = back_b_part + mul(halves(behind), trans_b, True)


def star_of_four(meta, terms, last, aux, rows):
    orders, width = last.shape[0], last.shape[-1]
    vmem = pl.BlockSpec(memory_space=pltpu.VMEM)
    return pl.pallas_call(
        functools.partial(star_body, orders=orders, rows=rows),
        out_shape=jax.ShapeDtypeStruct((3, orders, rows, width), jnp.float32),
        in_specs=[pl.BlockSpec(memory_space=pltpu.SMEM)] + [vmem] * (2 * BLOCK + 1),
        out_specs=vmem,
        scratch_shapes=[
            pltpu.VMEM((BLOCK + 1, orders, width, width), jnp.float32),
            pltpu.VMEM((BLOCK, orders) + aux[0].shape[1:], jnp.float32),
            pltpu.VMEM((2, width, width), jnp.float32),
        ],
        cost_estimate=pl.CostEstimate(
            flops=orders * 120 * width**3, bytes_accessed=orders * 8 * 4 * width**2, transcendentals=0
        ),
    )(meta, *terms, last, *aux)


def tall_dot(left, right):
    dims = (((0,), (0,)), ((), ()))
    return lax.dot_general(left, right, dims, preferred_element_type=jnp.float32)


def keep(outs, turn, item, value):
    for index, out in enumerate(outs):
        @pl.when(turn == index)
        def _():
            out[item] = value


def exit_body(place, own, after, *outs):
    keep(outs, pl.program_id(0), pl.program_id(1), tall_dot(own[...], after[...]))


def inner_body(place, own, before, after, *outs):
    turn, item = pl.program_id(0), pl.program_id(1)
    up = lax.rem(lax.rem(place[0] + turn, len(outs)), 2) == 0
    left = jnp.where(up, before[...], own[...])
    right = jnp.where(up, own[...], after[...])
    keep(outs, turn, item, tall_dot(left, right))


def partial_sums(body, place, operands, columns, count, orders, width):
    points = operands[0].shape[0]
    spot = lambda turn, place: lax.rem(place[0] + turn, count)
    specs = [
        pl.BlockSpec((points, width), lambda turn, item, place, col=col: (0, col(spot(turn, place), item)))
        for col in columns
    ]
    whole = pl.BlockSpec((orders, width, width), lambda turn, item, place: (0, 0, 0))
    return pl.pallas_call(
        body,
        out_shape=[jax.ShapeDtypeStruct((orders, width, width), jnp.float32)] * count,
        grid_spec=pltpu.PrefetchScalarGridSpec(
            num_scalar_prefetch=1, grid=(count, orders), in_specs=specs, out_specs=[whole] * count
        ),
        cost_estimate=pl.CostEstimate(
            flops=2 * count * orders * points * width**2,
            bytes_accessed=count * orders * width * (4 * points + 4 * width),
            transcendentals=0,
        ),
    )(place, *operands)


def body(modes, exit_modes, pattern, attenuation, reflection, *, chunks):
    sections, count = lax.axis_size("sec"), lax.axis_size("grid")
    sec, spot = lax.axis_index("sec"), lax.axis_index("grid")
    orders = pattern.shape[1]
    width = modes.shape[2] // orders
    share = orders // count
    fields = modes[0]
    place = jnp.reshape(spot, (1,)).astype(jnp.int32)
    everywhere = range(sections)

    def route(pairs):
        return [(s * count + g, t * count + h) for (s, g), (t, h) in pairs]

    def send(value, pairs):
        return lax.ppermute(value, AXES, route(pairs))

    def summed(parts, secs):
        total = parts[0]
        for turn in range(1, count):
            pairs = [((s, g), (s, (g + turn) % count)) for s in secs for g in range(count)]
            total = total + send(parts[turn], pairs)
        return total

    def columns(parity, items):
        return jnp.concatenate(
            [
                fields[:, (g * share + j) * width : (g * share + j + 1) * width]
                for g in range(parity, count, 2)
                for j in items
            ],
            axis=1,
        )

    arrived = []
    for items in chunks:
        ups = [((s, g), (s + 1, g)) for s in range(sections - 1) for g in range(count)]
        downs = [((s + 1, g), (s, g)) for s in range(sections - 1) for g in range(count)]
        arrived.append((send(columns(0, items), ups), send(columns(1, items), downs)))

    def own_orders(value):
        return lax.dynamic_slice_in_dim(value, spot * share, share, 0)

    rows_of = [own_orders(attenuation.reshape(orders, width)), own_orders(reflection.reshape(orders, width))]
    flags = own_orders(pattern[0]).astype(jnp.float32)
    rows_of += [jnp.broadcast_to(flags[:, side : side + 1], (share, width)) for side in (0, 1)]
    aux = jnp.stack(rows_of, axis=1)
    ring = [
        [(s, s - s % BLOCK + (s + turn) % BLOCK) for s in everywhere] for turn in range(BLOCK)
    ]
    all_aux = [aux] + [
        send(aux, [((s, g), (t, g)) for s, t in ring[turn] for g in range(count)]) for turn in range(1, BLOCK)
    ]

    final = sections - 1
    exit_columns = [lambda at, item: at * share + item] * 2
    exit_parts = partial_sums(exit_body, place, (fields, exit_modes), exit_columns, count, share, width)
    last = summed(exit_parts, [final])
    at_end = sec == final
    if sections == BLOCK:
        got = send(last, [((final, g), (final - 2, g)) for g in range(count)])
        held = jnp.where(at_end, last, got)
        hops = [(final, final - 1), (final - 2, final - 3)]
        got = send(held, [((s, g), (t, g)) for s, t in hops for g in range(count)])
        last = jnp.where(jnp.logical_or(at_end, sec == final - 2), held, got)

    odd = spot % 2
    results = []
    for items, (before, after) in zip(chunks, arrived):
        number = len(items)
        columns_of = [
            lambda at, item, first=items[0]: at * share + first + item,
            lambda at, item, number=number: lax.div(at, 2) * number + item,
            lambda at, item, number=number: lax.div(at, 2) * number + item,
        ]
        parts = partial_sums(inner_body, place, (fields, before, after), columns_of, count, number, width)
        own = summed(parts, everywhere)
        tail = last[items[0] : items[0] + number]
        some_aux = [a[items[0] : items[0] + number] for a in all_aux]
        if sections == BLOCK:
            holds = lambda s, g: s > 0 if g % 2 == 0 else s < final
            terms = [own] + [
                send(own, [((s, g), (t, g)) for s, t in ring[turn] for g in range(count) if holds(s, g)])
                for turn in range(1, BLOCK)
            ]
            shifted = 1 - odd
            rows = width // sections
            first_row = sec * rows
        else:
            back = send(own, [((s + 1, g), (s, g)) for s in range(final) for g in range(0, count, 2)])
            own = jnp.where(at_end, tail, jnp.where(odd == 0, back, own))
            terms = [own] + [
                send(own, [((s, g), (t, g)) for s, t in ring[turn] for g in range(count)])
                for turn in range(1, BLOCK)
            ]
            shifted = 0
            rows, first_row = width, 0
        froms = [(sec - turn) % BLOCK for turn in range(BLOCK)]
        if sections != BLOCK:
            tail = sum(jnp.where(f == BLOCK - 1, t, 0.0) for f, t in zip(froms, terms))
        meta = jnp.stack([(f - shifted) % (BLOCK + 1) for f in froms] + froms + [first_row + 0 * sec])
        merged = star_of_four(meta.astype(jnp.int32), terms, tail, some_aux, rows)
        results.append(merged)
    merged = jnp.concatenate(results, axis=1) if len(results) > 1 else results[0]
    if sections > BLOCK:
        merged = later_levels(merged, sections, sec)
    return merged


def pair_body(first, second, out):
    for order in range(out.shape[1]):
        trans_a, front_a, back_a = (first[i, order] for i in range(3))
        trans_b, front_b, back_b = (second[i, order] for i in range(3))
        bounce = halves(mul(halves(back_a), halves(front_b)))
        square = halves(mul(bounce, bounce))
        inner = trans_a + mul(bounce, halves(trans_a))
        inner = halves(inner + mul(square, halves(inner)))
        behind = trans_b + mul(halves(trans_b), bounce)
        behind = halves(behind + mul(halves(behind), square))
        left = halves(trans_b)
        out[0, order] = mul(left, inner)
        out[1, order] = front_a + mul(halves(trans_a.T), halves(mul(halves(front_b), inner)))
        out[2, order] = back_b + mul(left, halves(mul(halves(back_a), behind, True)))


def later_levels(merged, sections, sec):
    vmem = pl.BlockSpec(memory_space=pltpu.VMEM)
    star = pl.pallas_call(
        pair_body, out_shape=jax.ShapeDtypeStruct(merged.shape, merged.dtype), in_specs=[vmem] * 2, out_specs=vmem
    )
    stride = BLOCK
    while stride < sections:
        other = lax.ppermute(merged, "sec", [(s, s ^ stride) for s in range(sections)])
        high = lax.rem(lax.div(sec, stride), 2) == 1
        merged = star(jnp.where(high, other, merged), jnp.where(high, merged, other))
        stride *= 2
    rows = merged.shape[2] // sections
    return lax.dynamic_slice_in_dim(merged, sec * rows, rows, 2)


def solution(mesh):
    share = 8 // mesh.shape["grid"]
    chunks = [list(range(share))]
    in_specs = (
        P(("groups", "sec"), "grid", None),
        P(("groups", "grid"), None),
        P(("groups", "sec"), None, None),
        P(("groups", "sec"), None),
        P(("groups", "sec"), None),
    )
    out_specs = P("groups", "grid", "sec", None)
    step = functools.partial(body, chunks=chunks)
    return jax.shard_map(step, mesh=mesh, in_specs=in_specs, out_specs=out_specs, check_vma=False)
```

time: 282 us -> 76.1 us (0.27)
  waiting for transfers between devices: 179 us -> 16.4 us
  matrix products: 43.1 us -> 0 us
  starting transfers between devices: 5.45 us -> 29.9 us
  local copies, waits for them, and re-layouts: 25.1 us -> 6.74 us
  Pallas kernels: 0 us -> 18.2 us
  between operations: 13.8 us -> 0.26 us
  other arithmetic: 14.2 us -> 3.89 us
    ppermute x3 -> x16, waiting for transfers between devices: 146 us -> 16.4 us  [send(): return lax.ppermute(value, AXES, route(pairs))]
    dot_general x23 -> x0, matrix products: 43.1 us -> none  [the longest x22 39.9 us: batch_mul(): jnp.einsum('kij,kjl->kil', left_side, right_side, precision=lax.Precision...]
    psum x1 -> x0, waiting for transfers between devices: 33.6 us -> none  [body(): intersections = lax.psum(stacked, 'grid')]
    ppermute x3 -> x16, starting transfers between devices: 5.44 us -> 29.9 us  [send(): return lax.ppermute(value, AXES, route(pairs))]
    pallas_call x0 -> x3, Pallas kernels: none -> 18.2 us  [the longest x2 13.8 us: partial_sums(): pl.pallas_call(body, out_shape=[jax.ShapeDtypeStruct((orders, width, widt...]
    optimization_barrier x10 -> x0, local copies, waits for them, and re-layouts: 16.9 us -> none  [batch_mul(): return lax.optimization_barrier(product)]
    another operation x8 -> x1, other arithmetic: 6.62 us -> 0.01 us  [body(): aux = jnp.stack(rows_of, axis=1)]
    select_n x4 -> x2, other arithmetic: 6.04 us -> 0.7 us  [the longest x1 0.68 us: body(): last = jnp.where(jnp.logical_or(at_end, sec == final - 2), held, got)]
  transfers between devices with their start and end apart: 4 -> 16, of which waited for: 4 -> 6; matrix products, arithmetic and copies ran while one was open for 1% -> 7% of each run, Pallas kernels for 0% -> 18%
where the time goes in v1:
time: 76.1 us; the launch traced here: 75.4 us
  starting transfers between devices  29.9 us (39%)
  Pallas kernels  18.2 us (24%)
  waiting for transfers between devices  16.4 us (22%)
  local copies, waits for them, and re-layouts  6.74 us (9%)
  other arithmetic  3.89 us (5%)
    ppermute x16, starting transfers between devices, send(): return lax.ppermute(value, AXES, route(pairs))  29.9 us
    ppermute x16, waiting for transfers between devices, send(): return lax.ppermute(value, AXES, route(pairs))  16.4 us
    pallas_call x2, Pallas kernels, partial_sums(): pl.pallas_call(body, out_shape=[jax.ShapeDtypeStruct((orders, width, widt...  13.8 us
    pallas_call x1, Pallas kernels, star_of_four(): pl.pallas_call(functools.partial(star_body, orders=orders, rows=rows), ou...  4.41 us
    unnamed x24, local copies, waits for them, and re-layouts  3.26 us
    add x2, other arithmetic, summed(): total = total + send(parts[turn], pairs)  1.94 us
    slice x1, local copies, waits for them, and re-layouts, columns(): fields[:, (g * share + j) * width:(g * share + j + 1) * width]  1.68 us
  transfers between devices with their start and end apart: 16, of which 6 were waited for; matrix products, arithmetic and copies ran while one was open for 7% of the time, Pallas kernels for 18%

profile of v1, /device:TPU:0, one launch (start us, length us, event | category | flops | bytes accessed | tf_op | source)
XLA Modules:
  0.0 75.4 jit_solution(8811857382294883791)
XLA Ops:
  0.0 1.7 %fusion = (bf16[1024,256]{1,0:T(8,128)(2,1)S(1)}, bf16[1024,256]{1,0:T(8,128)(2,1)S(1)}, bf16[1024,256]{1,0:T(8,128)(2,1)S(1)}, bf16[1024,256]{1,0:T(8,128)(2,1)S(1)}) fusion(bf16[1024,1024]{1,0:T(8,128)(2,1)} %bitcast.16), kind=kLoop, calls=%fused_computation.12 | loop fusion | bytes 4194304 | tf_op jit(solution)/shard_map/slice | solution.py:185
  1.8 5.0 %collective-permute-start = (bf16[1024,512]{1,0:T(8,128)(2,1)S(1)}, bf16[1024,512]{1,0:T(8,128)(2,1)S(1)}, u32[]{:S(2)}, u32[]{:S(2)}) collective-permute-start(bf16[1024,512]{1,0:T(8,128)(2,1)S(1)} %pad_maximum_fusion), channel_id=1, source_target_pairs={{0,4},{1,5},{2,6},{3,7},{4,8},{5,9},{6,10},{7,11},{8,12},{9,13},{1... | collective-permute-start | bytes 3145736 | tf_op jit(solution)/shard_map/ppermute | solution.py:173
  6.8 1.1 %pad_maximum_fusion.1 = bf16[1024,512]{1,0:T(8,128)(2,1)} fusion(bf16[1024,256]{1,0:T(8,128)(2,1)S(1)} %get-tuple-element.24, bf16[1024,256]{1,0:T(8,128)(2,1)S(1)} %get-tuple-element.23), kind=kLoop, calls=%fused_computation.1 | loop fusion | flops 2097152 | bytes 2097152 | tf_op jit(solution)/shard_map/concatenate | solution.py:183
  7.9 1.3 %collective-permute-start.1 = (bf16[1024,512]{1,0:T(8,128)(2,1)}, bf16[1024,512]{1,0:T(8,128)(2,1)S(1)}, u32[]{:S(2)}, u32[]{:S(2)}) collective-permute-start(bf16[1024,512]{1,0:T(8,128)(2,1)} %pad_maximum_fusion.1), channel_id=1, source_target_pairs={{4,0},{5,1},{6,2},{7,3},{8,4},{9,5},{10,6},{11,7},{12,8},{13,9},{1... | collective-permute-start | bytes 3145736 | tf_op jit(solution)/shard_map/ppermute | solution.py:173
  9.2 6.6 %shard_map.56 = (f32[2,128,128]{2,1,0:T(8,128)}, f32[2,128,128]{2,1,0:T(8,128)}, f32[2,128,128]{2,1,0:T(8,128)}, f32[2,128,128]{2,1,0:T(8,128)}) custom-call(s32[1]{0:T(128)} %bitcast.9.place, bf16[1024,1024]{1,0:T(8,128)(2,1)} %bitcast.17, bf16[1024,1024]{1,0:T(8,128)(2,1)} %after.1), custom_call_target="tpu_custom_call" | custom-call | flops 268435456 | bytes 4718592 | tf_op jit(solution)/shard_map/pallas_call | solution.py:145
  19.6 1.0 %add_add_fusion = f32[2,128,128]{2,1,0:T(8,128)S(1)} fusion(f32[2,128,128]{2,1,0:T(8,128)S(1)} %collective-permute-done.10, f32[2,128,128]{2,1,0:T(8,128)S(1)} %collective-permute-done.9, f32[2,128,128]{2,1,0:T(8,128)} %get-tuple-element.17, f32[2,128,128]{2,1,0:T(8,128)} %copy-done.3), kind=kLoop, calls=%fused_computation.2 | loop fusion | flops 98304 | bytes 655360 | tf_op jit(solution)/shard_map/add | solution.py:179
  21.4 3.3 %collective-permute-start.13 = (f32[2,4,128]{2,1,0:T(4,128)S(1)}, f32[2,4,128]{2,1,0:T(4,128)S(1)}, u32[]{:S(2)}, u32[]{:S(2)}) collective-permute-start(f32[2,4,128]{2,1,0:T(4,128)S(1)} %pad_maximum_fusion.2.refs_5_), channel_id=1, source_target_pairs={{0,4},{1,5},{2,6},{3,7},{4,8},{5,9},{6,10},{7,11},{8,12},{9,13},{1... | collective-permute-start | bytes 12296 | tf_op jit(solution)/shard_map/ppermute | solution.py:173
  24.7 11.3 %collective-permute-start.14 = (f32[2,4,128]{2,1,0:T(4,128)S(1)}, f32[2,4,128]{2,1,0:T(4,128)S(1)}, u32[]{:S(2)}, u32[]{:S(2)}) collective-permute-start(f32[2,4,128]{2,1,0:T(4,128)S(1)} %pad_maximum_fusion.2.refs_5_), channel_id=1, source_target_pairs={{0,8},{1,9},{2,10},{3,11},{4,12},{5,13},{6,14},{7,15},{8,0},{9,1},... | collective-permute-start | bytes 12296 | tf_op jit(solution)/shard_map/ppermute | solution.py:173
  36.7 0.9 %copy-done = bf16[1024,512]{1,0:T(8,128)(2,1)} copy-done((bf16[1024,512]{1,0:T(8,128)(2,1)}, bf16[1024,512]{1,0:T(8,128)(2,1)S(1)}, u32[]{:S(2)}) %copy-start) | copy-done | bytes 1048600
  37.7 1.0 %copy-done.1 = bf16[1024,512]{1,0:T(8,128)(2,1)} copy-done((bf16[1024,512]{1,0:T(8,128)(2,1)}, bf16[1024,512]{1,0:T(8,128)(2,1)S(1)}, u32[]{:S(2)}) %copy-start.1) | copy-done | bytes 1048600
  38.7 7.1 %shard_map.55 = (f32[2,128,128]{2,1,0:T(8,128)}, f32[2,128,128]{2,1,0:T(8,128)}, f32[2,128,128]{2,1,0:T(8,128)}, f32[2,128,128]{2,1,0:T(8,128)}) custom-call(s32[1]{0:T(128)} %bitcast.9.place, bf16[1024,1024]{1,0:T(8,128)(2,1)} %bitcast.18, bf16[1024,512]{1,0:T(8,128)(2,1)} %copy-done, bf16[1024,512]{1,0:T(8,128)(2,1)} %copy-done.1), custom_call_target="tpu_custom_call" | custom-call | flops 268435456 | bytes 4718592 | tf_op jit(solution)/shard_map/pallas_call | solution.py:145
  45.8 1.0 %collective-permute-start.3 = (f32[2,128,128]{2,1,0:T(8,128)}, f32[2,128,128]{2,1,0:T(8,128)S(1)}, u32[]{:S(2)}, u32[]{:S(2)}) collective-permute-start(f32[2,128,128]{2,1,0:T(8,128)} %get-tuple-element.15), channel_id=1, source_target_pairs={{0,2},{1,3},{2,0},{3,1},{4,6},{5,7},{6,4},{7,5},{8,10},{9,11},{10,... | collective-permute-start | bytes 393224 | tf_op jit(solution)/shard_map/ppermute | solution.py:173
  47.1 2.5 %collective-permute-done.4 = f32[2,128,128]{2,1,0:T(8,128)S(1)} collective-permute-done((f32[2,128,128]{2,1,0:T(8,128)}, f32[2,128,128]{2,1,0:T(8,128)S(1)}, u32[]{:S(2)}, u32[]{:S(2)}) %collective-permute-start.4) | collective-permute-done | bytes 131104 | tf_op jit(solution)/shard_map/ppermute | solution.py:173
  49.6 4.1 %collective-permute-done.3 = f32[2,128,128]{2,1,0:T(8,128)S(1)} collective-permute-done((f32[2,128,128]{2,1,0:T(8,128)}, f32[2,128,128]{2,1,0:T(8,128)S(1)}, u32[]{:S(2)}, u32[]{:S(2)}) %collective-permute-start.3) | collective-permute-done | bytes 131104 | tf_op jit(solution)/shard_map/ppermute | solution.py:173
  53.7 1.3 %collective-permute-start.12 = (f32[2,128,128]{2,1,0:T(8,128)S(1)}, f32[2,128,128]{2,1,0:T(8,128)S(1)}, u32[]{:S(2)}, u32[]{:S(2)}) collective-permute-start(f32[2,128,128]{2,1,0:T(8,128)S(1)} %broadcast_select_fusion), channel_id=1, source_target_pairs={{12,8},{13,9},{14,10},{15,11},{4,0},{5,1},{6,2},{7,3},{28,24},{29,... | collective-permute-start | bytes 393224 | tf_op jit(solution)/shard_map/ppermute | solution.py:173
  55.0 0.9 %add_add_fusion.1.refs_0_ = f32[2,128,128]{2,1,0:T(8,128)S(1)} fusion(f32[2,128,128]{2,1,0:T(8,128)S(1)} %collective-permute-done.4, f32[2,128,128]{2,1,0:T(8,128)S(1)} %collective-permute-done.3, f32[2,128,128]{2,1,0:T(8,128)} %get-tuple-element.13, f32[2,128,128]{2,1,0:T(8,128)S(1)} %collective-permute-done.2), kind=kLoop, calls=%fused_computation.3 | loop fusion | flops 98304 | bytes 655360 | tf_op jit(solution)/shard_map/add | solution.py:179
  55.9 1.3 %collective-permute-start.5 = (f32[2,128,128]{2,1,0:T(8,128)S(1)}, f32[2,128,128]{2,1,0:T(8,128)S(1)}, u32[]{:S(2)}, u32[]{:S(2)}) collective-permute-start(f32[2,128,128]{2,1,0:T(8,128)S(1)} %add_add_fusion.1.refs_0_), channel_id=1, source_target_pairs={{1,5},{3,7},{4,8},{5,9},{6,10},{7,11},{8,12},{9,13},{10,14},{11,15... | collective-permute-start | bytes 393224 | tf_op jit(solution)/shard_map/ppermute | solution.py:173
  57.2 1.3 %collective-permute-start.6 = (f32[2,128,128]{2,1,0:T(8,128)S(1)}, f32[2,128,128]{2,1,0:T(8,128)S(1)}, u32[]{:S(2)}, u32[]{:S(2)}) collective-permute-start(f32[2,128,128]{2,1,0:T(8,128)S(1)} %add_add_fusion.1.refs_0_), channel_id=1, source_target_pairs={{1,9},{3,11},{4,12},{5,13},{6,14},{7,15},{8,0},{9,1},{10,2},{11,3}... | collective-permute-start | bytes 393224 | tf_op jit(solution)/shard_map/ppermute | solution.py:173
  58.5 2.0 %collective-permute-done.12 = f32[2,128,128]{2,1,0:T(8,128)S(1)} collective-permute-done((f32[2,128,128]{2,1,0:T(8,128)S(1)}, f32[2,128,128]{2,1,0:T(8,128)S(1)}, u32[]{:S(2)}, u32[]{:S(2)}) %collective-permute-start.12) | collective-permute-done | bytes 131104 | tf_op jit(solution)/shard_map/ppermute | solution.py:173
  60.5 1.3 %collective-permute-start.7 = (f32[2,128,128]{2,1,0:T(8,128)S(1)}, f32[2,128,128]{2,1,0:T(8,128)S(1)}, u32[]{:S(2)}, u32[]{:S(2)}) collective-permute-start(f32[2,128,128]{2,1,0:T(8,128)S(1)} %add_add_fusion.1.refs_0_), channel_id=1, source_target_pairs={{1,13},{3,15},{4,0},{5,1},{6,2},{7,3},{8,4},{9,5},{10,6},{11,7},{1... | collective-permute-start | bytes 393224 | tf_op jit(solution)/shard_map/ppermute | solution.py:173
  62.5 2.3 %collective-permute-done.5.refs_1_ = f32[2,128,128]{2,1,0:T(8,128)S(1)} collective-permute-done((f32[2,128,128]{2,1,0:T(8,128)S(1)}, f32[2,128,128]{2,1,0:T(8,128)S(1)}, u32[]{:S(2)}, u32[]{:S(2)}) %collective-permute-start.5) | collective-permute-done | bytes 131104 | tf_op jit(solution)/shard_map/ppermute | solution.py:173
  64.8 4.6 %collective-permute-done.6.refs_2_ = f32[2,128,128]{2,1,0:T(8,128)S(1)} collective-permute-done((f32[2,128,128]{2,1,0:T(8,128)S(1)}, f32[2,128,128]{2,1,0:T(8,128)S(1)}, u32[]{:S(2)}, u32[]{:S(2)}) %collective-permute-start.6) | collective-permute-done | bytes 131104 | tf_op jit(solution)/shard_map/ppermute | solution.py:173
  69.4 0.9 %collective-permute-done.7.refs_3_ = f32[2,128,128]{2,1,0:T(8,128)S(1)} collective-permute-done((f32[2,128,128]{2,1,0:T(8,128)S(1)}, f32[2,128,128]{2,1,0:T(8,128)S(1)}, u32[]{:S(2)}, u32[]{:S(2)}) %collective-permute-start.7) | collective-permute-done | bytes 131104 | tf_op jit(solution)/shard_map/ppermute | solution.py:173
  71.0 4.4 %shard_map.57 = f32[3,2,32,128]{3,2,1,0:T(8,128)} custom-call(s32[9]{0:T(128)} %stack.48.meta, f32[2,128,128]{2,1,0:T(8,128)} %copy-done.2, f32[2,128,128]{2,1,0:T(8,128)} %copy-done.6, f32[2,128,128]{2,1,0:T(8,128)} %copy-done.7, f32[2,128,128]{2,1,0:T(8,128)} %copy-done.8, f32[2,128,128]{2,1,0:T(8,128)} %broadcast_select_fusion.1.refs_4_, ...), custom_call_target="tpu_custom_call" | custom-call | flops 503316480 | bytes 1048576 | tf_op jit(solution)/shard_map/pallas_call | solution.py:97
  (50 shorter events, 6.9 us)
Async XLA Ops:
  1.8 34.9 %collective-permute-start = (bf16[1024,512]{1,0:T(8,128)(2,1)S(1)}, bf16[1024,512]{1,0:T(8,128)(2,1)S(1)}, u32[]{:S(2)}, u32[]{:S(2)}) collective-permute-start(bf16[1024,512]{1,0:T(8,128)(2,1)S(1)} %pad_maximum_fusion), channel_id=1, source_target_pairs={{0,4},{1,5},{2,6},{3,7},{4,8},{5,9},{6,10},{7,11},{8,12},{9,13},{1... | collective-permute-start | bytes 3145736 | tf_op jit(solution)/shard_map/ppermute | solution.py:173
  7.9 28.8 %collective-permute-start.1 = (bf16[1024,512]{1,0:T(8,128)(2,1)}, bf16[1024,512]{1,0:T(8,128)(2,1)S(1)}, u32[]{:S(2)}, u32[]{:S(2)}) collective-permute-start(bf16[1024,512]{1,0:T(8,128)(2,1)} %pad_maximum_fusion.1), channel_id=1, source_target_pairs={{4,0},{5,1},{6,2},{7,3},{8,4},{9,5},{10,6},{11,7},{12,8},{13,9},{1... | collective-permute-start | bytes 3145736 | tf_op jit(solution)/shard_map/ppermute | solution.py:173
  9.2 9.4 %copy-start.5 = (s32[1,8,2]{1,2,0:T(2,128)S(1)}, s32[1,8,2]{1,2,0:T(2,128)}, u32[]{:S(2)}) copy-start(s32[1,8,2]{1,2,0:T(2,128)} %param.7) | copy-start | bytes 196
  15.8 3.1 %collective-permute-start.10 = (f32[2,128,128]{2,1,0:T(8,128)}, f32[2,128,128]{2,1,0:T(8,128)S(1)}, u32[]{:S(2)}, u32[]{:S(2)}) collective-permute-start(f32[2,128,128]{2,1,0:T(8,128)} %get-tuple-element.20), channel_id=1, source_target_pairs={{12,15},{13,12},{14,13},{15,14},{28,31},{29,28},{30,29},{31,30}} | collective-permute-start | bytes 393224 | tf_op jit(solution)/shard_map/ppermute | solution.py:173
  16.5 2.4 %collective-permute-start.9 = (f32[2,128,128]{2,1,0:T(8,128)}, f32[2,128,128]{2,1,0:T(8,128)S(1)}, u32[]{:S(2)}, u32[]{:S(2)}) collective-permute-start(f32[2,128,128]{2,1,0:T(8,128)} %get-tuple-element.19), channel_id=1, source_target_pairs={{12,14},{13,15},{14,12},{15,13},{28,30},{29,31},{30,28},{31,29}} | collective-permute-start | bytes 393224 | tf_op jit(solution)/shard_map/ppermute | solution.py:173
  17.1 1.8 %collective-permute-start.8 = (f32[2,128,128]{2,1,0:T(8,128)}, f32[2,128,128]{2,1,0:T(8,128)S(1)}, u32[]{:S(2)}, u32[]{:S(2)}) collective-permute-start(f32[2,128,128]{2,1,0:T(8,128)} %get-tuple-element.18), channel_id=1, source_target_pairs={{12,13},{13,14},{14,15},{15,12},{28,29},{29,30},{30,31},{31,28}} | collective-permute-start | bytes 393224 | tf_op jit(solution)/shard_map/ppermute | solution.py:173
  20.6 26.3 %collective-permute-start.11 = (f32[2,128,128]{2,1,0:T(8,128)S(1)}, f32[2,128,128]{2,1,0:T(8,128)S(1)}, u32[]{:S(2)}, u32[]{:S(2)}) collective-permute-start(f32[2,128,128]{2,1,0:T(8,128)S(1)} %add_add_fusion), channel_id=1, source_target_pairs={{12,4},{13,5},{14,6},{15,7},{28,20},{29,21},{30,22},{31,23}} | collective-permute-start | bytes 393224 | tf_op jit(solution)/shard_map/ppermute | solution.py:173
  21.4 28.2 %copy-start.4 = (f32[2,4,128]{2,1,0:T(4,128)}, f32[2,4,128]{2,1,0:T(4,128)S(1)}, u32[]{:S(2)}) copy-start(f32[2,4,128]{2,1,0:T(4,128)S(1)} %pad_maximum_fusion.2.refs_5_) | copy-start | bytes 12292
  21.4 35.8 %collective-permute-start.13 = (f32[2,4,128]{2,1,0:T(4,128)S(1)}, f32[2,4,128]{2,1,0:T(4,128)S(1)}, u32[]{:S(2)}, u32[]{:S(2)}) collective-permute-start(f32[2,4,128]{2,1,0:T(4,128)S(1)} %pad_maximum_fusion.2.refs_5_), channel_id=1, source_target_pairs={{0,4},{1,5},{2,6},{3,7},{4,8},{5,9},{6,10},{7,11},{8,12},{9,13},{1... | collective-permute-start | bytes 12296 | tf_op jit(solution)/shard_map/ppermute | solution.py:173
  24.7 37.8 %collective-permute-start.14 = (f32[2,4,128]{2,1,0:T(4,128)S(1)}, f32[2,4,128]{2,1,0:T(4,128)S(1)}, u32[]{:S(2)}, u32[]{:S(2)}) collective-permute-start(f32[2,4,128]{2,1,0:T(4,128)S(1)} %pad_maximum_fusion.2.refs_5_), channel_id=1, source_target_pairs={{0,8},{1,9},{2,10},{3,11},{4,12},{5,13},{6,14},{7,15},{8,0},{9,1},... | collective-permute-start | bytes 12296 | tf_op jit(solution)/shard_map/ppermute | solution.py:173
  37.7 1.0 %copy-start.1 = (bf16[1024,512]{1,0:T(8,128)(2,1)}, bf16[1024,512]{1,0:T(8,128)(2,1)S(1)}, u32[]{:S(2)}) copy-start(bf16[1024,512]{1,0:T(8,128)(2,1)S(1)} %collective-permute-done.1.after) | copy-start | bytes 3145732
  45.8 3.7 %collective-permute-start.4 = (f32[2,128,128]{2,1,0:T(8,128)}, f32[2,128,128]{2,1,0:T(8,128)S(1)}, u32[]{:S(2)}, u32[]{:S(2)}) collective-permute-start(f32[2,128,128]{2,1,0:T(8,128)} %get-tuple-element.16), channel_id=1, source_target_pairs={{0,3},{1,0},{2,1},{3,2},{4,7},{5,4},{6,5},{7,6},{8,11},{9,8},{10,9... | collective-permute-start | bytes 393224 | tf_op jit(solution)/shard_map/ppermute | solution.py:173
  45.8 7.9 %collective-permute-start.3 = (f32[2,128,128]{2,1,0:T(8,128)}, f32[2,128,128]{2,1,0:T(8,128)S(1)}, u32[]{:S(2)}, u32[]{:S(2)}) collective-permute-start(f32[2,128,128]{2,1,0:T(8,128)} %get-tuple-element.15), channel_id=1, source_target_pairs={{0,2},{1,3},{2,0},{3,1},{4,6},{5,7},{6,4},{7,5},{8,10},{9,11},{10,... | collective-permute-start | bytes 393224 | tf_op jit(solution)/shard_map/ppermute | solution.py:173
  46.8 8.1 %collective-permute-start.2 = (f32[2,128,128]{2,1,0:T(8,128)}, f32[2,128,128]{2,1,0:T(8,128)S(1)}, u32[]{:S(2)}, u32[]{:S(2)}) collective-permute-start(f32[2,128,128]{2,1,0:T(8,128)} %get-tuple-element.14), channel_id=1, source_target_pairs={{0,1},{1,2},{2,3},{3,0},{4,5},{5,6},{6,7},{7,4},{8,9},{9,10},{10,1... | collective-permute-start | bytes 393224 | tf_op jit(solution)/shard_map/ppermute | solution.py:173
  49.6 12.9 %collective-permute-start.15 = (f32[2,4,128]{2,1,0:T(4,128)S(1)}, f32[2,4,128]{2,1,0:T(4,128)S(1)}, u32[]{:S(2)}, u32[]{:S(2)}) collective-permute-start(f32[2,4,128]{2,1,0:T(4,128)S(1)} %pad_maximum_fusion.2.refs_5_), channel_id=1, source_target_pairs={{0,12},{1,13},{2,14},{3,15},{4,0},{5,1},{6,2},{7,3},{8,4},{9,5},{1... | collective-permute-start | bytes 12296 | tf_op jit(solution)/shard_map/ppermute | solution.py:173
  53.7 6.8 %collective-permute-start.12 = (f32[2,128,128]{2,1,0:T(8,128)S(1)}, f32[2,128,128]{2,1,0:T(8,128)S(1)}, u32[]{:S(2)}, u32[]{:S(2)}) collective-permute-start(f32[2,128,128]{2,1,0:T(8,128)S(1)} %broadcast_select_fusion), channel_id=1, source_target_pairs={{12,8},{13,9},{14,10},{15,11},{4,0},{5,1},{6,2},{7,3},{28,24},{29,... | collective-permute-start | bytes 393224 | tf_op jit(solution)/shard_map/ppermute | solution.py:173
  55.9 14.4 %copy-start.2 = (f32[2,128,128]{2,1,0:T(8,128)}, f32[2,128,128]{2,1,0:T(8,128)S(1)}, u32[]{:S(2)}) copy-start(f32[2,128,128]{2,1,0:T(8,128)S(1)} %add_add_fusion.1.refs_0_) | copy-start | bytes 393220
  55.9 8.9 %collective-permute-start.5 = (f32[2,128,128]{2,1,0:T(8,128)S(1)}, f32[2,128,128]{2,1,0:T(8,128)S(1)}, u32[]{:S(2)}, u32[]{:S(2)}) collective-permute-start(f32[2,128,128]{2,1,0:T(8,128)S(1)} %add_add_fusion.1.refs_0_), channel_id=1, source_target_pairs={{1,5},{3,7},{4,8},{5,9},{6,10},{7,11},{8,12},{9,13},{10,14},{11,15... | collective-permute-start | bytes 393224 | tf_op jit(solution)/shard_map/ppermute | solution.py:173
  57.2 13.1 %copy-start.9 = (f32[2,4,128]{2,1,0:T(4,128)}, f32[2,4,128]{2,1,0:T(4,128)S(1)}, u32[]{:S(2)}) copy-start(f32[2,4,128]{2,1,0:T(4,128)S(1)} %collective-permute-done.13.refs_6_) | copy-start | bytes 12292
  57.2 12.2 %collective-permute-start.6 = (f32[2,128,128]{2,1,0:T(8,128)S(1)}, f32[2,128,128]{2,1,0:T(8,128)S(1)}, u32[]{:S(2)}, u32[]{:S(2)}) collective-permute-start(f32[2,128,128]{2,1,0:T(8,128)S(1)} %add_add_fusion.1.refs_0_), channel_id=1, source_target_pairs={{1,9},{3,11},{4,12},{5,13},{6,14},{7,15},{8,0},{9,1},{10,2},{11,3}... | collective-permute-start | bytes 393224 | tf_op jit(solution)/shard_map/ppermute | solution.py:173
  60.5 9.8 %collective-permute-start.7 = (f32[2,128,128]{2,1,0:T(8,128)S(1)}, f32[2,128,128]{2,1,0:T(8,128)S(1)}, u32[]{:S(2)}, u32[]{:S(2)}) collective-permute-start(f32[2,128,128]{2,1,0:T(8,128)S(1)} %add_add_fusion.1.refs_0_), channel_id=1, source_target_pairs={{1,13},{3,15},{4,0},{5,1},{6,2},{7,3},{8,4},{9,5},{10,6},{11,7},{1... | collective-permute-start | bytes 393224 | tf_op jit(solution)/shard_map/ppermute | solution.py:173
  62.5 7.8 %copy-start.10 = (f32[2,4,128]{2,1,0:T(4,128)}, f32[2,4,128]{2,1,0:T(4,128)S(1)}, u32[]{:S(2)}) copy-start(f32[2,4,128]{2,1,0:T(4,128)S(1)} %collective-permute-done.14.refs_7_) | copy-start | bytes 12292
  62.5 7.8 %copy-start.11 = (f32[2,4,128]{2,1,0:T(4,128)}, f32[2,4,128]{2,1,0:T(4,128)S(1)}, u32[]{:S(2)}) copy-start(f32[2,4,128]{2,1,0:T(4,128)S(1)} %collective-permute-done.15.refs_8_) | copy-start | bytes 12292
  64.8 5.5 %copy-start.6 = (f32[2,128,128]{2,1,0:T(8,128)}, f32[2,128,128]{2,1,0:T(8,128)S(1)}, u32[]{:S(2)}) copy-start(f32[2,128,128]{2,1,0:T(8,128)S(1)} %collective-permute-done.5.refs_1_) | copy-start | bytes 393220
  (4 other events, 3.1 us)

commit v2 on v1

--- a/solution.py
+++ b/solution.py
@@ -7,8 +7,10 @@
 from jax.experimental.pallas import tpu as pltpu
 from jax.sharding import PartitionSpec as P
 
+CHUNKS = lambda share: [list(range(share))]
 BLOCK = 4
 AXES = ("sec", "grid")
+ROOM = pltpu.CompilerParams(vmem_limit_bytes=16 * 2**20)
 
 
 def halves(matrix):
@@ -25,9 +27,12 @@
     return dot(left[0], right[0]) + (dot(left[0], right[1]) + dot(left[1], right[0]))
 
 
-def star_body(meta, *refs, orders, rows):
+def star_body(meta, *refs, orders, rows, earlier):
     terms, last, aux = refs[:BLOCK], refs[BLOCK], refs[BLOCK + 1 : 2 * BLOCK + 1]
-    out, tbuf, abuf, rbuf = refs[2 * BLOCK + 1 :]
+    done = refs[2 * BLOCK + 1 : -4]
+    out, tbuf, abuf, rbuf = refs[-4:]
+    for ready in done:
+        out[:, :earlier] = ready[...]
     for slot in range(BLOCK):
         tbuf[meta[slot]] = terms[slot][...]
         abuf[meta[BLOCK + slot]] = aux[slot][...]
@@ -86,28 +91,30 @@
         ahead = ahead + mul(halves(ahead), bounce)
         behind = behind + mul(halves(behind), bounce, True)
         ahead = mul(halves(ahead), trans_a)
-        out[0, order] = ahead[:rows]
-        out[1, order] = front_a_part + ahead[rows:]
-        out[2, order] = back_b_part + mul(halves(behind), trans_b, True)
-
-
-def star_of_four(meta, terms, last, aux, rows):
+        out[0, earlier + order] = ahead[:rows]
+        out[1, earlier + order] = front_a_part + ahead[rows:]
+        out[2, earlier + order] = back_b_part + mul(halves(behind), trans_b, True)
+
+
+def star_of_four(meta, terms, last, aux, rows, done):
     orders, width = last.shape[0], last.shape[-1]
+    earlier = sum(ready.shape[1] for ready in done)
     vmem = pl.BlockSpec(memory_space=pltpu.VMEM)
     return pl.pallas_call(
-        functools.partial(star_body, orders=orders, rows=rows),
-        out_shape=jax.ShapeDtypeStruct((3, orders, rows, width), jnp.float32),
-        in_specs=[pl.BlockSpec(memory_space=pltpu.SMEM)] + [vmem] * (2 * BLOCK + 1),
+        functools.partial(star_body, orders=orders, rows=rows, earlier=earlier),
+        out_shape=jax.ShapeDtypeStruct((3, earlier + orders, rows, width), jnp.float32),
+        in_specs=[pl.BlockSpec(memory_space=pltpu.SMEM)] + [vmem] * (2 * BLOCK + 1 + len(done)),
         out_specs=vmem,
         scratch_shapes=[
             pltpu.VMEM((BLOCK + 1, orders, width, width), jnp.float32),
             pltpu.VMEM((BLOCK, orders) + aux[0].shape[1:], jnp.float32),
             pltpu.VMEM((2, width, width), jnp.float32),
         ],
+        compiler_params=ROOM,
         cost_estimate=pl.CostEstimate(
             flops=orders * 120 * width**3, bytes_accessed=orders * 8 * 4 * width**2, transcendentals=0
         ),
-    )(meta, *terms, last, *aux)
+    )(meta, *terms, last, *aux, *done)
 
 
 def tall_dot(left, right):
@@ -115,45 +122,98 @@
     return lax.dot_general(left, right, dims, preferred_element_type=jnp.float32)
 
 
-def keep(outs, turn, item, value):
-    for index, out in enumerate(outs):
-        @pl.when(turn == index)
-        def _():
-            out[item] = value
-
-
-def exit_body(place, own, after, *outs):
-    keep(outs, pl.program_id(0), pl.program_id(1), tall_dot(own[...], after[...]))
-
-
-def inner_body(place, own, before, after, *outs):
-    turn, item = pl.program_id(0), pl.program_id(1)
-    up = lax.rem(lax.rem(place[0] + turn, len(outs)), 2) == 0
-    left = jnp.where(up, before[...], own[...])
-    right = jnp.where(up, own[...], after[...])
-    keep(outs, turn, item, tall_dot(left, right))
-
-
-def partial_sums(body, place, operands, columns, count, orders, width):
-    points = operands[0].shape[0]
-    spot = lambda turn, place: lax.rem(place[0] + turn, count)
-    specs = [
-        pl.BlockSpec((points, width), lambda turn, item, place, col=col: (0, col(spot(turn, place), item)))
-        for col in columns
-    ]
-    whole = pl.BlockSpec((orders, width, width), lambda turn, item, place: (0, 0, 0))
+def hand_out(place, terms, outs):
+    count = len(outs)
+    for turn, out in enumerate(outs):
+        out[...] = terms[lax.rem(place[0] + turn, count)]
+
+
+def exit_body(place, own, after, *refs):
+    outs, terms = refs[:-1], refs[-1]
+    count, share, width = terms.shape[:3]
+    for spot in range(count):
+        for item in range(share):
+            columns = pl.ds((spot * share + item) * width, width)
+            terms[spot, item] = tall_dot(own[:, columns], after[:, columns])
+    hand_out(place, terms, outs)
+
+
+def exit_sums(place, fields, exit_modes, count, share, width):
+    points, modes = fields.shape
+    whole = pl.BlockSpec(memory_space=pltpu.VMEM)
     return pl.pallas_call(
-        body,
-        out_shape=[jax.ShapeDtypeStruct((orders, width, width), jnp.float32)] * count,
-        grid_spec=pltpu.PrefetchScalarGridSpec(
-            num_scalar_prefetch=1, grid=(count, orders), in_specs=specs, out_specs=[whole] * count
+        exit_body,
+        out_shape=[jax.ShapeDtypeStruct((share, width, width), jnp.float32)] * count,
+        in_specs=[pl.BlockSpec(memory_space=pltpu.SMEM), whole, whole],
+        out_specs=[whole] * count,
+        scratch_shapes=[pltpu.VMEM((count, share, width, width), jnp.float32)],
+        compiler_params=ROOM,
+        cost_estimate=pl.CostEstimate(
+            flops=2 * points * modes * width, bytes_accessed=4 * points * modes, transcendentals=0
         ),
+    )(place, fields, exit_modes)
+
+
+def inner_body(place, fields, before, after, *refs, items, share):
+    outs, terms = refs[:-1], refs[-1]
+    count, number, width = terms.shape[:3]
+    for spot in range(count):
+        for index, item in enumerate(items):
+            own = fields[:, pl.ds((spot * share + item) * width, width)]
+            columns = pl.ds((spot // 2 * number + index) * width, width)
+            if spot % 2 == 0:
+                terms[spot, index] = tall_dot(before[:, columns], own)
+            else:
+                terms[spot, index] = tall_dot(own, after[:, columns])
+    hand_out(place, terms, outs)
+
+
+def inner_sums(place, fields, before, after, count, share, items, width):
+    points, number = fields.shape[0], len(items)
+    whole = pl.BlockSpec(memory_space=pltpu.VMEM)
+    return pl.pallas_call(
+        functools.partial(inner_body, items=items, share=share),
+        out_shape=[jax.ShapeDtypeStruct((number, width, width), jnp.float32)] * count,
+        in_specs=[pl.BlockSpec(memory_space=pltpu.SMEM), whole, whole, whole],
+        out_specs=[whole] * count,
+        scratch_shapes=[pltpu.VMEM((count, number, width, width), jnp.float32)],
+        compiler_params=ROOM,
         cost_estimate=pl.CostEstimate(
-            flops=2 * count * orders * points * width**2,
-            bytes_accessed=count * orders * width * (4 * points + 4 * width),
+            flops=2 * count * number * points * width**2,
+            bytes_accessed=count * number * width * (4 * points + 4 * width),
             transcendentals=0,
         ),
-    )(place, *operands)
+    )(place, fields, before, after)
+
+
+def pack_body(fields, *refs, items, share, width):
+    outs, semaphores = refs[:-1], refs[-1]
+    number = len(items)
+    copies = []
+    for spot in range(semaphores.shape[0]):
+        source = pl.ds((spot * share + items[0]) * width, number * width)
+        target = pl.ds(spot // 2 * number * width, number * width)
+        copy = pltpu.make_async_copy(
+            fields.at[:, source], outs[spot % 2].at[:, target], semaphores.at[spot]
+        )
+        copy.start()
+        copies.append(copy)
+    for copy in copies:
+        copy.wait()
+
+
+def packed(fields, count, share, items, width):
+    far = pl.BlockSpec(memory_space=pl.ANY)
+    shape = (fields.shape[0], count // 2 * len(items) * width)
+    return pl.pallas_call(
+        functools.partial(pack_body, items=items, share=share, width=width),
+        out_shape=[jax.ShapeDtypeStruct(shape, fields.dtype)] * 2,
+        in_specs=[far],
+        out_specs=[far] * 2,
+        scratch_shapes=[pltpu.SemaphoreType.DMA((count,))],
+        compiler_params=ROOM,
+        cost_estimate=pl.CostEstimate(flops=0, bytes_accessed=8 * shape[0] * shape[1], transcendentals=0),
+    )(fields)
 
 
 def body(modes, exit_modes, pattern, attenuation, reflection, *, chunks):
@@ -179,21 +239,13 @@
             total = total + send(parts[turn], pairs)
         return total
 
-    def columns(parity, items):
-        return jnp.concatenate(
-            [
-                fields[:, (g * share + j) * width : (g * share + j + 1) * width]
-                for g in range(parity, count, 2)
-                for j in items
-            ],
-            axis=1,
-        )
-
-    arrived = []
+    ups = [((s, g), (s + 1, g)) for s in range(sections - 1) for g in range(count)]
+    downs = [(t, s) for s, t in ups]
+    arrived, source = [], fields
     for items in chunks:
-        ups = [((s, g), (s + 1, g)) for s in range(sections - 1) for g in range(count)]
-        downs = [((s + 1, g), (s, g)) for s in range(sections - 1) for g in range(count)]
-        arrived.append((send(columns(0, items), ups), send(columns(1, items), downs)))
+        for_up, for_down = packed(source, count, share, items, width)
+        source, for_up, for_down = lax.optimization_barrier((fields, for_up, for_down))
+        arrived.append((send(for_up, ups), send(for_down, downs)))
 
     def own_orders(value):
         return lax.dynamic_slice_in_dim(value, spot * share, share, 0)
@@ -210,8 +262,7 @@
     ]
 
     final = sections - 1
-    exit_columns = [lambda at, item: at * share + item] * 2
-    exit_parts = partial_sums(exit_body, place, (fields, exit_modes), exit_columns, count, share, width)
+    exit_parts = exit_sums(place, fields, exit_modes, count, share, width)
     last = summed(exit_parts, [final])
     at_end = sec == final
     if sections == BLOCK:
@@ -222,16 +273,13 @@
         last = jnp.where(jnp.logical_or(at_end, sec == final - 2), held, got)
 
     odd = spot % 2
-    results = []
+    done = []
     for items, (before, after) in zip(chunks, arrived):
         number = len(items)
-        columns_of = [
-            lambda at, item, first=items[0]: at * share + first + item,
-            lambda at, item, number=number: lax.div(at, 2) * number + item,
-            lambda at, item, number=number: lax.div(at, 2) * number + item,
-        ]
-        parts = partial_sums(inner_body, place, (fields, before, after), columns_of, count, number, width)
+        parts = inner_sums(place, fields, before, after, count, share, items, width)
         own = summed(parts, everywhere)
+        if items is not chunks[-1]:
+            own = lax.optimization_barrier((own,) + arrived[-1])[0]
         tail = last[items[0] : items[0] + number]
         some_aux = [a[items[0] : items[0] + number] for a in all_aux]
         if sections == BLOCK:
@@ -256,9 +304,8 @@
         if sections != BLOCK:
             tail = sum(jnp.where(f == BLOCK - 1, t, 0.0) for f, t in zip(froms, terms))
         meta = jnp.stack([(f - shifted) % (BLOCK + 1) for f in froms] + froms + [first_row + 0 * sec])
-        merged = star_of_four(meta.astype(jnp.int32), terms, tail, some_aux, rows)
-        results.append(merged)
-    merged = jnp.concatenate(results, axis=1) if len(results) > 1 else results[0]
+        merged = star_of_four(meta.astype(jnp.int32), terms, tail, some_aux, rows, done)
+        done = [merged]
     if sections > BLOCK:
         merged = later_levels(merged, sections, sec)
     return merged
@@ -297,7 +344,7 @@
 
 def solution(mesh):
     share = 8 // mesh.shape["grid"]
-    chunks = [list(range(share))]
+    chunks = CHUNKS(share)
     in_specs = (
         P(("groups", "sec"), "grid", None),
         P(("groups", "grid"), None),

time: 76.1 us -> 67.2 us (0.88)
  Pallas kernels: 18.2 us -> 8.91 us
  starting transfers between devices: 29.9 us -> 34.2 us
  other arithmetic: 3.89 us -> 1.21 us
  local copies, waits for them, and re-layouts: 6.74 us -> 4.39 us
  waiting for transfers between devices: 16.4 us -> 17.8 us
    pallas_call x3 -> x4, Pallas kernels: 18.2 us -> 8.91 us  [the longest x1 3.77 us: star_of_four(): pl.pallas_call(functools.partial(star_body, orders=orders, rows=rows, ear...]
    ppermute x16, starting transfers between devices: 29.9 us -> 34.2 us  [send(): return lax.ppermute(value, AXES, route(pairs))]
    slice x1 -> x0, local copies, waits for them, and re-layouts: 1.68 us -> none  [columns(): fields[:, (g * share + j) * width:(g * share + j + 1) * width]]
    ppermute x16, waiting for transfers between devices: 16.4 us -> 17.8 us  [send(): return lax.ppermute(value, AXES, route(pairs))]
    concatenate x2 -> x0, other arithmetic: 1.17 us -> none  [columns(): jnp.concatenate([fields[:, (g * share + j) * width:(g * share + j + 1) *...]
    add x2, other arithmetic: 1.94 us -> 1.09 us  [summed(): total = total + send(parts[turn], pairs)]
    unnamed x24 -> x8, local copies, waits for them, and re-layouts: 3.26 us -> 3.18 us
  transfers between devices with their start and end apart: 16 -> 16, of which waited for: 6 -> 7; matrix products, arithmetic and copies ran while one was open for 7% -> 4% of each run, Pallas kernels for 18% -> 6%
where the time goes in v2:
time: 67.2 us; the launch traced here: 66.8 us
  starting transfers between devices  34.2 us (51%)
  waiting for transfers between devices  17.8 us (26%)
  Pallas kernels  8.91 us (13%)
  local copies, waits for them, and re-layouts  4.39 us (7%)
  other arithmetic  1.21 us (2%)
    ppermute x16, starting transfers between devices, send(): return lax.ppermute(value, AXES, route(pairs))  34.2 us
    ppermute x16, waiting for transfers between devices, send(): return lax.ppermute(value, AXES, route(pairs))  17.8 us
    pallas_call x1, Pallas kernels, star_of_four(): pl.pallas_call(functools.partial(star_body, orders=orders, rows=rows, ear...  3.77 us
    unnamed x8, local copies, waits for them, and re-layouts  3.18 us
    pallas_call x1, Pallas kernels, inner_sums(): pl.pallas_call(functools.partial(inner_body, items=items, share=share), o...  2.05 us
    pallas_call x1, Pallas kernels, exit_sums(): pl.pallas_call(exit_body, out_shape=[jax.ShapeDtypeStruct((share, width,...  1.73 us
    pallas_call x1, Pallas kernels, packed(): pl.pallas_call(functools.partial(pack_body, items=items, share=share, wid...  1.37 us
  transfers between devices with their start and end apart: 16, of which 7 were waited for; matrix products, arithmetic and copies ran while one was open for 4% of the time, Pallas kernels for 6%

profile of v2, /device:TPU:0, one launch (start us, length us, event | category | flops | bytes accessed | tf_op | source)
XLA Modules:
  0.0 66.8 jit_solution(7696278440804932878)
XLA Ops:
  0.0 1.6 %copy-done = bf16[1,1024,1024]{2,1,0:T(8,128)(2,1)S(1)} copy-done((bf16[1,1024,1024]{2,1,0:T(8,128)(2,1)S(1)}, bf16[1,1024,1024]{2,1,0:T(8,128)(2,1)}, u32[]{:S(2)}) %copy-start) | copy-done | bytes 2097176
  1.6 1.4 %shard_map.55 = (bf16[1024,512]{1,0:T(8,128)(2,1)}, bf16[1024,512]{1,0:T(8,128)(2,1)}) custom-call(bf16[1024,1024]{1,0:T(8,128)(2,1)S(1)} %bitcast.16), custom_call_target="tpu_custom_call" | custom-call | bytes 4194304 | tf_op jit(solution)/shard_map/pallas_call | solution.py:208
  3.0 5.0 %collective-permute-start = (bf16[1024,512]{1,0:T(8,128)(2,1)}, bf16[1024,512]{1,0:T(8,128)(2,1)S(1)}, u32[]{:S(2)}, u32[]{:S(2)}) collective-permute-start(bf16[1024,512]{1,0:T(8,128)(2,1)} %get-tuple-element.19), channel_id=1, source_target_pairs={{0,4},{1,5},{2,6},{3,7},{4,8},{5,9},{6,10},{7,11},{8,12},{9,13},{1... | collective-permute-start | bytes 3145736 | tf_op jit(solution)/shard_map/ppermute | solution.py:233
  8.0 1.3 %collective-permute-start.1 = (bf16[1024,512]{1,0:T(8,128)(2,1)}, bf16[1024,512]{1,0:T(8,128)(2,1)}, u32[]{:S(2)}, u32[]{:S(2)}) collective-permute-start(bf16[1024,512]{1,0:T(8,128)(2,1)} %get-tuple-element.20), channel_id=1, source_target_pairs={{4,0},{5,1},{6,2},{7,3},{8,4},{9,5},{10,6},{11,7},{12,8},{13,9},{1... | collective-permute-start | bytes 3145736 | tf_op jit(solution)/shard_map/ppermute | solution.py:233
  9.3 1.6 %copy-done.2 = bf16[1024,1024]{1,0:T(8,128)(2,1)S(1)} copy-done((bf16[1024,1024]{1,0:T(8,128)(2,1)S(1)}, bf16[1024,1024]{1,0:T(8,128)(2,1)}, u32[]{:S(2)}) %copy-start.2) | copy-done | bytes 2097176
  10.9 1.7 %shard_map.57 = (f32[2,128,128]{2,1,0:T(8,128)S(1)}, f32[2,128,128]{2,1,0:T(8,128)S(1)}, f32[2,128,128]{2,1,0:T(8,128)S(1)}, f32[2,128,128]{2,1,0:T(8,128)}) custom-call(s32[1]{0:T(128)} %bitcast.9.place, bf16[1024,1024]{1,0:T(8,128)(2,1)S(1)} %bitcast.17, bf16[1024,1024]{1,0:T(8,128)(2,1)S(1)} %copy-done.2), custom_call_target="tpu_custom_call" | custom-call | flops 268435456 | bytes 4194304 | tf_op jit(solution)/shard_map/pallas_call | solution.py:144
  12.6 1.3 %collective-permute-start.10 = (f32[2,128,128]{2,1,0:T(8,128)}, f32[2,128,128]{2,1,0:T(8,128)}, u32[]{:S(2)}, u32[]{:S(2)}) collective-permute-start(f32[2,128,128]{2,1,0:T(8,128)} %get-tuple-element.28), channel_id=1, source_target_pairs={{12,15},{13,12},{14,13},{15,14},{28,31},{29,28},{30,29},{31,30}} | collective-permute-start | bytes 393224 | tf_op jit(solution)/shard_map/ppermute | solution.py:233
  13.9 1.3 %collective-permute-start.9 = (f32[2,128,128]{2,1,0:T(8,128)S(1)}, f32[2,128,128]{2,1,0:T(8,128)}, u32[]{:S(2)}, u32[]{:S(2)}) collective-permute-start(f32[2,128,128]{2,1,0:T(8,128)S(1)} %get-tuple-element.27), channel_id=1, source_target_pairs={{12,14},{13,15},{14,12},{15,13},{28,30},{29,31},{30,28},{31,29}} | collective-permute-start | bytes 393224 | tf_op jit(solution)/shard_map/ppermute | solution.py:233
  15.2 1.3 %collective-permute-start.8 = (f32[2,128,128]{2,1,0:T(8,128)S(1)}, f32[2,128,128]{2,1,0:T(8,128)}, u32[]{:S(2)}, u32[]{:S(2)}) collective-permute-start(f32[2,128,128]{2,1,0:T(8,128)S(1)} %get-tuple-element.26), channel_id=1, source_target_pairs={{12,13},{13,14},{14,15},{15,12},{28,29},{29,30},{30,31},{31,28}} | collective-permute-start | bytes 393224 | tf_op jit(solution)/shard_map/ppermute | solution.py:233
  19.5 3.3 %collective-permute-start.13 = (f32[2,4,128]{2,1,0:T(4,128)S(1)}, f32[2,4,128]{2,1,0:T(4,128)S(1)}, u32[]{:S(2)}, u32[]{:S(2)}) collective-permute-start(f32[2,4,128]{2,1,0:T(4,128)S(1)} %pad_maximum_fusion.refs_5_), channel_id=1, source_target_pairs={{0,4},{1,5},{2,6},{3,7},{4,8},{5,9},{6,10},{7,11},{8,12},{9,13},{1... | collective-permute-start | bytes 12296 | tf_op jit(solution)/shard_map/ppermute | solution.py:233
  22.9 10.2 %collective-permute-start.14 = (f32[2,4,128]{2,1,0:T(4,128)S(1)}, f32[2,4,128]{2,1,0:T(4,128)S(1)}, u32[]{:S(2)}, u32[]{:S(2)}) collective-permute-start(f32[2,4,128]{2,1,0:T(4,128)S(1)} %pad_maximum_fusion.refs_5_), channel_id=1, source_target_pairs={{0,8},{1,9},{2,10},{3,11},{4,12},{5,13},{6,14},{7,15},{8,0},{9,1},... | collective-permute-start | bytes 12296 | tf_op jit(solution)/shard_map/ppermute | solution.py:233
  33.1 1.7 %collective-permute-done.1.after = bf16[1024,512]{1,0:T(8,128)(2,1)} collective-permute-done((bf16[1024,512]{1,0:T(8,128)(2,1)}, bf16[1024,512]{1,0:T(8,128)(2,1)}, u32[]{:S(2)}, u32[]{:S(2)}) %collective-permute-start.1) | collective-permute-done | bytes 1048608 | tf_op jit(solution)/shard_map/ppermute | solution.py:233
  34.8 2.0 %shard_map.56 = (f32[2,128,128]{2,1,0:T(8,128)S(1)}, f32[2,128,128]{2,1,0:T(8,128)S(1)}, f32[2,128,128]{2,1,0:T(8,128)S(1)}, f32[2,128,128]{2,1,0:T(8,128)S(1)}) custom-call(s32[1]{0:T(128)} %bitcast.9.place, bf16[1024,1024]{1,0:T(8,128)(2,1)S(1)} %bitcast.18, bf16[1024,512]{1,0:T(8,128)(2,1)S(1)} %collective-permute-done.before, ...), custom_call_target="tpu_custom_call" | custom-call | flops 268435456 | bytes 4718592 | tf_op jit(solution)/shard_map/pallas_call | solution.py:174
  37.0 1.6 %collective-permute-start.3 = (f32[2,128,128]{2,1,0:T(8,128)S(1)}, f32[2,128,128]{2,1,0:T(8,128)S(1)}, u32[]{:S(2)}, u32[]{:S(2)}) collective-permute-start(f32[2,128,128]{2,1,0:T(8,128)S(1)} %get-tuple-element.23), channel_id=1, source_target_pairs={{0,2},{1,3},{2,0},{3,1},{4,6},{5,7},{6,4},{7,5},{8,10},{9,11},{10,... | collective-permute-start | bytes 393224 | tf_op jit(solution)/shard_map/ppermute | solution.py:233
  39.8 2.9 %collective-permute-start.15 = (f32[2,4,128]{2,1,0:T(4,128)S(1)}, f32[2,4,128]{2,1,0:T(4,128)S(1)}, u32[]{:S(2)}, u32[]{:S(2)}) collective-permute-start(f32[2,4,128]{2,1,0:T(4,128)S(1)} %pad_maximum_fusion.refs_5_), channel_id=1, source_target_pairs={{0,12},{1,13},{2,14},{3,15},{4,0},{5,1},{6,2},{7,3},{8,4},{9,5},{1... | collective-permute-start | bytes 12296 | tf_op jit(solution)/shard_map/ppermute | solution.py:233
  42.7 2.8 %collective-permute-done.3 = f32[2,128,128]{2,1,0:T(8,128)S(1)} collective-permute-done((f32[2,128,128]{2,1,0:T(8,128)S(1)}, f32[2,128,128]{2,1,0:T(8,128)S(1)}, u32[]{:S(2)}, u32[]{:S(2)}) %collective-permute-start.3) | collective-permute-done | bytes 131104 | tf_op jit(solution)/shard_map/ppermute | solution.py:233
  45.5 1.3 %collective-permute-start.12 = (f32[2,128,128]{2,1,0:T(8,128)S(1)}, f32[2,128,128]{2,1,0:T(8,128)S(1)}, u32[]{:S(2)}, u32[]{:S(2)}) collective-permute-start(f32[2,128,128]{2,1,0:T(8,128)S(1)} %broadcast_select_fusion), channel_id=1, source_target_pairs={{12,8},{13,9},{14,10},{15,11},{4,0},{5,1},{6,2},{7,3},{28,24},{29,... | collective-permute-start | bytes 393224 | tf_op jit(solution)/shard_map/ppermute | solution.py:233
  46.9 1.3 %collective-permute-start.5 = (f32[2,128,128]{2,1,0:T(8,128)S(1)}, f32[2,128,128]{2,1,0:T(8,128)S(1)}, u32[]{:S(2)}, u32[]{:S(2)}) collective-permute-start(f32[2,128,128]{2,1,0:T(8,128)S(1)} %add_add_fusion.1.refs_0_), channel_id=1, source_target_pairs={{1,5},{3,7},{4,8},{5,9},{6,10},{7,11},{8,12},{9,13},{10,14},{11,15... | collective-permute-start | bytes 393224 | tf_op jit(solution)/shard_map/ppermute | solution.py:233
  48.2 1.3 %collective-permute-start.6 = (f32[2,128,128]{2,1,0:T(8,128)S(1)}, f32[2,128,128]{2,1,0:T(8,128)S(1)}, u32[]{:S(2)}, u32[]{:S(2)}) collective-permute-start(f32[2,128,128]{2,1,0:T(8,128)S(1)} %add_add_fusion.1.refs_0_), channel_id=1, source_target_pairs={{1,9},{3,11},{4,12},{5,13},{6,14},{7,15},{8,0},{9,1},{10,2},{11,3}... | collective-permute-start | bytes 393224 | tf_op jit(solution)/shard_map/ppermute | solution.py:233
  49.5 3.0 %collective-permute-done.12 = f32[2,128,128]{2,1,0:T(8,128)S(1)} collective-permute-done((f32[2,128,128]{2,1,0:T(8,128)S(1)}, f32[2,128,128]{2,1,0:T(8,128)S(1)}, u32[]{:S(2)}, u32[]{:S(2)}) %collective-permute-start.12) | collective-permute-done | bytes 131104 | tf_op jit(solution)/shard_map/ppermute | solution.py:233
  52.5 1.3 %collective-permute-start.7 = (f32[2,128,128]{2,1,0:T(8,128)S(1)}, f32[2,128,128]{2,1,0:T(8,128)S(1)}, u32[]{:S(2)}, u32[]{:S(2)}) collective-permute-start(f32[2,128,128]{2,1,0:T(8,128)S(1)} %add_add_fusion.1.refs_0_), channel_id=1, source_target_pairs={{1,13},{3,15},{4,0},{5,1},{6,2},{7,3},{8,4},{9,5},{10,6},{11,7},{1... | collective-permute-start | bytes 393224 | tf_op jit(solution)/shard_map/ppermute | solution.py:233
  53.8 4.0 %collective-permute-done.5.refs_1_ = f32[2,128,128]{2,1,0:T(8,128)S(1)} collective-permute-done((f32[2,128,128]{2,1,0:T(8,128)S(1)}, f32[2,128,128]{2,1,0:T(8,128)S(1)}, u32[]{:S(2)}, u32[]{:S(2)}) %collective-permute-start.5) | collective-permute-done | bytes 131104 | tf_op jit(solution)/shard_map/ppermute | solution.py:233
  57.8 4.6 %collective-permute-done.6.refs_2_ = f32[2,128,128]{2,1,0:T(8,128)S(1)} collective-permute-done((f32[2,128,128]{2,1,0:T(8,128)S(1)}, f32[2,128,128]{2,1,0:T(8,128)S(1)}, u32[]{:S(2)}, u32[]{:S(2)}) %collective-permute-start.6) | collective-permute-done | bytes 131104 | tf_op jit(solution)/shard_map/ppermute | solution.py:233
  63.0 3.8 %shard_map.58 = f32[3,2,32,128]{3,2,1,0:T(8,128)} custom-call(s32[9]{0:T(128)S(1)} %stack.48.meta, f32[2,128,128]{2,1,0:T(8,128)S(1)} %add_add_fusion.1.refs_0_, f32[2,128,128]{2,1,0:T(8,128)S(1)} %collective-permute-done.5.refs_1_, f32[2,128,128]{2,1,0:T(8,128)S(1)} %collective-permute-done.6.refs_2_, f32[2,128,128]{2,1,0:T(8,128)S(1)} %collective-permute-done.7.refs_3_, ...), custom_call_target="tpu_custom_call" | custom-call | flops 503316480 | bytes 1048576 | tf_op jit(solution)/shard_map/pallas_call | solution.py:103
  (32 shorter events, 5.0 us)
Async XLA Ops:
  0.0 1.6 %copy-start = (bf16[1,1024,1024]{2,1,0:T(8,128)(2,1)S(1)}, bf16[1,1024,1024]{2,1,0:T(8,128)(2,1)}, u32[]{:S(2)}) copy-start(bf16[1,1024,1024]{2,1,0:T(8,128)(2,1)} %param.5) | copy-start | bytes 6291460
  1.6 7.7 %copy-start.1 = (bf16[1,1024,1024]{2,1,0:T(8,128)(2,1)S(1)}, bf16[1,1024,1024]{2,1,0:T(8,128)(2,1)}, u32[]{:S(2)}) copy-start(bf16[1,1024,1024]{2,1,0:T(8,128)(2,1)} %param.5) | copy-start | bytes 6291460
  3.0 30.2 %collective-permute-start = (bf16[1024,512]{1,0:T(8,128)(2,1)}, bf16[1024,512]{1,0:T(8,128)(2,1)S(1)}, u32[]{:S(2)}, u32[]{:S(2)}) collective-permute-start(bf16[1024,512]{1,0:T(8,128)(2,1)} %get-tuple-element.19), channel_id=1, source_target_pairs={{0,4},{1,5},{2,6},{3,7},{4,8},{5,9},{6,10},{7,11},{8,12},{9,13},{1... | collective-permute-start | bytes 3145736 | tf_op jit(solution)/shard_map/ppermute | solution.py:233
  8.0 26.9 %collective-permute-start.1 = (bf16[1024,512]{1,0:T(8,128)(2,1)}, bf16[1024,512]{1,0:T(8,128)(2,1)}, u32[]{:S(2)}, u32[]{:S(2)}) collective-permute-start(bf16[1024,512]{1,0:T(8,128)(2,1)} %get-tuple-element.20), channel_id=1, source_target_pairs={{4,0},{5,1},{6,2},{7,3},{8,4},{9,5},{10,6},{11,7},{12,8},{13,9},{1... | collective-permute-start | bytes 3145736 | tf_op jit(solution)/shard_map/ppermute | solution.py:233
  9.3 1.6 %copy-start.2 = (bf16[1024,1024]{1,0:T(8,128)(2,1)S(1)}, bf16[1024,1024]{1,0:T(8,128)(2,1)}, u32[]{:S(2)}) copy-start(bf16[1024,1024]{1,0:T(8,128)(2,1)} %after.1) | copy-start | bytes 6291460
  10.9 6.4 %copy-start.3 = (s32[1,8,2]{1,2,0:T(2,128)S(1)}, s32[1,8,2]{1,2,0:T(2,128)}, u32[]{:S(2)}) copy-start(s32[1,8,2]{1,2,0:T(2,128)} %param.7) | copy-start | bytes 196
  12.6 5.0 %collective-permute-start.10 = (f32[2,128,128]{2,1,0:T(8,128)}, f32[2,128,128]{2,1,0:T(8,128)}, u32[]{:S(2)}, u32[]{:S(2)}) collective-permute-start(f32[2,128,128]{2,1,0:T(8,128)} %get-tuple-element.28), channel_id=1, source_target_pairs={{12,15},{13,12},{14,13},{15,14},{28,31},{29,28},{30,29},{31,30}} | collective-permute-start | bytes 393224 | tf_op jit(solution)/shard_map/ppermute | solution.py:233
  13.9 3.7 %collective-permute-start.9 = (f32[2,128,128]{2,1,0:T(8,128)S(1)}, f32[2,128,128]{2,1,0:T(8,128)}, u32[]{:S(2)}, u32[]{:S(2)}) collective-permute-start(f32[2,128,128]{2,1,0:T(8,128)S(1)} %get-tuple-element.27), channel_id=1, source_target_pairs={{12,14},{13,15},{14,12},{15,13},{28,30},{29,31},{30,28},{31,29}} | collective-permute-start | bytes 393224 | tf_op jit(solution)/shard_map/ppermute | solution.py:233
  15.2 2.4 %collective-permute-start.8 = (f32[2,128,128]{2,1,0:T(8,128)S(1)}, f32[2,128,128]{2,1,0:T(8,128)}, u32[]{:S(2)}, u32[]{:S(2)}) collective-permute-start(f32[2,128,128]{2,1,0:T(8,128)S(1)} %get-tuple-element.26), channel_id=1, source_target_pairs={{12,13},{13,14},{14,15},{15,12},{28,29},{29,30},{30,31},{31,28}} | collective-permute-start | bytes 393224 | tf_op jit(solution)/shard_map/ppermute | solution.py:233
  18.7 19.8 %collective-permute-start.11 = (f32[2,128,128]{2,1,0:T(8,128)S(1)}, f32[2,128,128]{2,1,0:T(8,128)S(1)}, u32[]{:S(2)}, u32[]{:S(2)}) collective-permute-start(f32[2,128,128]{2,1,0:T(8,128)S(1)} %add_add_fusion), channel_id=1, source_target_pairs={{12,4},{13,5},{14,6},{15,7},{28,20},{29,21},{30,22},{31,23}} | collective-permute-start | bytes 393224 | tf_op jit(solution)/shard_map/ppermute | solution.py:233
  19.5 28.6 %collective-permute-start.13 = (f32[2,4,128]{2,1,0:T(4,128)S(1)}, f32[2,4,128]{2,1,0:T(4,128)S(1)}, u32[]{:S(2)}, u32[]{:S(2)}) collective-permute-start(f32[2,4,128]{2,1,0:T(4,128)S(1)} %pad_maximum_fusion.refs_5_), channel_id=1, source_target_pairs={{0,4},{1,5},{2,6},{3,7},{4,8},{5,9},{6,10},{7,11},{8,12},{9,13},{1... | collective-permute-start | bytes 12296 | tf_op jit(solution)/shard_map/ppermute | solution.py:233
  22.9 30.9 %collective-permute-start.14 = (f32[2,4,128]{2,1,0:T(4,128)S(1)}, f32[2,4,128]{2,1,0:T(4,128)S(1)}, u32[]{:S(2)}, u32[]{:S(2)}) collective-permute-start(f32[2,4,128]{2,1,0:T(4,128)S(1)} %pad_maximum_fusion.refs_5_), channel_id=1, source_target_pairs={{0,8},{1,9},{2,10},{3,11},{4,12},{5,13},{6,14},{7,15},{8,0},{9,1},... | collective-permute-start | bytes 12296 | tf_op jit(solution)/shard_map/ppermute | solution.py:233
  36.9 2.9 %collective-permute-start.4 = (f32[2,128,128]{2,1,0:T(8,128)S(1)}, f32[2,128,128]{2,1,0:T(8,128)S(1)}, u32[]{:S(2)}, u32[]{:S(2)}) collective-permute-start(f32[2,128,128]{2,1,0:T(8,128)S(1)} %get-tuple-element.24), channel_id=1, source_target_pairs={{0,3},{1,0},{2,1},{3,2},{4,7},{5,4},{6,5},{7,6},{8,11},{9,8},{10,9... | collective-permute-start | bytes 393224 | tf_op jit(solution)/shard_map/ppermute | solution.py:233
  37.0 8.6 %collective-permute-start.3 = (f32[2,128,128]{2,1,0:T(8,128)S(1)}, f32[2,128,128]{2,1,0:T(8,128)S(1)}, u32[]{:S(2)}, u32[]{:S(2)}) collective-permute-start(f32[2,128,128]{2,1,0:T(8,128)S(1)} %get-tuple-element.23), channel_id=1, source_target_pairs={{0,2},{1,3},{2,0},{3,1},{4,6},{5,7},{6,4},{7,5},{8,10},{9,11},{10,... | collective-permute-start | bytes 393224 | tf_op jit(solution)/shard_map/ppermute | solution.py:233
  38.5 8.3 %collective-permute-start.2 = (f32[2,128,128]{2,1,0:T(8,128)S(1)}, f32[2,128,128]{2,1,0:T(8,128)S(1)}, u32[]{:S(2)}, u32[]{:S(2)}) collective-permute-start(f32[2,128,128]{2,1,0:T(8,128)S(1)} %get-tuple-element.22), channel_id=1, source_target_pairs={{0,1},{1,2},{2,3},{3,0},{4,5},{5,6},{6,7},{7,4},{8,9},{9,10},{10,1... | collective-permute-start | bytes 393224 | tf_op jit(solution)/shard_map/ppermute | solution.py:233
  39.8 14.0 %collective-permute-start.15 = (f32[2,4,128]{2,1,0:T(4,128)S(1)}, f32[2,4,128]{2,1,0:T(4,128)S(1)}, u32[]{:S(2)}, u32[]{:S(2)}) collective-permute-start(f32[2,4,128]{2,1,0:T(4,128)S(1)} %pad_maximum_fusion.refs_5_), channel_id=1, source_target_pairs={{0,12},{1,13},{2,14},{3,15},{4,0},{5,1},{6,2},{7,3},{8,4},{9,5},{1... | collective-permute-start | bytes 12296 | tf_op jit(solution)/shard_map/ppermute | solution.py:233
  45.5 7.0 %collective-permute-start.12 = (f32[2,128,128]{2,1,0:T(8,128)S(1)}, f32[2,128,128]{2,1,0:T(8,128)S(1)}, u32[]{:S(2)}, u32[]{:S(2)}) collective-permute-start(f32[2,128,128]{2,1,0:T(8,128)S(1)} %broadcast_select_fusion), channel_id=1, source_target_pairs={{12,8},{13,9},{14,10},{15,11},{4,0},{5,1},{6,2},{7,3},{28,24},{29,... | collective-permute-start | bytes 393224 | tf_op jit(solution)/shard_map/ppermute | solution.py:233
  46.9 11.0 %collective-permute-start.5 = (f32[2,128,128]{2,1,0:T(8,128)S(1)}, f32[2,128,128]{2,1,0:T(8,128)S(1)}, u32[]{:S(2)}, u32[]{:S(2)}) collective-permute-start(f32[2,128,128]{2,1,0:T(8,128)S(1)} %add_add_fusion.1.refs_0_), channel_id=1, source_target_pairs={{1,5},{3,7},{4,8},{5,9},{6,10},{7,11},{8,12},{9,13},{10,14},{11,15... | collective-permute-start | bytes 393224 | tf_op jit(solution)/shard_map/ppermute | solution.py:233
  48.2 14.3 %collective-permute-start.6 = (f32[2,128,128]{2,1,0:T(8,128)S(1)}, f32[2,128,128]{2,1,0:T(8,128)S(1)}, u32[]{:S(2)}, u32[]{:S(2)}) collective-permute-start(f32[2,128,128]{2,1,0:T(8,128)S(1)} %add_add_fusion.1.refs_0_), channel_id=1, source_target_pairs={{1,9},{3,11},{4,12},{5,13},{6,14},{7,15},{8,0},{9,1},{10,2},{11,3}... | collective-permute-start | bytes 393224 | tf_op jit(solution)/shard_map/ppermute | solution.py:233
  52.5 10.5 %collective-permute-start.7 = (f32[2,128,128]{2,1,0:T(8,128)S(1)}, f32[2,128,128]{2,1,0:T(8,128)S(1)}, u32[]{:S(2)}, u32[]{:S(2)}) collective-permute-start(f32[2,128,128]{2,1,0:T(8,128)S(1)} %add_add_fusion.1.refs_0_), channel_id=1, source_target_pairs={{1,13},{3,15},{4,0},{5,1},{6,2},{7,3},{8,4},{9,5},{10,6},{11,7},{1... | collective-permute-start | bytes 393224 | tf_op jit(solution)/shard_map/ppermute | solution.py:233

commit v3 on v2

v3 whole, which is shorter than its diff:
```python
import functools

import jax
import jax.numpy as jnp
from jax import lax
from jax.experimental import pallas as pl
from jax.experimental.pallas import tpu as pltpu
from jax.sharding import PartitionSpec as P

BLOCK = 4
AXES = ("sec", "grid")
ROOM = pltpu.CompilerParams(vmem_limit_bytes=16 * 2**20)


def halves(matrix):
    high = matrix.astype(jnp.bfloat16)
    return high, (matrix - high.astype(jnp.float32)).astype(jnp.bfloat16)


def mul(left, right, flip=False):
    dims = (((1,), (1 if flip else 0,)), ((), ()))

    def dot(a, b):
        return lax.dot_general(a, b, dims, preferred_element_type=jnp.float32)

    return dot(left[0], right[0]) + (dot(left[0], right[1]) + dot(left[1], right[0]))


def star_body(place, *refs, orders, rows):
    terms = refs[:BLOCK]
    out, tbuf, abuf, rbuf = refs[BLOCK:]
    width = out.shape[-1]
    for slot in range(BLOCK):
        origin = lax.rem(place[1] + BLOCK - slot, BLOCK)
        tbuf[lax.rem(origin + BLOCK - place[2], BLOCK)] = terms[slot][:, :width]
        abuf[origin] = terms[slot][:, width:]
    first_row = place[1] * rows if rows < width else 0
    picked = pl.ds(pl.multiple_of(first_row, 8), rows) if rows < width else pl.ds(0, rows)
    row = lax.broadcasted_iota(jnp.int32, (width, width), 0)
    col = lax.broadcasted_iota(jnp.int32, (width, width), 1)
    part_row = lax.broadcasted_iota(jnp.int32, (rows, width), 0) + first_row
    part_col = lax.broadcasted_iota(jnp.int32, (rows, width), 1)
    upper = jnp.logical_and(row < width // 2, col >= width // 2)
    lower = jnp.logical_and(row >= width // 2, col < width // 2)

    def diag(vector):
        return jnp.where(row == col, vector, 0.0)

    def part_diag(vector):
        return jnp.where(part_row == part_col, vector, 0.0)

    for order in range(orders):
        trans, front, back = [], [], []
        for sec in range(BLOCK):
            decay = abuf[sec, order, 0:1, :]
            mirror = abuf[sec, order, 1:2, :]
            mask = jnp.where(
                upper, abuf[sec, order, 2:3, :], jnp.where(lower, abuf[sec, order, 3:4, :], 1.0)
            )
            passing = jnp.broadcast_to(jnp.sqrt(1.0 - mirror * mirror), (width, width)).T
            trans.append(passing * (tbuf[sec, order] * mask) * decay)
            front.append(decay * decay * mirror)
            back.append(-mirror)
        bounce_a = back[0] * front[1]
        bounce_b = back[2] * front[3]
        gain_a = (1.0 + bounce_a * bounce_a) * (1.0 + bounce_a)
        gain_b = (1.0 + bounce_b * bounce_b) * (1.0 + bounce_b)
        flip_0 = trans[0].T
        flip_2 = trans[2].T
        rbuf[0] = flip_0
        rbuf[1] = trans[3]
        flip_0_part = rbuf[0, picked, :]
        trans_3_part = rbuf[1, picked, :]
        s0, s1, s2, s3 = [halves(t) for t in trans]
        trans_a = halves(mul(halves(trans[1] * gain_a), s0))
        back_a = halves(diag(back[1]) + mul(halves(trans[1] * (back[0] * gain_a)), s1, True))
        front_b = halves(diag(front[2]) + mul(halves(flip_2 * (front[3] * gain_b)), s2))
        trans_b = halves(mul(halves(trans[3] * gain_b), s2))
        flip_a_part = halves(mul(halves(flip_0_part * gain_a), s1, True))
        trans_b_part = mul(halves(trans_3_part * gain_b), s2)
        front_a_part = part_diag(front[0]) + mul(halves(flip_0_part * (front[1] * gain_a)), s0)
        back_b_part = part_diag(back[3]) + mul(halves(trans_3_part * (back[2] * gain_b)), s3, True)
        bounce = halves(mul(back_a, front_b))
        ahead = jnp.concatenate([trans_b_part, mul(flip_a_part, front_b)], axis=0)
        behind = mul(halves(trans_b_part), back_a)
        ahead = ahead + mul(halves(mul(halves(ahead), bounce)), bounce)
        behind = behind + mul(halves(mul(halves(behind), bounce, True)), bounce, True)
        ahead = ahead + mul(halves(ahead), bounce)
        behind = behind + mul(halves(behind), bounce, True)
        ahead = mul(halves(ahead), trans_a)
        out[0, order] = ahead[:rows]
        out[1, order] = front_a_part + ahead[rows:]
        out[2, order] = back_b_part + mul(halves(behind), trans_b, True)


def star_of_four(place, terms, rows):
    orders, width = terms[0].shape[0], terms[0].shape[-1]
    extra = terms[0].shape[1] - width
    vmem = pl.BlockSpec(memory_space=pltpu.VMEM)
    return pl.pallas_call(
        functools.partial(star_body, orders=orders, rows=rows),
        out_shape=jax.ShapeDtypeStruct((3, orders, rows, width), jnp.float32),
        in_specs=[pl.BlockSpec(memory_space=pltpu.SMEM)] + [vmem] * BLOCK,
        out_specs=vmem,
        scratch_shapes=[
            pltpu.VMEM((BLOCK, orders, width, width), jnp.float32),
            pltpu.VMEM((BLOCK, orders, extra, width), jnp.float32),
            pltpu.VMEM((2, width, width), jnp.float32),
        ],
        compiler_params=ROOM,
        cost_estimate=pl.CostEstimate(
            flops=orders * 120 * width**3, bytes_accessed=orders * 8 * 4 * width**2, transcendentals=0
        ),
    )(place, *terms)


def own_body(place, pattern, decays, mirrors, *refs):
    parts, (exits, hop, out) = refs[:-3], refs[-3:]
    width = out.shape[-1]
    out[:, width:] = jnp.zeros_like(out[:, width:])
    share = out.shape[0]
    for index in range(share):
        total = parts[0][index]
        for part in parts[1:]:
            total = total + part[index]
        total = jnp.where(place[3] == 1, exits[index], total)
        out[index, :width] = jnp.where(place[3] == 2, hop[index], total)
        order = place[0] * share + index
        columns = pl.ds(pl.multiple_of(order * width, width), width)
        out[index, width : width + 1] = decays[:, columns]
        out[index, width + 1 : width + 2] = mirrors[:, columns]
        for side in (0, 1):
            flag = pattern[0, order, side].astype(jnp.float32)
            out[index, width + 2 + side : width + 3 + side] = jnp.full((1, width), flag)


def own_terms(place, pattern, decays, mirrors, parts, exits, hop):
    number, width = parts[0].shape[0], parts[0].shape[-1]
    vmem, smem = pl.BlockSpec(memory_space=pltpu.VMEM), pl.BlockSpec(memory_space=pltpu.SMEM)
    return pl.pallas_call(
        own_body,
        out_shape=jax.ShapeDtypeStruct((number, width + 8, width), jnp.float32),
        in_specs=[smem] * 2 + [vmem] * (4 + len(parts)),
        out_specs=vmem,
        compiler_params=ROOM,
        cost_estimate=pl.CostEstimate(
            flops=4 * number * width**2, bytes_accessed=28 * number * width**2, transcendentals=0
        ),
    )(place, pattern, decays, mirrors, *parts, exits, hop)


def tall_dot(left, right):
    dims = (((0,), (0,)), ((), ()))
    return lax.dot_general(left, right, dims, preferred_element_type=jnp.float32)


def hand_out(place, terms, outs):
    count = len(outs)
    for turn, out in enumerate(outs):
        out[...] = terms[lax.rem(place[0] + turn, count)]


def exit_body(place, own, after, *refs):
    outs, terms = refs[:-1], refs[-1]
    count, share, width = terms.shape[:3]
    for spot in range(count):
        for item in range(share):
            columns = pl.ds((spot * share + item) * width, width)
            terms[spot, item] = tall_dot(own[:, columns], after[:, columns])
    hand_out(place, terms, outs)


def exit_sums(place, fields, exit_modes, count, share, width):
    points, modes = fields.shape
    whole = pl.BlockSpec(memory_space=pltpu.VMEM)
    return pl.pallas_call(
        exit_body,
        out_shape=[jax.ShapeDtypeStruct((share, width, width), jnp.float32)] * count,
        in_specs=[pl.BlockSpec(memory_space=pltpu.SMEM), whole, whole],
        out_specs=[whole] * count,
        scratch_shapes=[pltpu.VMEM((count, share, width, width), jnp.float32)],
        compiler_params=ROOM,
        cost_estimate=pl.CostEstimate(
            flops=2 * points * modes * width, bytes_accessed=4 * points * modes, transcendentals=0
        ),
    )(place, fields, exit_modes)


def inner_body(place, fields, arrived, *refs):
    outs, terms = refs[:-1], refs[-1]
    count, share, width = terms.shape[:3]

    def fill(left, right):
        for order in range(count * share):
            columns = pl.ds(order * width, width)
            terms[order // share, order % share] = tall_dot(left[:, columns], right[:, columns])

    even = lax.rem(place[0], 2) == 0

    @pl.when(even)
    def _():
        fill(arrived, fields)

    @pl.when(jnp.logical_not(even))
    def _():
        fill(fields, arrived)

    hand_out(place, terms, outs)


def inner_sums(place, fields, arrived, count, share, width):
    points, modes = fields.shape
    whole = pl.BlockSpec(memory_space=pltpu.VMEM)
    return pl.pallas_call(
        inner_body,
        out_shape=[jax.ShapeDtypeStruct((share, width, width), jnp.float32)] * count,
        in_specs=[pl.BlockSpec(memory_space=pltpu.SMEM), whole, whole],
        out_specs=[whole] * count,
        scratch_shapes=[pltpu.VMEM((count, share, width, width), jnp.float32)],
        compiler_params=ROOM,
        cost_estimate=pl.CostEstimate(
            flops=2 * points * modes * width, bytes_accessed=4 * points * modes, transcendentals=0
        ),
    )(place, fields, arrived)


def body(modes, exit_modes, pattern, attenuation, reflection):
    sections, count = lax.axis_size("sec"), lax.axis_size("grid")
    sec, spot = lax.axis_index("sec"), lax.axis_index("grid")
    orders = pattern.shape[1]
    width = modes.shape[2] // orders
    share = orders // count
    fields = modes[0]
    final = sections - 1
    small = sections == BLOCK
    even = 1 - lax.rem(spot, 2)
    if small:
        late = even
        special = jnp.where(even == 1, jnp.where(sec == 0, 2, 0), jnp.where(sec == final, 1, 0))
    else:
        late = 0 * even
        special = jnp.where(sec == final, 1, 0)
    place = jnp.stack([spot, sec, late, special]).astype(jnp.int32)

    def send(value, pairs):
        return lax.ppermute(value, AXES, [(s * count + g, t * count + h) for (s, g), (t, h) in pairs])

    def gathered(parts, members):
        got = [parts[0]]
        for turn in range(1, count):
            got.append(send(parts[turn], [(row[g], row[(g + turn) % count]) for row in members for g in range(count)]))
        return got

    steps = [((s + g % 2, g), (s + 1 - g % 2, g)) for s in range(final) for g in range(count)]
    arrived = send(fields, steps)

    exit_parts = exit_sums(place, fields, exit_modes, count, share, width)
    exits = sum(gathered(exit_parts, [[(final, g) for g in range(count)]]))
    hop = send(exits, [((final, g), (0, g)) for g in range(0, count, 2)]) if small else exits

    parts = inner_sums(place, fields, arrived, count, share, width)
    parts = gathered(parts, [[(s + 1 - g % 2, g) for g in range(count)] for s in range(final)])
    if not small:
        own = sum(parts)
        back = send(own, [((s + 1, g), (s, g)) for s in range(final) for g in range(0, count, 2)])
        parts = [jnp.where(even == 1, back, own)]
    own = own_terms(place, pattern, attenuation, reflection, parts, exits, hop)
    terms = [own]
    for turn in range(1, BLOCK):
        ring = [(s, s - s % BLOCK + (s + turn) % BLOCK) for s in range(sections)]
        terms.append(send(own, [((s, g), (t, g)) for s, t in ring for g in range(count)]))
    merged = star_of_four(place, terms, width // sections if small else width)
    return merged if small else later_levels(merged, sections, sec)


def pair_body(first, second, out):
    for order in range(out.shape[1]):
        trans_a, front_a, back_a = (first[i, order] for i in range(3))
        trans_b, front_b, back_b = (second[i, order] for i in range(3))
        bounce = halves(mul(halves(back_a), halves(front_b)))
        square = halves(mul(bounce, bounce))
        inner = trans_a + mul(bounce, halves(trans_a))
        inner = halves(inner + mul(square, halves(inner)))
        behind = trans_b + mul(halves(trans_b), bounce)
        behind = halves(behind + mul(halves(behind), square))
        left = halves(trans_b)
        out[0, order] = mul(left, inner)
        out[1, order] = front_a + mul(halves(trans_a.T), halves(mul(halves(front_b), inner)))
        out[2, order] = back_b + mul(left, halves(mul(halves(back_a), behind, True)))


def later_levels(merged, sections, sec):
    vmem = pl.BlockSpec(memory_space=pltpu.VMEM)
    star = pl.pallas_call(
        pair_body, out_shape=jax.ShapeDtypeStruct(merged.shape, merged.dtype), in_specs=[vmem] * 2, out_specs=vmem
    )
    stride = BLOCK
    while stride < sections:
        other = lax.ppermute(merged, "sec", [(s, s ^ stride) for s in range(sections)])
        high = lax.rem(lax.div(sec, stride), 2) == 1
        merged = star(jnp.where(high, other, merged), jnp.where(high, merged, other))
        stride *= 2
    rows = merged.shape[2] // sections
    return lax.dynamic_slice_in_dim(merged, sec * rows, rows, 2)


def solution(mesh):
    in_specs = (
        P(("groups", "sec"), "grid", None),
        P(("groups", "grid"), None),
        P(("groups", "sec"), None, None),
        P(("groups", "sec"), None),
        P(("groups", "sec"), None),
    )
    out_specs = P("groups", "grid", "sec", None)
    return jax.shard_map(body, mesh=mesh, in_specs=in_specs, out_specs=out_specs, check_vma=False)
```

time: 67.2 us -> 63 us (0.938); the launches traced: 66.8 us -> 61.9 us
  starting transfers between devices: 34.2 us -> 26.8 us
  waiting for transfers between devices: 17.8 us -> 23.8 us
  Pallas kernels: 8.91 us -> 7.67 us
  local copies, waits for them, and re-layouts: 4.39 us -> 3.28 us
  other arithmetic: 1.21 us -> 0.11 us
    ppermute x16 -> x11, starting transfers between devices: 34.2 us -> 26.8 us  [send(): lax.ppermute(value, AXES, [(s * count + g, t * count + h) for (s, g), (t,...]
    ppermute x16 -> x11, waiting for transfers between devices: 17.8 us -> 23.8 us  [send(): lax.ppermute(value, AXES, [(s * count + g, t * count + h) for (s, g), (t,...]
    pallas_call x3, Pallas kernels: 7.18 us -> 6.05 us  [the longest x1 3.78 us: star_of_four(): pl.pallas_call(functools.partial(star_body, orders=orders, rows=rows), ou...]
    add x2 -> x1, other arithmetic: 1.09 us -> 0.03 us  [body(): exits = sum(gathered(exit_parts, [[(final, g) for g in range(count)]]))]
    dynamic_slice x1 -> x0, local copies, waits for them, and re-layouts: 0.71 us -> none  [own_orders(): return lax.dynamic_slice_in_dim(value, spot * share, share, 0)]
    unnamed x8 -> x11, local copies, waits for them, and re-layouts: 3.18 us -> 3.28 us
  transfers between devices with their start and end apart: 16 -> 11, of which waited for: 7 -> 3; matrix products, arithmetic and copies ran while one was open for 4% -> 0% of each run, Pallas kernels for 6% -> 5%
where the time goes in v3:
time: 63 us; the launch traced here: 61.9 us
  starting transfers between devices  26.8 us (43%)
  waiting for transfers between devices  23.8 us (38%)
  Pallas kernels  7.67 us (12%)
  local copies, waits for them, and re-layouts  3.28 us (5%)
    ppermute x11, starting transfers between devices, send(): lax.ppermute(value, AXES, [(s * count + g, t * count + h) for (s, g), (t,...  26.8 us
    ppermute x11, waiting for transfers between devices, send(): lax.ppermute(value, AXES, [(s * count + g, t * count + h) for (s, g), (t,...  23.8 us
    pallas_call x1, Pallas kernels, star_of_four(): pl.pallas_call(functools.partial(star_body, orders=orders, rows=rows), ou...  3.78 us
    unnamed x11, local copies, waits for them, and re-layouts  3.28 us
    pallas_call x1, Pallas kernels, inner_sums(): pl.pallas_call(inner_body, out_shape=[jax.ShapeDtypeStruct((share, width,...  1.63 us
    pallas_call x1, Pallas kernels, exit_sums(): pl.pallas_call(exit_body, out_shape=[jax.ShapeDtypeStruct((share, width,...  1.62 us
  transfers between devices with their start and end apart: 11, of which 3 were waited for; matrix products, arithmetic and copies ran while one was open for 0% of the time, Pallas kernels for 5%

profile of v3, /device:TPU:0, one launch (start us, length us, event | category | flops | bytes accessed | tf_op | source)
XLA Modules:
  0.0 61.9 jit_solution(853798806288000201)
XLA Ops:
  0.0 5.1 %collective-permute-start = (bf16[1024,1024]{1,0:T(8,128)(2,1)}, bf16[1024,1024]{1,0:T(8,128)(2,1)S(1)}, u32[]{:S(2)}, u32[]{:S(2)}) collective-permute-start(bf16[1024,1024]{1,0:T(8,128)(2,1)} %bitcast.5), channel_id=1, source_target_pairs={{0,4},{5,1},{2,6},{7,3},{4,8},{9,5},{6,10},{11,7},{8,12},{13,9},{1... | collective-permute-start | bytes 6291464 | tf_op jit(solution)/shard_map/ppermute | solution.py:246
  5.1 0.1 pad_add_fusion.place
  5.2 1.6 %copy-done = bf16[1,1024,1024]{2,1,0:T(8,128)(2,1)S(1)} copy-done((bf16[1,1024,1024]{2,1,0:T(8,128)(2,1)S(1)}, bf16[1,1024,1024]{2,1,0:T(8,128)(2,1)}, u32[]{:S(2)}) %copy-start) | copy-done | bytes 2097176
  6.8 1.6 %copy-done.1 = bf16[1024,1024]{1,0:T(8,128)(2,1)S(1)} copy-done((bf16[1024,1024]{1,0:T(8,128)(2,1)S(1)}, bf16[1024,1024]{1,0:T(8,128)(2,1)}, u32[]{:S(2)}) %copy-start.1) | copy-done | bytes 2097176
  8.3 1.6 %shard_map.56 = (f32[2,128,128]{2,1,0:T(8,128)S(1)}, f32[2,128,128]{2,1,0:T(8,128)S(1)}, f32[2,128,128]{2,1,0:T(8,128)S(1)}, f32[2,128,128]{2,1,0:T(8,128)S(1)}) custom-call(s32[4]{0:T(128)S(1)} %pad_add_fusion.place, bf16[1024,1024]{1,0:T(8,128)(2,1)S(1)} %bitcast.6, bf16[1024,1024]{1,0:T(8,128)(2,1)S(1)} %copy-done.1), custom_call_target="tpu_custom_call" | custom-call | flops 268435456 | bytes 4194304 | tf_op jit(solution)/shard_map/pallas_call | solution.py:176
  10.0 0.7 %collective-permute-start.6 = (f32[2,128,128]{2,1,0:T(8,128)S(1)}, f32[2,128,128]{2,1,0:T(8,128)S(1)}, u32[]{:S(2)}, u32[]{:S(2)}) collective-permute-start(f32[2,128,128]{2,1,0:T(8,128)S(1)} %get-tuple-element.20), channel_id=1, source_target_pairs={{12,15},{13,12},{14,13},{15,14},{28,31},{29,28},{30,29},{31,30}} | collective-permute-start | bytes 393224 | tf_op jit(solution)/shard_map/ppermute | solution.py:246
  10.6 0.7 %collective-permute-start.5 = (f32[2,128,128]{2,1,0:T(8,128)S(1)}, f32[2,128,128]{2,1,0:T(8,128)S(1)}, u32[]{:S(2)}, u32[]{:S(2)}) collective-permute-start(f32[2,128,128]{2,1,0:T(8,128)S(1)} %get-tuple-element.19), channel_id=1, source_target_pairs={{12,14},{13,15},{14,12},{15,13},{28,30},{29,31},{30,28},{31,29}} | collective-permute-start | bytes 393224 | tf_op jit(solution)/shard_map/ppermute | solution.py:246
  11.3 0.7 %collective-permute-start.4 = (f32[2,128,128]{2,1,0:T(8,128)S(1)}, f32[2,128,128]{2,1,0:T(8,128)S(1)}, u32[]{:S(2)}, u32[]{:S(2)}) collective-permute-start(f32[2,128,128]{2,1,0:T(8,128)S(1)} %get-tuple-element.18), channel_id=1, source_target_pairs={{12,13},{13,14},{14,15},{15,12},{28,29},{29,30},{30,31},{31,28}} | collective-permute-start | bytes 393224 | tf_op jit(solution)/shard_map/ppermute | solution.py:246
  12.1 0.0 copy-start.2
  12.1 0.0 copy-start.3
  12.1 1.4 %collective-permute-start.7 = (f32[2,128,128]{2,1,0:T(8,128)S(1)}, f32[2,128,128]{2,1,0:T(8,128)S(1)}, u32[]{:S(2)}, u32[]{:S(2)}) collective-permute-start(f32[2,128,128]{2,1,0:T(8,128)S(1)} %add_add_fusion.refs_4_), channel_id=1, source_target_pairs={{12,0},{14,2},{28,16},{30,18}} | collective-permute-start | bytes 393224 | tf_op jit(solution)/shard_map/ppermute | solution.py:246
  13.5 15.2 %collective-permute-done.arrived = bf16[1024,1024]{1,0:T(8,128)(2,1)S(1)} collective-permute-done((bf16[1024,1024]{1,0:T(8,128)(2,1)}, bf16[1024,1024]{1,0:T(8,128)(2,1)S(1)}, u32[]{:S(2)}, u32[]{:S(2)}) %collective-permute-start) | collective-permute-done | bytes 2097184 | tf_op jit(solution)/shard_map/ppermute | solution.py:246
  28.8 1.6 %shard_map.55 = (f32[2,128,128]{2,1,0:T(8,128)S(1)}, f32[2,128,128]{2,1,0:T(8,128)S(1)}, f32[2,128,128]{2,1,0:T(8,128)S(1)}, f32[2,128,128]{2,1,0:T(8,128)S(1)}) custom-call(s32[4]{0:T(128)S(1)} %pad_add_fusion.place, bf16[1024,1024]{1,0:T(8,128)(2,1)S(1)} %bitcast.7, bf16[1024,1024]{1,0:T(8,128)(2,1)S(1)} %collective-permute-done.arrived), custom_call_target="tpu_custom_call" | custom-call | flops 268435456 | bytes 4194304 | tf_op jit(solution)/shard_map/pallas_call | solution.py:214
  30.4 0.7 %collective-permute-start.1 = (f32[2,128,128]{2,1,0:T(8,128)S(1)}, f32[2,128,128]{2,1,0:T(8,128)S(1)}, u32[]{:S(2)}, u32[]{:S(2)}) collective-permute-start(f32[2,128,128]{2,1,0:T(8,128)S(1)} %get-tuple-element.14), channel_id=1, source_target_pairs={{4,1},{1,6},{6,3},{3,4},{8,5},{5,10},{10,7},{7,8},{12,9},{9,14},{1... | collective-permute-start | bytes 393224 | tf_op jit(solution)/shard_map/ppermute | solution.py:246
  31.1 0.7 %collective-permute-start.2 = (f32[2,128,128]{2,1,0:T(8,128)S(1)}, f32[2,128,128]{2,1,0:T(8,128)S(1)}, u32[]{:S(2)}, u32[]{:S(2)}) collective-permute-start(f32[2,128,128]{2,1,0:T(8,128)S(1)} %get-tuple-element.15), channel_id=1, source_target_pairs={{4,6},{1,3},{6,4},{3,1},{8,10},{5,7},{10,8},{7,5},{12,14},{9,11},{... | collective-permute-start | bytes 393224 | tf_op jit(solution)/shard_map/ppermute | solution.py:246
  31.8 0.7 %collective-permute-start.3 = (f32[2,128,128]{2,1,0:T(8,128)S(1)}, f32[2,128,128]{2,1,0:T(8,128)S(1)}, u32[]{:S(2)}, u32[]{:S(2)}) collective-permute-start(f32[2,128,128]{2,1,0:T(8,128)S(1)} %get-tuple-element.16), channel_id=1, source_target_pairs={{4,3},{1,4},{6,1},{3,6},{8,7},{5,8},{10,5},{7,10},{12,11},{9,12},{... | collective-permute-start | bytes 393224 | tf_op jit(solution)/shard_map/ppermute | solution.py:246
  32.5 0.1 copy.6.pattern
  32.6 0.6 %shard_map.57.refs_0_ = f32[2,136,128]{2,1,0:T(8,128)S(1)} custom-call(s32[4]{0:T(128)S(1)} %pad_add_fusion.place, s32[1,8,2]{2,1,0:T(8,128)S(1)} %copy.6.pattern, f32[1,1024]{1,0:T(1,128)S(1)} %copy-done.2, f32[1,1024]{1,0:T(1,128)S(1)} %copy-done.3, f32[2,128,128]{2,1,0:T(8,128)S(1)} %get-tuple-element.13.refs_0_, ...), custom_call_target="tpu_custom_call" | custom-call | flops 131072 | bytes 917504 | tf_op jit(solution)/shard_map/pallas_call | solution.py:140
  33.2 12.4 %collective-permute-start.8 = (f32[2,136,128]{2,1,0:T(8,128)S(1)}, f32[2,136,128]{2,1,0:T(8,128)S(1)}, u32[]{:S(2)}, u32[]{:S(2)}) collective-permute-start(f32[2,136,128]{2,1,0:T(8,128)S(1)} %shard_map.57.refs_0_), channel_id=1, source_target_pairs={{0,4},{1,5},{2,6},{3,7},{4,8},{5,9},{6,10},{7,11},{8,12},{9,13},{1... | collective-permute-start | bytes 417800 | tf_op jit(solution)/shard_map/ppermute | solution.py:246
  45.6 2.6 %collective-permute-start.9 = (f32[2,136,128]{2,1,0:T(8,128)S(1)}, f32[2,136,128]{2,1,0:T(8,128)S(1)}, u32[]{:S(2)}, u32[]{:S(2)}) collective-permute-start(f32[2,136,128]{2,1,0:T(8,128)S(1)} %shard_map.57.refs_0_), channel_id=1, source_target_pairs={{0,8},{1,9},{2,10},{3,11},{4,12},{5,13},{6,14},{7,15},{8,0},{9,1},... | collective-permute-start | bytes 417800 | tf_op jit(solution)/shard_map/ppermute | solution.py:246
  48.2 1.3 %collective-permute-start.10 = (f32[2,136,128]{2,1,0:T(8,128)S(1)}, f32[2,136,128]{2,1,0:T(8,128)S(1)}, u32[]{:S(2)}, u32[]{:S(2)}) collective-permute-start(f32[2,136,128]{2,1,0:T(8,128)S(1)} %shard_map.57.refs_0_), channel_id=1, source_target_pairs={{0,12},{1,13},{2,14},{3,15},{4,0},{5,1},{6,2},{7,3},{8,4},{9,5},{1... | collective-permute-start | bytes 417800 | tf_op jit(solution)/shard_map/ppermute | solution.py:246
  49.5 1.7 %collective-permute-done.8.refs_1_ = f32[2,136,128]{2,1,0:T(8,128)S(1)} collective-permute-done((f32[2,136,128]{2,1,0:T(8,128)S(1)}, f32[2,136,128]{2,1,0:T(8,128)S(1)}, u32[]{:S(2)}, u32[]{:S(2)}) %collective-permute-start.8) | collective-permute-done | bytes 139296 | tf_op jit(solution)/shard_map/ppermute | solution.py:246
  51.3 6.8 %collective-permute-done.9.refs_2_ = f32[2,136,128]{2,1,0:T(8,128)S(1)} collective-permute-done((f32[2,136,128]{2,1,0:T(8,128)S(1)}, f32[2,136,128]{2,1,0:T(8,128)S(1)}, u32[]{:S(2)}, u32[]{:S(2)}) %collective-permute-start.9) | collective-permute-done | bytes 139296 | tf_op jit(solution)/shard_map/ppermute | solution.py:246
  58.1 3.8 %shard_map.58 = f32[3,2,32,128]{3,2,1,0:T(8,128)} custom-call(s32[4]{0:T(128)S(1)} %pad_add_fusion.place, f32[2,136,128]{2,1,0:T(8,128)S(1)} %shard_map.57.refs_0_, f32[2,136,128]{2,1,0:T(8,128)S(1)} %collective-permute-done.8.refs_1_, f32[2,136,128]{2,1,0:T(8,128)S(1)} %collective-permute-done.9.refs_2_, f32[2,136,128]{2,1,0:T(8,128)S(1)} %collective-permute-done.10.refs_3_), custom_call_target="tpu_custom_call" | custom-call | flops 503316480 | bytes 1048576 | tf_op jit(solution)/shard_map/pallas_call | solution.py:100
  (15 shorter events, 0.1 us)
Async XLA Ops:
  0.0 28.8 %collective-permute-start = (bf16[1024,1024]{1,0:T(8,128)(2,1)}, bf16[1024,1024]{1,0:T(8,128)(2,1)S(1)}, u32[]{:S(2)}, u32[]{:S(2)}) collective-permute-start(bf16[1024,1024]{1,0:T(8,128)(2,1)} %bitcast.5), channel_id=1, source_target_pairs={{0,4},{5,1},{2,6},{7,3},{4,8},{9,5},{6,10},{11,7},{8,12},{13,9},{1... | collective-permute-start | bytes 6291464 | tf_op jit(solution)/shard_map/ppermute | solution.py:246
  5.2 1.6 %copy-start = (bf16[1,1024,1024]{2,1,0:T(8,128)(2,1)S(1)}, bf16[1,1024,1024]{2,1,0:T(8,128)(2,1)}, u32[]{:S(2)}) copy-start(bf16[1,1024,1024]{2,1,0:T(8,128)(2,1)} %param.5) | copy-start | bytes 6291460
  6.7 1.6 %copy-start.1 = (bf16[1024,1024]{1,0:T(8,128)(2,1)S(1)}, bf16[1024,1024]{1,0:T(8,128)(2,1)}, u32[]{:S(2)}) copy-start(bf16[1024,1024]{1,0:T(8,128)(2,1)} %after.1) | copy-start | bytes 6291460
  10.0 2.0 %collective-permute-start.6 = (f32[2,128,128]{2,1,0:T(8,128)S(1)}, f32[2,128,128]{2,1,0:T(8,128)S(1)}, u32[]{:S(2)}, u32[]{:S(2)}) collective-permute-start(f32[2,128,128]{2,1,0:T(8,128)S(1)} %get-tuple-element.20), channel_id=1, source_target_pairs={{12,15},{13,12},{14,13},{15,14},{28,31},{29,28},{30,29},{31,30}} | collective-permute-start | bytes 393224 | tf_op jit(solution)/shard_map/ppermute | solution.py:246
  10.6 1.4 %collective-permute-start.5 = (f32[2,128,128]{2,1,0:T(8,128)S(1)}, f32[2,128,128]{2,1,0:T(8,128)S(1)}, u32[]{:S(2)}, u32[]{:S(2)}) collective-permute-start(f32[2,128,128]{2,1,0:T(8,128)S(1)} %get-tuple-element.19), channel_id=1, source_target_pairs={{12,14},{13,15},{14,12},{15,13},{28,30},{29,31},{30,28},{31,29}} | collective-permute-start | bytes 393224 | tf_op jit(solution)/shard_map/ppermute | solution.py:246
  11.3 0.7 %collective-permute-start.4 = (f32[2,128,128]{2,1,0:T(8,128)S(1)}, f32[2,128,128]{2,1,0:T(8,128)S(1)}, u32[]{:S(2)}, u32[]{:S(2)}) collective-permute-start(f32[2,128,128]{2,1,0:T(8,128)S(1)} %get-tuple-element.18), channel_id=1, source_target_pairs={{12,13},{13,14},{14,15},{15,12},{28,29},{29,30},{30,31},{31,28}} | collective-permute-start | bytes 393224 | tf_op jit(solution)/shard_map/ppermute | solution.py:246
  12.1 20.4 %copy-start.4 = (s32[1,8,2]{1,2,0:T(2,128)S(1)}, s32[1,8,2]{1,2,0:T(2,128)}, u32[]{:S(2)}) copy-start(s32[1,8,2]{1,2,0:T(2,128)} %param.7) | copy-start | bytes 196
  12.1 20.5 %copy-start.2 = (f32[1,1024]{1,0:T(1,128)S(1)}, f32[1,1024]{1,0:T(1,128)}, u32[]{:S(2)}) copy-start(f32[1,1024]{1,0:T(1,128)} %decays.1) | copy-start | bytes 12292
  12.1 20.5 %copy-start.3 = (f32[1,1024]{1,0:T(1,128)S(1)}, f32[1,1024]{1,0:T(1,128)}, u32[]{:S(2)}) copy-start(f32[1,1024]{1,0:T(1,128)} %mirrors.1) | copy-start | bytes 12292
  12.1 20.4 %collective-permute-start.7 = (f32[2,128,128]{2,1,0:T(8,128)S(1)}, f32[2,128,128]{2,1,0:T(8,128)S(1)}, u32[]{:S(2)}, u32[]{:S(2)}) collective-permute-start(f32[2,128,128]{2,1,0:T(8,128)S(1)} %add_add_fusion.refs_4_), channel_id=1, source_target_pairs={{12,0},{14,2},{28,16},{30,18}} | collective-permute-start | bytes 393224 | tf_op jit(solution)/shard_map/ppermute | solution.py:246
  30.4 2.1 %collective-permute-start.1 = (f32[2,128,128]{2,1,0:T(8,128)S(1)}, f32[2,128,128]{2,1,0:T(8,128)S(1)}, u32[]{:S(2)}, u32[]{:S(2)}) collective-permute-start(f32[2,128,128]{2,1,0:T(8,128)S(1)} %get-tuple-element.14), channel_id=1, source_target_pairs={{4,1},{1,6},{6,3},{3,4},{8,5},{5,10},{10,7},{7,8},{12,9},{9,14},{1... | collective-permute-start | bytes 393224 | tf_op jit(solution)/shard_map/ppermute | solution.py:246
  31.1 1.5 %collective-permute-start.2 = (f32[2,128,128]{2,1,0:T(8,128)S(1)}, f32[2,128,128]{2,1,0:T(8,128)S(1)}, u32[]{:S(2)}, u32[]{:S(2)}) collective-permute-start(f32[2,128,128]{2,1,0:T(8,128)S(1)} %get-tuple-element.15), channel_id=1, source_target_pairs={{4,6},{1,3},{6,4},{3,1},{8,10},{5,7},{10,8},{7,5},{12,14},{9,11},{... | collective-permute-start | bytes 393224 | tf_op jit(solution)/shard_map/ppermute | solution.py:246
  31.8 0.8 %collective-permute-start.3 = (f32[2,128,128]{2,1,0:T(8,128)S(1)}, f32[2,128,128]{2,1,0:T(8,128)S(1)}, u32[]{:S(2)}, u32[]{:S(2)}) collective-permute-start(f32[2,128,128]{2,1,0:T(8,128)S(1)} %get-tuple-element.16), channel_id=1, source_target_pairs={{4,3},{1,4},{6,1},{3,6},{8,7},{5,8},{10,5},{7,10},{12,11},{9,12},{... | collective-permute-start | bytes 393224 | tf_op jit(solution)/shard_map/ppermute | solution.py:246
  33.2 18.0 %collective-permute-start.8 = (f32[2,136,128]{2,1,0:T(8,128)S(1)}, f32[2,136,128]{2,1,0:T(8,128)S(1)}, u32[]{:S(2)}, u32[]{:S(2)}) collective-permute-start(f32[2,136,128]{2,1,0:T(8,128)S(1)} %shard_map.57.refs_0_), channel_id=1, source_target_pairs={{0,4},{1,5},{2,6},{3,7},{4,8},{5,9},{6,10},{7,11},{8,12},{9,13},{1... | collective-permute-start | bytes 417800 | tf_op jit(solution)/shard_map/ppermute | solution.py:246
  45.6 12.5 %collective-permute-start.9 = (f32[2,136,128]{2,1,0:T(8,128)S(1)}, f32[2,136,128]{2,1,0:T(8,128)S(1)}, u32[]{:S(2)}, u32[]{:S(2)}) collective-permute-start(f32[2,136,128]{2,1,0:T(8,128)S(1)} %shard_map.57.refs_0_), channel_id=1, source_target_pairs={{0,8},{1,9},{2,10},{3,11},{4,12},{5,13},{6,14},{7,15},{8,0},{9,1},... | collective-permute-start | bytes 417800 | tf_op jit(solution)/shard_map/ppermute | solution.py:246
  48.2 9.9 %collective-permute-start.10 = (f32[2,136,128]{2,1,0:T(8,128)S(1)}, f32[2,136,128]{2,1,0:T(8,128)S(1)}, u32[]{:S(2)}, u32[]{:S(2)}) collective-permute-start(f32[2,136,128]{2,1,0:T(8,128)S(1)} %shard_map.57.refs_0_), channel_id=1, source_target_pairs={{0,12},{1,13},{2,14},{3,15},{4,0},{5,1},{6,2},{7,3},{8,4},{9,5},{1... | collective-permute-start | bytes 417800 | tf_op jit(solution)/shard_map/ppermute | solution.py:246

commit v4 on v3

--- a/solution.py
+++ b/solution.py
@@ -23,7 +23,10 @@
     def dot(a, b):
         return lax.dot_general(a, b, dims, preferred_element_type=jnp.float32)
 
-    return dot(left[0], right[0]) + (dot(left[0], right[1]) + dot(left[1], right[0]))
+    both = jnp.concatenate([left[0], left[1]], axis=1)
+    axis = 1 if flip else 0
+    twice = jnp.concatenate([right[0], right[0]], axis=axis)
+    return dot(both, twice) + dot(left[0], right[1])
 
 
 def star_body(place, *refs, orders, rows):
@@ -49,7 +52,7 @@
     def part_diag(vector):
         return jnp.where(part_row == part_col, vector, 0.0)
 
-    for order in range(orders):
+    def steps(order):
         trans, front, back = [], [], []
         for sec in range(BLOCK):
             decay = abuf[sec, order, 0:1, :]
@@ -61,36 +64,62 @@
             trans.append(passing * (tbuf[sec, order] * mask) * decay)
             front.append(decay * decay * mirror)
             back.append(-mirror)
+        yield
         bounce_a = back[0] * front[1]
         bounce_b = back[2] * front[3]
         gain_a = (1.0 + bounce_a * bounce_a) * (1.0 + bounce_a)
         gain_b = (1.0 + bounce_b * bounce_b) * (1.0 + bounce_b)
         flip_0 = trans[0].T
         flip_2 = trans[2].T
-        rbuf[0] = flip_0
-        rbuf[1] = trans[3]
-        flip_0_part = rbuf[0, picked, :]
-        trans_3_part = rbuf[1, picked, :]
+        rbuf[2 * order] = flip_0
+        rbuf[2 * order + 1] = trans[3]
+        flip_0_part = rbuf[2 * order, picked, :]
+        trans_3_part = rbuf[2 * order + 1, picked, :]
+        yield
         s0, s1, s2, s3 = [halves(t) for t in trans]
+        yield
         trans_a = halves(mul(halves(trans[1] * gain_a), s0))
+        yield
         back_a = halves(diag(back[1]) + mul(halves(trans[1] * (back[0] * gain_a)), s1, True))
+        yield
         front_b = halves(diag(front[2]) + mul(halves(flip_2 * (front[3] * gain_b)), s2))
+        yield
         trans_b = halves(mul(halves(trans[3] * gain_b), s2))
+        yield
         flip_a_part = halves(mul(halves(flip_0_part * gain_a), s1, True))
+        yield
         trans_b_part = mul(halves(trans_3_part * gain_b), s2)
+        yield
         front_a_part = part_diag(front[0]) + mul(halves(flip_0_part * (front[1] * gain_a)), s0)
+        yield
         back_b_part = part_diag(back[3]) + mul(halves(trans_3_part * (back[2] * gain_b)), s3, True)
+        yield
         bounce = halves(mul(back_a, front_b))
+        yield
         ahead = jnp.concatenate([trans_b_part, mul(flip_a_part, front_b)], axis=0)
+        yield
         behind = mul(halves(trans_b_part), back_a)
-        ahead = ahead + mul(halves(mul(halves(ahead), bounce)), bounce)
-        behind = behind + mul(halves(mul(halves(behind), bounce, True)), bounce, True)
+        yield
+        square = halves(mul(bounce, bounce))
+        yield
         ahead = ahead + mul(halves(ahead), bounce)
+        yield
         behind = behind + mul(halves(behind), bounce, True)
+        yield
+        ahead = ahead + mul(halves(ahead), square)
+        yield
+        behind = behind + mul(halves(behind), square, True)
+        yield
         ahead = mul(halves(ahead), trans_a)
         out[0, order] = ahead[:rows]
         out[1, order] = front_a_part + ahead[rows:]
+        yield
         out[2, order] = back_b_part + mul(halves(behind), trans_b, True)
+        yield
+
+    running = [steps(order) for order in range(orders)]
+    while running:
+        running = [one for one in running if next(one, 0) is None]
 
 
 def star_of_four(place, terms, rows):
@@ -105,7 +134,7 @@
         scratch_shapes=[
             pltpu.VMEM((BLOCK, orders, width, width), jnp.float32),
             pltpu.VMEM((BLOCK, orders, extra, width), jnp.float32),
-            pltpu.VMEM((2, width, width), jnp.float32),
+            pltpu.VMEM((2 * orders, width, width), jnp.float32),
         ],
         compiler_params=ROOM,
         cost_estimate=pl.CostEstimate(

time: 63 us -> 61.7 us (0.979)
  Pallas kernels: 7.67 us -> 6.38 us
    pallas_call x1, Pallas kernels: 3.78 us -> 2.49 us  [star_of_four(): pl.pallas_call(functools.partial(star_body, orders=orders, rows=rows), ou...]
where the time goes in v4:
time: 61.7 us; the launch traced here: 60.6 us
  starting transfers between devices  26.8 us (43%)
  waiting for transfers between devices  23.8 us (39%)
  Pallas kernels  6.38 us (10%)
  local copies, waits for them, and re-layouts  3.28 us (5%)
    ppermute x11, starting transfers between devices, send(): lax.ppermute(value, AXES, [(s * count + g, t * count + h) for (s, g), (t,...  26.8 us
    ppermute x11, waiting for transfers between devices, send(): lax.ppermute(value, AXES, [(s * count + g, t * count + h) for (s, g), (t,...  23.8 us
    unnamed x11, local copies, waits for them, and re-layouts  3.28 us
    pallas_call x1, Pallas kernels, star_of_four(): pl.pallas_call(functools.partial(star_body, orders=orders, rows=rows), ou...  2.49 us
    pallas_call x1, Pallas kernels, inner_sums(): pl.pallas_call(inner_body, out_shape=[jax.ShapeDtypeStruct((share, width,...  1.63 us
    pallas_call x1, Pallas kernels, exit_sums(): pl.pallas_call(exit_body, out_shape=[jax.ShapeDtypeStruct((share, width,...  1.62 us
  transfers between devices with their start and end apart: 11, of which 3 were waited for; matrix products, arithmetic and copies ran while one was open for 0% of the time, Pallas kernels for 5%

profile of v4, /device:TPU:0, one launch (start us, length us, event | category | flops | bytes accessed | tf_op | source)
XLA Modules:
  0.0 60.6 jit_solution(8834622477287551620)
XLA Ops:
  0.0 5.1 %collective-permute-start = (bf16[1024,1024]{1,0:T(8,128)(2,1)}, bf16[1024,1024]{1,0:T(8,128)(2,1)S(1)}, u32[]{:S(2)}, u32[]{:S(2)}) collective-permute-start(bf16[1024,1024]{1,0:T(8,128)(2,1)} %bitcast.5), channel_id=1, source_target_pairs={{0,4},{5,1},{2,6},{7,3},{4,8},{9,5},{6,10},{11,7},{8,12},{13,9},{1... | collective-permute-start | bytes 6291464 | tf_op jit(solution)/shard_map/ppermute | solution.py:275
  5.1 0.1 pad_add_fusion.place
  5.2 1.6 %copy-done = bf16[1,1024,1024]{2,1,0:T(8,128)(2,1)S(1)} copy-done((bf16[1,1024,1024]{2,1,0:T(8,128)(2,1)S(1)}, bf16[1,1024,1024]{2,1,0:T(8,128)(2,1)}, u32[]{:S(2)}) %copy-start) | copy-done | bytes 2097176
  6.8 1.6 %copy-done.1 = bf16[1024,1024]{1,0:T(8,128)(2,1)S(1)} copy-done((bf16[1024,1024]{1,0:T(8,128)(2,1)S(1)}, bf16[1024,1024]{1,0:T(8,128)(2,1)}, u32[]{:S(2)}) %copy-start.1) | copy-done | bytes 2097176
  8.3 1.6 %shard_map.56 = (f32[2,128,128]{2,1,0:T(8,128)S(1)}, f32[2,128,128]{2,1,0:T(8,128)S(1)}, f32[2,128,128]{2,1,0:T(8,128)S(1)}, f32[2,128,128]{2,1,0:T(8,128)S(1)}) custom-call(s32[4]{0:T(128)S(1)} %pad_add_fusion.place, bf16[1024,1024]{1,0:T(8,128)(2,1)S(1)} %bitcast.6, bf16[1024,1024]{1,0:T(8,128)(2,1)S(1)} %copy-done.1), custom_call_target="tpu_custom_call" | custom-call | flops 268435456 | bytes 4194304 | tf_op jit(solution)/shard_map/pallas_call | solution.py:205
  10.0 0.7 %collective-permute-start.6 = (f32[2,128,128]{2,1,0:T(8,128)S(1)}, f32[2,128,128]{2,1,0:T(8,128)S(1)}, u32[]{:S(2)}, u32[]{:S(2)}) collective-permute-start(f32[2,128,128]{2,1,0:T(8,128)S(1)} %get-tuple-element.20), channel_id=1, source_target_pairs={{12,15},{13,12},{14,13},{15,14},{28,31},{29,28},{30,29},{31,30}} | collective-permute-start | bytes 393224 | tf_op jit(solution)/shard_map/ppermute | solution.py:275
  10.6 0.7 %collective-permute-start.5 = (f32[2,128,128]{2,1,0:T(8,128)S(1)}, f32[2,128,128]{2,1,0:T(8,128)S(1)}, u32[]{:S(2)}, u32[]{:S(2)}) collective-permute-start(f32[2,128,128]{2,1,0:T(8,128)S(1)} %get-tuple-element.19), channel_id=1, source_target_pairs={{12,14},{13,15},{14,12},{15,13},{28,30},{29,31},{30,28},{31,29}} | collective-permute-start | bytes 393224 | tf_op jit(solution)/shard_map/ppermute | solution.py:275
  11.3 0.7 %collective-permute-start.4 = (f32[2,128,128]{2,1,0:T(8,128)S(1)}, f32[2,128,128]{2,1,0:T(8,128)S(1)}, u32[]{:S(2)}, u32[]{:S(2)}) collective-permute-start(f32[2,128,128]{2,1,0:T(8,128)S(1)} %get-tuple-element.18), channel_id=1, source_target_pairs={{12,13},{13,14},{14,15},{15,12},{28,29},{29,30},{30,31},{31,28}} | collective-permute-start | bytes 393224 | tf_op jit(solution)/shard_map/ppermute | solution.py:275
  12.1 0.0 copy-start.4
  12.1 0.0 copy-start.3
  12.1 1.4 %collective-permute-start.7 = (f32[2,128,128]{2,1,0:T(8,128)S(1)}, f32[2,128,128]{2,1,0:T(8,128)S(1)}, u32[]{:S(2)}, u32[]{:S(2)}) collective-permute-start(f32[2,128,128]{2,1,0:T(8,128)S(1)} %add_add_fusion.refs_4_), channel_id=1, source_target_pairs={{12,0},{14,2},{28,16},{30,18}} | collective-permute-start | bytes 393224 | tf_op jit(solution)/shard_map/ppermute | solution.py:275
  13.5 15.2 %collective-permute-done.arrived = bf16[1024,1024]{1,0:T(8,128)(2,1)S(1)} collective-permute-done((bf16[1024,1024]{1,0:T(8,128)(2,1)}, bf16[1024,1024]{1,0:T(8,128)(2,1)S(1)}, u32[]{:S(2)}, u32[]{:S(2)}) %collective-permute-start) | collective-permute-done | bytes 2097184 | tf_op jit(solution)/shard_map/ppermute | solution.py:275
  28.8 1.6 %shard_map.55 = (f32[2,128,128]{2,1,0:T(8,128)S(1)}, f32[2,128,128]{2,1,0:T(8,128)S(1)}, f32[2,128,128]{2,1,0:T(8,128)S(1)}, f32[2,128,128]{2,1,0:T(8,128)S(1)}) custom-call(s32[4]{0:T(128)S(1)} %pad_add_fusion.place, bf16[1024,1024]{1,0:T(8,128)(2,1)S(1)} %bitcast.7, bf16[1024,1024]{1,0:T(8,128)(2,1)S(1)} %collective-permute-done.arrived), custom_call_target="tpu_custom_call" | custom-call | flops 268435456 | bytes 4194304 | tf_op jit(solution)/shard_map/pallas_call | solution.py:243
  30.4 0.7 %collective-permute-start.1 = (f32[2,128,128]{2,1,0:T(8,128)S(1)}, f32[2,128,128]{2,1,0:T(8,128)S(1)}, u32[]{:S(2)}, u32[]{:S(2)}) collective-permute-start(f32[2,128,128]{2,1,0:T(8,128)S(1)} %get-tuple-element.14), channel_id=1, source_target_pairs={{4,1},{1,6},{6,3},{3,4},{8,5},{5,10},{10,7},{7,8},{12,9},{9,14},{1... | collective-permute-start | bytes 393224 | tf_op jit(solution)/shard_map/ppermute | solution.py:275
  31.1 0.7 %collective-permute-start.2 = (f32[2,128,128]{2,1,0:T(8,128)S(1)}, f32[2,128,128]{2,1,0:T(8,128)S(1)}, u32[]{:S(2)}, u32[]{:S(2)}) collective-permute-start(f32[2,128,128]{2,1,0:T(8,128)S(1)} %get-tuple-element.15), channel_id=1, source_target_pairs={{4,6},{1,3},{6,4},{3,1},{8,10},{5,7},{10,8},{7,5},{12,14},{9,11},{... | collective-permute-start | bytes 393224 | tf_op jit(solution)/shard_map/ppermute | solution.py:275
  31.8 0.7 %collective-permute-start.3 = (f32[2,128,128]{2,1,0:T(8,128)S(1)}, f32[2,128,128]{2,1,0:T(8,128)S(1)}, u32[]{:S(2)}, u32[]{:S(2)}) collective-permute-start(f32[2,128,128]{2,1,0:T(8,128)S(1)} %get-tuple-element.16), channel_id=1, source_target_pairs={{4,3},{1,4},{6,1},{3,6},{8,7},{5,8},{10,5},{7,10},{12,11},{9,12},{... | collective-permute-start | bytes 393224 | tf_op jit(solution)/shard_map/ppermute | solution.py:275
  32.5 0.1 copy.6.pattern
  32.6 0.6 %shard_map.57.refs_0_ = f32[2,136,128]{2,1,0:T(8,128)S(1)} custom-call(s32[4]{0:T(128)S(1)} %pad_add_fusion.place, s32[1,8,2]{2,1,0:T(8,128)S(1)} %copy.6.pattern, f32[1,1024]{1,0:T(1,128)S(1)} %copy-done.2, f32[1,1024]{1,0:T(1,128)S(1)} %copy-done.3, f32[2,128,128]{2,1,0:T(8,128)S(1)} %get-tuple-element.13.refs_0_, ...), custom_call_target="tpu_custom_call" | custom-call | flops 131072 | bytes 917504 | tf_op jit(solution)/shard_map/pallas_call | solution.py:169
  33.2 12.4 %collective-permute-start.8 = (f32[2,136,128]{2,1,0:T(8,128)S(1)}, f32[2,136,128]{2,1,0:T(8,128)S(1)}, u32[]{:S(2)}, u32[]{:S(2)}) collective-permute-start(f32[2,136,128]{2,1,0:T(8,128)S(1)} %shard_map.57.refs_0_), channel_id=1, source_target_pairs={{0,4},{1,5},{2,6},{3,7},{4,8},{5,9},{6,10},{7,11},{8,12},{9,13},{1... | collective-permute-start | bytes 417800 | tf_op jit(solution)/shard_map/ppermute | solution.py:275
  45.6 2.6 %collective-permute-start.9 = (f32[2,136,128]{2,1,0:T(8,128)S(1)}, f32[2,136,128]{2,1,0:T(8,128)S(1)}, u32[]{:S(2)}, u32[]{:S(2)}) collective-permute-start(f32[2,136,128]{2,1,0:T(8,128)S(1)} %shard_map.57.refs_0_), channel_id=1, source_target_pairs={{0,8},{1,9},{2,10},{3,11},{4,12},{5,13},{6,14},{7,15},{8,0},{9,1},... | collective-permute-start | bytes 417800 | tf_op jit(solution)/shard_map/ppermute | solution.py:275
  48.2 1.3 %collective-permute-start.10 = (f32[2,136,128]{2,1,0:T(8,128)S(1)}, f32[2,136,128]{2,1,0:T(8,128)S(1)}, u32[]{:S(2)}, u32[]{:S(2)}) collective-permute-start(f32[2,136,128]{2,1,0:T(8,128)S(1)} %shard_map.57.refs_0_), channel_id=1, source_target_pairs={{0,12},{1,13},{2,14},{3,15},{4,0},{5,1},{6,2},{7,3},{8,4},{9,5},{1... | collective-permute-start | bytes 417800 | tf_op jit(solution)/shard_map/ppermute | solution.py:275
  49.5 1.7 %collective-permute-done.8.refs_1_ = f32[2,136,128]{2,1,0:T(8,128)S(1)} collective-permute-done((f32[2,136,128]{2,1,0:T(8,128)S(1)}, f32[2,136,128]{2,1,0:T(8,128)S(1)}, u32[]{:S(2)}, u32[]{:S(2)}) %collective-permute-start.8) | collective-permute-done | bytes 139296 | tf_op jit(solution)/shard_map/ppermute | solution.py:275
  51.3 6.8 %collective-permute-done.9.refs_2_ = f32[2,136,128]{2,1,0:T(8,128)S(1)} collective-permute-done((f32[2,136,128]{2,1,0:T(8,128)S(1)}, f32[2,136,128]{2,1,0:T(8,128)S(1)}, u32[]{:S(2)}, u32[]{:S(2)}) %collective-permute-start.9) | collective-permute-done | bytes 139296 | tf_op jit(solution)/shard_map/ppermute | solution.py:275
  58.1 2.5 %shard_map.58 = f32[3,2,32,128]{3,2,1,0:T(8,128)} custom-call(s32[4]{0:T(128)S(1)} %pad_add_fusion.place, f32[2,136,128]{2,1,0:T(8,128)S(1)} %shard_map.57.refs_0_, f32[2,136,128]{2,1,0:T(8,128)S(1)} %collective-permute-done.8.refs_1_, f32[2,136,128]{2,1,0:T(8,128)S(1)} %collective-permute-done.9.refs_2_, f32[2,136,128]{2,1,0:T(8,128)S(1)} %collective-permute-done.10.refs_3_), custom_call_target="tpu_custom_call" | custom-call | flops 503316480 | bytes 1048576 | tf_op jit(solution)/shard_map/pallas_call | solution.py:129
  (15 shorter events, 0.1 us)
Async XLA Ops:
  0.0 28.8 %collective-permute-start = (bf16[1024,1024]{1,0:T(8,128)(2,1)}, bf16[1024,1024]{1,0:T(8,128)(2,1)S(1)}, u32[]{:S(2)}, u32[]{:S(2)}) collective-permute-start(bf16[1024,1024]{1,0:T(8,128)(2,1)} %bitcast.5), channel_id=1, source_target_pairs={{0,4},{5,1},{2,6},{7,3},{4,8},{9,5},{6,10},{11,7},{8,12},{13,9},{1... | collective-permute-start | bytes 6291464 | tf_op jit(solution)/shard_map/ppermute | solution.py:275
  5.2 1.6 %copy-start = (bf16[1,1024,1024]{2,1,0:T(8,128)(2,1)S(1)}, bf16[1,1024,1024]{2,1,0:T(8,128)(2,1)}, u32[]{:S(2)}) copy-start(bf16[1,1024,1024]{2,1,0:T(8,128)(2,1)} %param.5) | copy-start | bytes 6291460
  6.7 1.6 %copy-start.1 = (bf16[1024,1024]{1,0:T(8,128)(2,1)S(1)}, bf16[1024,1024]{1,0:T(8,128)(2,1)}, u32[]{:S(2)}) copy-start(bf16[1024,1024]{1,0:T(8,128)(2,1)} %after.1) | copy-start | bytes 6291460
  10.0 2.0 %collective-permute-start.6 = (f32[2,128,128]{2,1,0:T(8,128)S(1)}, f32[2,128,128]{2,1,0:T(8,128)S(1)}, u32[]{:S(2)}, u32[]{:S(2)}) collective-permute-start(f32[2,128,128]{2,1,0:T(8,128)S(1)} %get-tuple-element.20), channel_id=1, source_target_pairs={{12,15},{13,12},{14,13},{15,14},{28,31},{29,28},{30,29},{31,30}} | collective-permute-start | bytes 393224 | tf_op jit(solution)/shard_map/ppermute | solution.py:275
  10.6 1.4 %collective-permute-start.5 = (f32[2,128,128]{2,1,0:T(8,128)S(1)}, f32[2,128,128]{2,1,0:T(8,128)S(1)}, u32[]{:S(2)}, u32[]{:S(2)}) collective-permute-start(f32[2,128,128]{2,1,0:T(8,128)S(1)} %get-tuple-element.19), channel_id=1, source_target_pairs={{12,14},{13,15},{14,12},{15,13},{28,30},{29,31},{30,28},{31,29}} | collective-permute-start | bytes 393224 | tf_op jit(solution)/shard_map/ppermute | solution.py:275
  11.3 0.7 %collective-permute-start.4 = (f32[2,128,128]{2,1,0:T(8,128)S(1)}, f32[2,128,128]{2,1,0:T(8,128)S(1)}, u32[]{:S(2)}, u32[]{:S(2)}) collective-permute-start(f32[2,128,128]{2,1,0:T(8,128)S(1)} %get-tuple-element.18), channel_id=1, source_target_pairs={{12,13},{13,14},{14,15},{15,12},{28,29},{29,30},{30,31},{31,28}} | collective-permute-start | bytes 393224 | tf_op jit(solution)/shard_map/ppermute | solution.py:275
  12.1 20.4 %copy-start.4 = (s32[1,8,2]{1,2,0:T(2,128)S(1)}, s32[1,8,2]{1,2,0:T(2,128)}, u32[]{:S(2)}) copy-start(s32[1,8,2]{1,2,0:T(2,128)} %param.7) | copy-start | bytes 196
  12.1 20.5 %copy-start.2 = (f32[1,1024]{1,0:T(1,128)S(1)}, f32[1,1024]{1,0:T(1,128)}, u32[]{:S(2)}) copy-start(f32[1,1024]{1,0:T(1,128)} %decays.1) | copy-start | bytes 12292
  12.1 20.5 %copy-start.3 = (f32[1,1024]{1,0:T(1,128)S(1)}, f32[1,1024]{1,0:T(1,128)}, u32[]{:S(2)}) copy-start(f32[1,1024]{1,0:T(1,128)} %mirrors.1) | copy-start | bytes 12292
  12.1 20.4 %collective-permute-start.7 = (f32[2,128,128]{2,1,0:T(8,128)S(1)}, f32[2,128,128]{2,1,0:T(8,128)S(1)}, u32[]{:S(2)}, u32[]{:S(2)}) collective-permute-start(f32[2,128,128]{2,1,0:T(8,128)S(1)} %add_add_fusion.refs_4_), channel_id=1, source_target_pairs={{12,0},{14,2},{28,16},{30,18}} | collective-permute-start | bytes 393224 | tf_op jit(solution)/shard_map/ppermute | solution.py:275
  30.4 2.1 %collective-permute-start.1 = (f32[2,128,128]{2,1,0:T(8,128)S(1)}, f32[2,128,128]{2,1,0:T(8,128)S(1)}, u32[]{:S(2)}, u32[]{:S(2)}) collective-permute-start(f32[2,128,128]{2,1,0:T(8,128)S(1)} %get-tuple-element.14), channel_id=1, source_target_pairs={{4,1},{1,6},{6,3},{3,4},{8,5},{5,10},{10,7},{7,8},{12,9},{9,14},{1... | collective-permute-start | bytes 393224 | tf_op jit(solution)/shard_map/ppermute | solution.py:275
  31.1 1.5 %collective-permute-start.2 = (f32[2,128,128]{2,1,0:T(8,128)S(1)}, f32[2,128,128]{2,1,0:T(8,128)S(1)}, u32[]{:S(2)}, u32[]{:S(2)}) collective-permute-start(f32[2,128,128]{2,1,0:T(8,128)S(1)} %get-tuple-element.15), channel_id=1, source_target_pairs={{4,6},{1,3},{6,4},{3,1},{8,10},{5,7},{10,8},{7,5},{12,14},{9,11},{... | collective-permute-start | bytes 393224 | tf_op jit(solution)/shard_map/ppermute | solution.py:275
  31.8 0.8 %collective-permute-start.3 = (f32[2,128,128]{2,1,0:T(8,128)S(1)}, f32[2,128,128]{2,1,0:T(8,128)S(1)}, u32[]{:S(2)}, u32[]{:S(2)}) collective-permute-start(f32[2,128,128]{2,1,0:T(8,128)S(1)} %get-tuple-element.16), channel_id=1, source_target_pairs={{4,3},{1,4},{6,1},{3,6},{8,7},{5,8},{10,5},{7,10},{12,11},{9,12},{... | collective-permute-start | bytes 393224 | tf_op jit(solution)/shard_map/ppermute | solution.py:275
  33.2 18.0 %collective-permute-start.8 = (f32[2,136,128]{2,1,0:T(8,128)S(1)}, f32[2,136,128]{2,1,0:T(8,128)S(1)}, u32[]{:S(2)}, u32[]{:S(2)}) collective-permute-start(f32[2,136,128]{2,1,0:T(8,128)S(1)} %shard_map.57.refs_0_), channel_id=1, source_target_pairs={{0,4},{1,5},{2,6},{3,7},{4,8},{5,9},{6,10},{7,11},{8,12},{9,13},{1... | collective-permute-start | bytes 417800 | tf_op jit(solution)/shard_map/ppermute | solution.py:275
  45.6 12.5 %collective-permute-start.9 = (f32[2,136,128]{2,1,0:T(8,128)S(1)}, f32[2,136,128]{2,1,0:T(8,128)S(1)}, u32[]{:S(2)}, u32[]{:S(2)}) collective-permute-start(f32[2,136,128]{2,1,0:T(8,128)S(1)} %shard_map.57.refs_0_), channel_id=1, source_target_pairs={{0,8},{1,9},{2,10},{3,11},{4,12},{5,13},{6,14},{7,15},{8,0},{9,1},... | collective-permute-start | bytes 417800 | tf_op jit(solution)/shard_map/ppermute | solution.py:275
  48.2 9.9 %collective-permute-start.10 = (f32[2,136,128]{2,1,0:T(8,128)S(1)}, f32[2,136,128]{2,1,0:T(8,128)S(1)}, u32[]{:S(2)}, u32[]{:S(2)}) collective-permute-start(f32[2,136,128]{2,1,0:T(8,128)S(1)} %shard_map.57.refs_0_), channel_id=1, source_target_pairs={{0,12},{1,13},{2,14},{3,15},{4,0},{5,1},{6,2},{7,3},{8,4},{9,5},{1... | collective-permute-start | bytes 417800 | tf_op jit(solution)/shard_map/ppermute | solution.py:275

commit v5 on v4

--- a/solution.py
+++ b/solution.py
@@ -215,42 +215,69 @@
     )(place, fields, exit_modes)
 
 
-def inner_body(place, fields, arrived, *refs):
-    outs, terms = refs[:-1], refs[-1]
-    count, share, width = terms.shape[:3]
+def pack_body(place, fields, mine, sibling, *, pairs):
+    parity = lax.rem(place[0], 2)
+    size = mine.shape[1] // pairs
+    for pair in range(pairs):
+        target = pl.ds(pair * size, size)
+        mine[:, target] = fields[:, pl.ds(pl.multiple_of((2 * pair + parity) * size, 128), size)]
+        sibling[:, target] = fields[:, pl.ds(pl.multiple_of((2 * pair + 1 - parity) * size, 128), size)]
+
+
+def packed(place, fields, pairs):
+    points, modes = fields.shape
+    vmem = pl.BlockSpec(memory_space=pltpu.VMEM)
+    return pl.pallas_call(
+        functools.partial(pack_body, pairs=pairs),
+        out_shape=[jax.ShapeDtypeStruct((points, modes // 2), fields.dtype)] * 2,
+        in_specs=[pl.BlockSpec(memory_space=pltpu.SMEM), vmem],
+        out_specs=[vmem] * 2,
+        compiler_params=ROOM,
+        cost_estimate=pl.CostEstimate(flops=0, bytes_accessed=4 * points * modes, transcendentals=0),
+    )(place, fields)
+
+
+def inner_body(place, *refs, pairs):
+    own, arrived, outs, terms = refs[:2], refs[2:4], refs[4:-1], refs[-1]
+    share, width = terms.shape[1], terms.shape[-1]
 
     def fill(left, right):
-        for order in range(count * share):
+        for order in range(pairs * share):
             columns = pl.ds(order * width, width)
-            terms[order // share, order % share] = tall_dot(left[:, columns], right[:, columns])
+            terms[order // share, order % share] = tall_dot(left[0][:, columns], right[0][:, columns]) + tall_dot(
+                left[1][:, columns], right[1][:, columns]
+            )
 
     even = lax.rem(place[0], 2) == 0
 
     @pl.when(even)
     def _():
-        fill(arrived, fields)
+        fill(arrived, own)
 
     @pl.when(jnp.logical_not(even))
     def _():
-        fill(fields, arrived)
-
-    hand_out(place, terms, outs)
-
-
-def inner_sums(place, fields, arrived, count, share, width):
-    points, modes = fields.shape
+        fill(own, arrived)
+
+    for turn, out in enumerate(outs):
+        out[...] = terms[lax.rem(lax.div(place[0], 2) + turn, pairs)]
+
+
+def inner_sums(place, own, arrived, pairs, share, width):
+    points = own[0].shape[0]
     whole = pl.BlockSpec(memory_space=pltpu.VMEM)
     return pl.pallas_call(
-        inner_body,
-        out_shape=[jax.ShapeDtypeStruct((share, width, width), jnp.float32)] * count,
-        in_specs=[pl.BlockSpec(memory_space=pltpu.SMEM), whole, whole],
-        out_specs=[whole] * count,
-        scratch_shapes=[pltpu.VMEM((count, share, width, width), jnp.float32)],
+        functools.partial(inner_body, pairs=pairs),
+        out_shape=[jax.ShapeDtypeStruct((share, width, width), jnp.float32)] * pairs,
+        in_specs=[pl.BlockSpec(memory_space=pltpu.SMEM)] + [whole] * 4,
+        out_specs=[whole] * pairs,
+        scratch_shapes=[pltpu.VMEM((pairs, share, width, width), jnp.float32)],
         compiler_params=ROOM,
         cost_estimate=pl.CostEstimate(
-            flops=2 * points * modes * width, bytes_accessed=4 * points * modes, transcendentals=0
+            flops=4 * points * pairs * share * width**2,
+            bytes_accessed=8 * points * pairs * share * width,
+            transcendentals=0,
         ),
-    )(place, fields, arrived)
+    )(place, *own, *arrived)
 
 
 def body(modes, exit_modes, pattern, attenuation, reflection):
@@ -280,15 +307,21 @@
             got.append(send(parts[turn], [(row[g], row[(g + turn) % count]) for row in members for g in range(count)]))
         return got
 
+    pairs = count // 2
+    mine, sibling = packed(place, fields, pairs)
     steps = [((s + g % 2, g), (s + 1 - g % 2, g)) for s in range(final) for g in range(count)]
-    arrived = send(fields, steps)
+    beside = send(sibling, [((s, g), (s, g ^ 1)) for s in range(sections) for g in range(count)])
+    own_fields = (mine, beside)
+    arrived = (send(mine, steps), send(beside, steps))
 
     exit_parts = exit_sums(place, fields, exit_modes, count, share, width)
     exits = sum(gathered(exit_parts, [[(final, g) for g in range(count)]]))
     hop = send(exits, [((final, g), (0, g)) for g in range(0, count, 2)]) if small else exits
 
-    parts = inner_sums(place, fields, arrived, count, share, width)
-    parts = gathered(parts, [[(s + 1 - g % 2, g) for g in range(count)] for s in range(final)])
+    parts = list(inner_sums(place, own_fields, arrived, pairs, share, width))
+    for turn in range(1, pairs):
+        ring = [((s, g), (s, (g + 2 * turn) % count)) for s in range(sections) for g in range(count)]
+        parts[turn] = send(parts[turn], ring)
     if not small:
         own = sum(parts)
         back = send(own, [((s + 1, g), (s, g)) for s in range(final) for g in range(0, count, 2)])

time: 61.7 us -> 58.4 us (0.947); the launches traced: 60.6 us -> 58.1 us
  starting transfers between devices: 26.8 us -> 19.3 us
  waiting for transfers between devices: 23.8 us -> 29.9 us
  local copies, waits for them, and re-layouts: 3.28 us -> 1.7 us
    ppermute x11, starting transfers between devices: 26.8 us -> 19.3 us  [send(): lax.ppermute(value, AXES, [(s * count + g, t * count + h) for (s, g), (t,...]
    ppermute x11, waiting for transfers between devices: 23.8 us -> 29.9 us  [send(): lax.ppermute(value, AXES, [(s * count + g, t * count + h) for (s, g), (t,...]
    unnamed x11, local copies, waits for them, and re-layouts: 3.28 us -> 1.7 us
    pallas_call x1 -> x2, Pallas kernels: 1.63 us -> 2.18 us  [the longest x1 1.36 us: inner_sums(): pl.pallas_call(functools.partial(inner_body, pairs=pairs), out_shape=[jax...]
  transfers between devices with their start and end apart: 11 -> 11, of which waited for: 3 -> 6; matrix products, arithmetic and copies ran while one was open for 0% -> 0% of each run, Pallas kernels for 5% -> 5%
where the time goes in v5:
time: 58.4 us; the launch traced here: 58.1 us
  waiting for transfers between devices  29.9 us (51%)
  starting transfers between devices  19.3 us (33%)
  Pallas kernels  6.93 us (12%)
  local copies, waits for them, and re-layouts  1.7 us (3%)
    ppermute x11, waiting for transfers between devices, send(): lax.ppermute(value, AXES, [(s * count + g, t * count + h) for (s, g), (t,...  29.9 us
    ppermute x11, starting transfers between devices, send(): lax.ppermute(value, AXES, [(s * count + g, t * count + h) for (s, g), (t,...  19.3 us
    pallas_call x1, Pallas kernels, star_of_four(): pl.pallas_call(functools.partial(star_body, orders=orders, rows=rows), ou...  2.49 us
    unnamed x11, local copies, waits for them, and re-layouts  1.7 us
    pallas_call x1, Pallas kernels, exit_sums(): pl.pallas_call(exit_body, out_shape=[jax.ShapeDtypeStruct((share, width,...  1.63 us
    pallas_call x1, Pallas kernels, inner_sums(): pl.pallas_call(functools.partial(inner_body, pairs=pairs), out_shape=[jax...  1.36 us
  transfers between devices with their start and end apart: 11, of which 6 were waited for; matrix products, arithmetic and copies ran while one was open for 0% of the time, Pallas kernels for 5%

profile of v5, /device:TPU:0, one launch (start us, length us, event | category | flops | bytes accessed | tf_op | source)
XLA Modules:
  0.0 58.1 jit_solution(10611607618770902429)
XLA Ops:
  0.0 0.1 pad_add_fusion.place
  0.1 1.6 %copy-done = bf16[1,1024,1024]{2,1,0:T(8,128)(2,1)S(1)} copy-done((bf16[1,1024,1024]{2,1,0:T(8,128)(2,1)S(1)}, bf16[1,1024,1024]{2,1,0:T(8,128)(2,1)}, u32[]{:S(2)}) %copy-start) | copy-done | bytes 2097176
  1.7 0.8 %shard_map.55 = (bf16[1024,512]{1,0:T(8,128)(2,1)S(1)}, bf16[1024,512]{1,0:T(8,128)(2,1)S(1)}) custom-call(s32[4]{0:T(128)S(1)} %pad_add_fusion.place, bf16[1024,1024]{1,0:T(8,128)(2,1)S(1)} %bitcast.5), custom_call_target="tpu_custom_call" | custom-call | bytes 4194304 | tf_op jit(solution)/shard_map/pallas_call | solution.py:230
  2.5 0.5 collective-permute-start
  3.0 4.6 %collective-permute-start.1 = (bf16[1024,512]{1,0:T(8,128)(2,1)S(1)}, bf16[1024,512]{1,0:T(8,128)(2,1)S(1)}, u32[]{:S(2)}, u32[]{:S(2)}) collective-permute-start(bf16[1024,512]{1,0:T(8,128)(2,1)S(1)} %get-tuple-element.13.refs_0_), channel_id=1, source_target_pairs={{0,4},{5,1},{2,6},{7,3},{4,8},{9,5},{6,10},{11,7},{8,12},{13,9},{1... | collective-permute-start | bytes 3145736 | tf_op jit(solution)/shard_map/ppermute | solution.py:302
  7.6 3.5 %collective-permute-start.2 = (bf16[1024,512]{1,0:T(8,128)(2,1)S(1)}, bf16[1024,512]{1,0:T(8,128)(2,1)S(1)}, u32[]{:S(2)}, u32[]{:S(2)}) collective-permute-start(bf16[1024,512]{1,0:T(8,128)(2,1)S(1)} %collective-permute-done.refs_1_), channel_id=1, source_target_pairs={{0,4},{5,1},{2,6},{7,3},{4,8},{9,5},{6,10},{11,7},{8,12},{13,9},{1... | collective-permute-start | bytes 3145736 | tf_op jit(solution)/shard_map/ppermute | solution.py:302
  11.1 1.6 %shard_map.57 = (f32[2,128,128]{2,1,0:T(8,128)S(1)}, f32[2,128,128]{2,1,0:T(8,128)S(1)}, f32[2,128,128]{2,1,0:T(8,128)S(1)}, f32[2,128,128]{2,1,0:T(8,128)S(1)}) custom-call(s32[4]{0:T(128)S(1)} %pad_add_fusion.place, bf16[1024,1024]{1,0:T(8,128)(2,1)S(1)} %bitcast.6, bf16[1024,1024]{1,0:T(8,128)(2,1)S(1)} %copy-done.1), custom_call_target="tpu_custom_call" | custom-call | flops 268435456 | bytes 4194304 | tf_op jit(solution)/shard_map/pallas_call | solution.py:205
  12.7 0.7 %collective-permute-start.4 = (f32[2,128,128]{2,1,0:T(8,128)S(1)}, f32[2,128,128]{2,1,0:T(8,128)S(1)}, u32[]{:S(2)}, u32[]{:S(2)}) collective-permute-start(f32[2,128,128]{2,1,0:T(8,128)S(1)} %get-tuple-element.18), channel_id=1, source_target_pairs={{12,13},{13,14},{14,15},{15,12},{28,29},{29,30},{30,31},{31,28}} | collective-permute-start | bytes 393224 | tf_op jit(solution)/shard_map/ppermute | solution.py:302
  13.4 0.7 %collective-permute-start.5 = (f32[2,128,128]{2,1,0:T(8,128)S(1)}, f32[2,128,128]{2,1,0:T(8,128)S(1)}, u32[]{:S(2)}, u32[]{:S(2)}) collective-permute-start(f32[2,128,128]{2,1,0:T(8,128)S(1)} %get-tuple-element.19), channel_id=1, source_target_pairs={{12,14},{13,15},{14,12},{15,13},{28,30},{29,31},{30,28},{31,29}} | collective-permute-start | bytes 393224 | tf_op jit(solution)/shard_map/ppermute | solution.py:302
  14.1 0.7 %collective-permute-start.6 = (f32[2,128,128]{2,1,0:T(8,128)S(1)}, f32[2,128,128]{2,1,0:T(8,128)S(1)}, u32[]{:S(2)}, u32[]{:S(2)}) collective-permute-start(f32[2,128,128]{2,1,0:T(8,128)S(1)} %get-tuple-element.20), channel_id=1, source_target_pairs={{12,15},{13,12},{14,13},{15,14},{28,31},{29,28},{30,29},{31,30}} | collective-permute-start | bytes 393224 | tf_op jit(solution)/shard_map/ppermute | solution.py:302
  14.9 1.4 %collective-permute-start.7 = (f32[2,128,128]{2,1,0:T(8,128)S(1)}, f32[2,128,128]{2,1,0:T(8,128)S(1)}, u32[]{:S(2)}, u32[]{:S(2)}) collective-permute-start(f32[2,128,128]{2,1,0:T(8,128)S(1)} %add_add_fusion.refs_2_), channel_id=1, source_target_pairs={{12,0},{14,2},{28,16},{30,18}} | collective-permute-start | bytes 393224 | tf_op jit(solution)/shard_map/ppermute | solution.py:302
  16.3 3.5 %collective-permute-done.1.refs_2_ = bf16[1024,512]{1,0:T(8,128)(2,1)S(1)} collective-permute-done((bf16[1024,512]{1,0:T(8,128)(2,1)S(1)}, bf16[1024,512]{1,0:T(8,128)(2,1)S(1)}, u32[]{:S(2)}, u32[]{:S(2)}) %collective-permute-start.1) | collective-permute-done | bytes 1048608 | tf_op jit(solution)/shard_map/ppermute | solution.py:302
  19.8 11.2 %collective-permute-done.2.refs_3_ = bf16[1024,512]{1,0:T(8,128)(2,1)S(1)} collective-permute-done((bf16[1024,512]{1,0:T(8,128)(2,1)S(1)}, bf16[1024,512]{1,0:T(8,128)(2,1)S(1)}, u32[]{:S(2)}, u32[]{:S(2)}) %collective-permute-start.2) | collective-permute-done | bytes 1048608 | tf_op jit(solution)/shard_map/ppermute | solution.py:302
  31.1 1.4 %shard_map.56 = (f32[2,128,128]{2,1,0:T(8,128)S(1)}, f32[2,128,128]{2,1,0:T(8,128)S(1)}) custom-call(s32[4]{0:T(128)S(1)} %pad_add_fusion.place, bf16[1024,512]{1,0:T(8,128)(2,1)S(1)} %get-tuple-element.13.refs_0_, bf16[1024,512]{1,0:T(8,128)(2,1)S(1)} %collective-permute-done.refs_1_, bf16[1024,512]{1,0:T(8,128)(2,1)S(1)} %collective-permute-done.1.refs_2_, ...), custom_call_target="tpu_custom_call" | custom-call | flops 268435456 | bytes 4194304 | tf_op jit(solution)/shard_map/pallas_call | solution.py:268
  32.4 1.6 %collective-permute-start.3 = (f32[2,128,128]{2,1,0:T(8,128)S(1)}, f32[2,128,128]{2,1,0:T(8,128)S(1)}, u32[]{:S(2)}, u32[]{:S(2)}) collective-permute-start(f32[2,128,128]{2,1,0:T(8,128)S(1)} %get-tuple-element.16), channel_id=1, source_target_pairs={{0,2},{1,3},{2,0},{3,1},{4,6},{5,7},{6,4},{7,5},{8,10},{9,11},{10,... | collective-permute-start | bytes 393224 | tf_op jit(solution)/shard_map/ppermute | solution.py:302
  34.0 0.1 copy.6.pattern
  34.1 4.3 %collective-permute-done.3.refs_1_ = f32[2,128,128]{2,1,0:T(8,128)S(1)} collective-permute-done((f32[2,128,128]{2,1,0:T(8,128)S(1)}, f32[2,128,128]{2,1,0:T(8,128)S(1)}, u32[]{:S(2)}, u32[]{:S(2)}) %collective-permute-start.3) | collective-permute-done | bytes 131104 | tf_op jit(solution)/shard_map/ppermute | solution.py:302
  38.4 0.6 %shard_map.58.refs_0_ = f32[2,136,128]{2,1,0:T(8,128)S(1)} custom-call(s32[4]{0:T(128)S(1)} %pad_add_fusion.place, s32[1,8,2]{2,1,0:T(8,128)S(1)} %copy.6.pattern, f32[1,1024]{1,0:T(1,128)S(1)} %copy-done.2, f32[1,1024]{1,0:T(1,128)S(1)} %copy-done.3, f32[2,128,128]{2,1,0:T(8,128)S(1)} %get-tuple-element.15.refs_0_, ...), custom_call_target="tpu_custom_call" | custom-call | flops 131072 | bytes 917504 | tf_op jit(solution)/shard_map/pallas_call | solution.py:169
  39.0 3.6 %collective-permute-start.10 = (f32[2,136,128]{2,1,0:T(8,128)S(1)}, f32[2,136,128]{2,1,0:T(8,128)S(1)}, u32[]{:S(2)}, u32[]{:S(2)}) collective-permute-start(f32[2,136,128]{2,1,0:T(8,128)S(1)} %shard_map.58.refs_0_), channel_id=1, source_target_pairs={{0,12},{1,13},{2,14},{3,15},{4,0},{5,1},{6,2},{7,3},{8,4},{9,5},{1... | collective-permute-start | bytes 417800 | tf_op jit(solution)/shard_map/ppermute | solution.py:302
  42.7 2.2 %collective-permute-start.9 = (f32[2,136,128]{2,1,0:T(8,128)S(1)}, f32[2,136,128]{2,1,0:T(8,128)S(1)}, u32[]{:S(2)}, u32[]{:S(2)}) collective-permute-start(f32[2,136,128]{2,1,0:T(8,128)S(1)} %shard_map.58.refs_0_), channel_id=1, source_target_pairs={{0,8},{1,9},{2,10},{3,11},{4,12},{5,13},{6,14},{7,15},{8,0},{9,1},... | collective-permute-start | bytes 417800 | tf_op jit(solution)/shard_map/ppermute | solution.py:302
  44.8 1.4 %collective-permute-done.10.refs_3_ = f32[2,136,128]{2,1,0:T(8,128)S(1)} collective-permute-done((f32[2,136,128]{2,1,0:T(8,128)S(1)}, f32[2,136,128]{2,1,0:T(8,128)S(1)}, u32[]{:S(2)}, u32[]{:S(2)}) %collective-permute-start.10) | collective-permute-done | bytes 139296 | tf_op jit(solution)/shard_map/ppermute | solution.py:302
  46.3 5.6 %collective-permute-done.8.refs_1_ = f32[2,136,128]{2,1,0:T(8,128)S(1)} collective-permute-done((f32[2,136,128]{2,1,0:T(8,128)S(1)}, f32[2,136,128]{2,1,0:T(8,128)S(1)}, u32[]{:S(2)}, u32[]{:S(2)}) %collective-permute-start.8) | collective-permute-done | bytes 139296 | tf_op jit(solution)/shard_map/ppermute | solution.py:302
  51.9 3.8 %collective-permute-done.9.refs_2_ = f32[2,136,128]{2,1,0:T(8,128)S(1)} collective-permute-done((f32[2,136,128]{2,1,0:T(8,128)S(1)}, f32[2,136,128]{2,1,0:T(8,128)S(1)}, u32[]{:S(2)}, u32[]{:S(2)}) %collective-permute-start.9) | collective-permute-done | bytes 139296 | tf_op jit(solution)/shard_map/ppermute | solution.py:302
  55.7 2.5 %shard_map.59 = f32[3,2,32,128]{3,2,1,0:T(8,128)} custom-call(s32[4]{0:T(128)S(1)} %pad_add_fusion.place, f32[2,136,128]{2,1,0:T(8,128)S(1)} %shard_map.58.refs_0_, f32[2,136,128]{2,1,0:T(8,128)S(1)} %collective-permute-done.8.refs_1_, f32[2,136,128]{2,1,0:T(8,128)S(1)} %collective-permute-done.9.refs_2_, f32[2,136,128]{2,1,0:T(8,128)S(1)} %collective-permute-done.10.refs_3_), custom_call_target="tpu_custom_call" | custom-call | flops 503316480 | bytes 1048576 | tf_op jit(solution)/shard_map/pallas_call | solution.py:129
  (16 shorter events, 0.1 us)
Async XLA Ops:
  0.1 1.6 %copy-start = (bf16[1,1024,1024]{2,1,0:T(8,128)(2,1)S(1)}, bf16[1,1024,1024]{2,1,0:T(8,128)(2,1)}, u32[]{:S(2)}) copy-start(bf16[1,1024,1024]{2,1,0:T(8,128)(2,1)} %param.5) | copy-start | bytes 6291460
  1.7 9.4 %copy-start.1 = (bf16[1024,1024]{1,0:T(8,128)(2,1)S(1)}, bf16[1024,1024]{1,0:T(8,128)(2,1)}, u32[]{:S(2)}) copy-start(bf16[1024,1024]{1,0:T(8,128)(2,1)} %after.1) | copy-start | bytes 6291460
  2.5 5.1 %collective-permute-start = (bf16[1024,512]{1,0:T(8,128)(2,1)S(1)}, bf16[1024,512]{1,0:T(8,128)(2,1)S(1)}, u32[]{:S(2)}, u32[]{:S(2)}) collective-permute-start(bf16[1024,512]{1,0:T(8,128)(2,1)S(1)} %get-tuple-element.14), channel_id=1, source_target_pairs={{0,1},{1,0},{2,3},{3,2},{4,5},{5,4},{6,7},{7,6},{8,9},{9,8},{10,11... | collective-permute-start | bytes 3145736 | tf_op jit(solution)/shard_map/ppermute | solution.py:302
  3.0 16.8 %collective-permute-start.1 = (bf16[1024,512]{1,0:T(8,128)(2,1)S(1)}, bf16[1024,512]{1,0:T(8,128)(2,1)S(1)}, u32[]{:S(2)}, u32[]{:S(2)}) collective-permute-start(bf16[1024,512]{1,0:T(8,128)(2,1)S(1)} %get-tuple-element.13.refs_0_), channel_id=1, source_target_pairs={{0,4},{5,1},{2,6},{7,3},{4,8},{9,5},{6,10},{11,7},{8,12},{13,9},{1... | collective-permute-start | bytes 3145736 | tf_op jit(solution)/shard_map/ppermute | solution.py:302
  7.6 23.5 %collective-permute-start.2 = (bf16[1024,512]{1,0:T(8,128)(2,1)S(1)}, bf16[1024,512]{1,0:T(8,128)(2,1)S(1)}, u32[]{:S(2)}, u32[]{:S(2)}) collective-permute-start(bf16[1024,512]{1,0:T(8,128)(2,1)S(1)} %collective-permute-done.refs_1_), channel_id=1, source_target_pairs={{0,4},{5,1},{2,6},{7,3},{4,8},{9,5},{6,10},{11,7},{8,12},{13,9},{1... | collective-permute-start | bytes 3145736 | tf_op jit(solution)/shard_map/ppermute | solution.py:302
  12.7 2.0 %collective-permute-start.4 = (f32[2,128,128]{2,1,0:T(8,128)S(1)}, f32[2,128,128]{2,1,0:T(8,128)S(1)}, u32[]{:S(2)}, u32[]{:S(2)}) collective-permute-start(f32[2,128,128]{2,1,0:T(8,128)S(1)} %get-tuple-element.18), channel_id=1, source_target_pairs={{12,13},{13,14},{14,15},{15,12},{28,29},{29,30},{30,31},{31,28}} | collective-permute-start | bytes 393224 | tf_op jit(solution)/shard_map/ppermute | solution.py:302
  13.4 1.4 %collective-permute-start.5 = (f32[2,128,128]{2,1,0:T(8,128)S(1)}, f32[2,128,128]{2,1,0:T(8,128)S(1)}, u32[]{:S(2)}, u32[]{:S(2)}) collective-permute-start(f32[2,128,128]{2,1,0:T(8,128)S(1)} %get-tuple-element.19), channel_id=1, source_target_pairs={{12,14},{13,15},{14,12},{15,13},{28,30},{29,31},{30,28},{31,29}} | collective-permute-start | bytes 393224 | tf_op jit(solution)/shard_map/ppermute | solution.py:302
  14.1 0.7 %collective-permute-start.6 = (f32[2,128,128]{2,1,0:T(8,128)S(1)}, f32[2,128,128]{2,1,0:T(8,128)S(1)}, u32[]{:S(2)}, u32[]{:S(2)}) collective-permute-start(f32[2,128,128]{2,1,0:T(8,128)S(1)} %get-tuple-element.20), channel_id=1, source_target_pairs={{12,15},{13,12},{14,13},{15,14},{28,31},{29,28},{30,29},{31,30}} | collective-permute-start | bytes 393224 | tf_op jit(solution)/shard_map/ppermute | solution.py:302
  14.8 19.1 %copy-start.4 = (s32[1,8,2]{1,2,0:T(2,128)S(1)}, s32[1,8,2]{1,2,0:T(2,128)}, u32[]{:S(2)}) copy-start(s32[1,8,2]{1,2,0:T(2,128)} %param.7) | copy-start | bytes 196
  14.8 23.6 %copy-start.2 = (f32[1,1024]{1,0:T(1,128)S(1)}, f32[1,1024]{1,0:T(1,128)}, u32[]{:S(2)}) copy-start(f32[1,1024]{1,0:T(1,128)} %decays.1) | copy-start | bytes 12292
  14.9 23.6 %copy-start.3 = (f32[1,1024]{1,0:T(1,128)S(1)}, f32[1,1024]{1,0:T(1,128)}, u32[]{:S(2)}) copy-start(f32[1,1024]{1,0:T(1,128)} %mirrors.1) | copy-start | bytes 12292
  14.9 19.2 %collective-permute-start.7 = (f32[2,128,128]{2,1,0:T(8,128)S(1)}, f32[2,128,128]{2,1,0:T(8,128)S(1)}, u32[]{:S(2)}, u32[]{:S(2)}) collective-permute-start(f32[2,128,128]{2,1,0:T(8,128)S(1)} %add_add_fusion.refs_2_), channel_id=1, source_target_pairs={{12,0},{14,2},{28,16},{30,18}} | collective-permute-start | bytes 393224 | tf_op jit(solution)/shard_map/ppermute | solution.py:302
  32.4 6.0 %collective-permute-start.3 = (f32[2,128,128]{2,1,0:T(8,128)S(1)}, f32[2,128,128]{2,1,0:T(8,128)S(1)}, u32[]{:S(2)}, u32[]{:S(2)}) collective-permute-start(f32[2,128,128]{2,1,0:T(8,128)S(1)} %get-tuple-element.16), channel_id=1, source_target_pairs={{0,2},{1,3},{2,0},{3,1},{4,6},{5,7},{6,4},{7,5},{8,10},{9,11},{10,... | collective-permute-start | bytes 393224 | tf_op jit(solution)/shard_map/ppermute | solution.py:302
  39.0 7.2 %collective-permute-start.10 = (f32[2,136,128]{2,1,0:T(8,128)S(1)}, f32[2,136,128]{2,1,0:T(8,128)S(1)}, u32[]{:S(2)}, u32[]{:S(2)}) collective-permute-start(f32[2,136,128]{2,1,0:T(8,128)S(1)} %shard_map.58.refs_0_), channel_id=1, source_target_pairs={{0,12},{1,13},{2,14},{3,15},{4,0},{5,1},{6,2},{7,3},{8,4},{9,5},{1... | collective-permute-start | bytes 417800 | tf_op jit(solution)/shard_map/ppermute | solution.py:302
  42.7 9.2 %collective-permute-start.8 = (f32[2,136,128]{2,1,0:T(8,128)S(1)}, f32[2,136,128]{2,1,0:T(8,128)S(1)}, u32[]{:S(2)}, u32[]{:S(2)}) collective-permute-start(f32[2,136,128]{2,1,0:T(8,128)S(1)} %shard_map.58.refs_0_), channel_id=1, source_target_pairs={{0,4},{1,5},{2,6},{3,7},{4,8},{5,9},{6,10},{7,11},{8,12},{9,13},{1... | collective-permute-start | bytes 417800 | tf_op jit(solution)/shard_map/ppermute | solution.py:302
  42.7 13.0 %collective-permute-start.9 = (f32[2,136,128]{2,1,0:T(8,128)S(1)}, f32[2,136,128]{2,1,0:T(8,128)S(1)}, u32[]{:S(2)}, u32[]{:S(2)}) collective-permute-start(f32[2,136,128]{2,1,0:T(8,128)S(1)} %shard_map.58.refs_0_), channel_id=1, source_target_pairs={{0,8},{1,9},{2,10},{3,11},{4,12},{5,13},{6,14},{7,15},{8,0},{9,1},... | collective-permute-start | bytes 417800 | tf_op jit(solution)/shard_map/ppermute | solution.py:302

commit v6 on v4

--- a/solution.py
+++ b/solution.py
@@ -30,8 +30,11 @@
 
 
 def star_body(place, *refs, orders, rows):
-    terms = refs[:BLOCK]
-    out, tbuf, abuf, rbuf = refs[BLOCK:]
+    terms, done = refs[:BLOCK], refs[BLOCK:-4]
+    out, tbuf, abuf, rbuf = refs[-4:]
+    earlier = out.shape[1] - orders
+    for ready in done:
+        out[:, :earlier] = ready[...]
     width = out.shape[-1]
     for slot in range(BLOCK):
         origin = lax.rem(place[1] + BLOCK - slot, BLOCK)
@@ -111,10 +114,10 @@
         behind = behind + mul(halves(behind), square, True)
         yield
         ahead = mul(halves(ahead), trans_a)
-        out[0, order] = ahead[:rows]
-        out[1, order] = front_a_part + ahead[rows:]
-        yield
-        out[2, order] = back_b_part + mul(halves(behind), trans_b, True)
+        out[0, earlier + order] = ahead[:rows]
+        out[1, earlier + order] = front_a_part + ahead[rows:]
+        yield
+        out[2, earlier + order] = back_b_part + mul(halves(behind), trans_b, True)
         yield
 
     running = [steps(order) for order in range(orders)]
@@ -122,14 +125,15 @@
         running = [one for one in running if next(one, 0) is None]
 
 
-def star_of_four(place, terms, rows):
+def star_of_four(place, terms, rows, done):
     orders, width = terms[0].shape[0], terms[0].shape[-1]
     extra = terms[0].shape[1] - width
+    earlier = sum(ready.shape[1] for ready in done)
     vmem = pl.BlockSpec(memory_space=pltpu.VMEM)
     return pl.pallas_call(
         functools.partial(star_body, orders=orders, rows=rows),
-        out_shape=jax.ShapeDtypeStruct((3, orders, rows, width), jnp.float32),
-        in_specs=[pl.BlockSpec(memory_space=pltpu.SMEM)] + [vmem] * BLOCK,
+        out_shape=jax.ShapeDtypeStruct((3, earlier + orders, rows, width), jnp.float32),
+        in_specs=[pl.BlockSpec(memory_space=pltpu.SMEM)] + [vmem] * (BLOCK + len(done)),
         out_specs=vmem,
         scratch_shapes=[
             pltpu.VMEM((BLOCK, orders, width, width), jnp.float32),
@@ -140,34 +144,33 @@
         cost_estimate=pl.CostEstimate(
             flops=orders * 120 * width**3, bytes_accessed=orders * 8 * 4 * width**2, transcendentals=0
         ),
-    )(place, *terms)
-
-
-def own_body(place, pattern, decays, mirrors, *refs):
+    )(place, *terms, *done)
+
+
+def own_body(place, pattern, decays, mirrors, *refs, item):
     parts, (exits, hop, out) = refs[:-3], refs[-3:]
     width = out.shape[-1]
     out[:, width:] = jnp.zeros_like(out[:, width:])
-    share = out.shape[0]
-    for index in range(share):
-        total = parts[0][index]
-        for part in parts[1:]:
-            total = total + part[index]
-        total = jnp.where(place[3] == 1, exits[index], total)
-        out[index, :width] = jnp.where(place[3] == 2, hop[index], total)
-        order = place[0] * share + index
-        columns = pl.ds(pl.multiple_of(order * width, width), width)
-        out[index, width : width + 1] = decays[:, columns]
-        out[index, width + 1 : width + 2] = mirrors[:, columns]
-        for side in (0, 1):
-            flag = pattern[0, order, side].astype(jnp.float32)
-            out[index, width + 2 + side : width + 3 + side] = jnp.full((1, width), flag)
-
-
-def own_terms(place, pattern, decays, mirrors, parts, exits, hop):
+    share = exits.shape[0]
+    total = parts[0][0]
+    for part in parts[1:]:
+        total = total + part[0]
+    total = jnp.where(place[3] == 1, exits[item], total)
+    out[0, :width] = jnp.where(place[3] == 2, hop[item], total)
+    order = place[0] * share + item
+    columns = pl.ds(pl.multiple_of(order * width, width), width)
+    out[0, width : width + 1] = decays[:, columns]
+    out[0, width + 1 : width + 2] = mirrors[:, columns]
+    for side in (0, 1):
+        flag = pattern[0, order, side].astype(jnp.float32)
+        out[0, width + 2 + side : width + 3 + side] = jnp.full((1, width), flag)
+
+
+def own_terms(place, pattern, decays, mirrors, parts, exits, hop, item):
     number, width = parts[0].shape[0], parts[0].shape[-1]
     vmem, smem = pl.BlockSpec(memory_space=pltpu.VMEM), pl.BlockSpec(memory_space=pltpu.SMEM)
     return pl.pallas_call(
-        own_body,
+        functools.partial(own_body, item=item),
         out_shape=jax.ShapeDtypeStruct((number, width + 8, width), jnp.float32),
         in_specs=[smem] * 2 + [vmem] * (4 + len(parts)),
         out_specs=vmem,
@@ -183,74 +186,75 @@
     return lax.dot_general(left, right, dims, preferred_element_type=jnp.float32)
 
 
-def hand_out(place, terms, outs):
-    count = len(outs)
+def pack_body(place, fields, *outs, pairs):
+    share, width = len(outs) // 2, outs[0].shape[1] // pairs
+    parity = lax.rem(place[0], 2)
+    for index, out in enumerate(outs):
+        kind = parity if index % 2 == 0 else 1 - parity
+        for pair in range(pairs):
+            order = (2 * pair + kind) * share + index // 2
+            out[:, pl.ds(pair * width, width)] = fields[:, pl.ds(pl.multiple_of(order * width, width), width)]
+
+
+def packed(place, fields, pairs, share):
+    points, modes = fields.shape
+    vmem = pl.BlockSpec(memory_space=pltpu.VMEM)
+    return pl.pallas_call(
+        functools.partial(pack_body, pairs=pairs),
+        out_shape=[jax.ShapeDtypeStruct((points, modes // (2 * share)), fields.dtype)] * (2 * share),
+        in_specs=[pl.BlockSpec(memory_space=pltpu.SMEM), vmem],
+        out_specs=[vmem] * (2 * share),
+        compiler_params=ROOM,
+        cost_estimate=pl.CostEstimate(flops=0, bytes_accessed=4 * points * modes, transcendentals=0),
+    )(place, fields)
+
+
+def inner_body(place, *refs, pairs, ends):
+    outs, terms = refs[-1 - pairs : -1], refs[-1]
+    items, width = terms.shape[1], terms.shape[-1]
+    own, arrived = refs[: 2 * items], refs[2 * items : 4 * items]
+
+    def fill(left, right):
+        for pair in range(pairs):
+            for item in range(items):
+                columns = pl.ds(pair * width, width)
+                blocks = range(2 * item, 2 * item + 2)
+                first, second = [tall_dot(left[i][:, columns], right[i][:, columns]) for i in blocks]
+                terms[pair, item] = first + second
+
+    if ends:
+        fill(own, arrived)
+    else:
+        even = lax.rem(place[0], 2) == 0
+
+        @pl.when(even)
+        def _():
+            fill(arrived, own)
+
+        @pl.when(jnp.logical_not(even))
+        def _():
+            fill(own, arrived)
+
     for turn, out in enumerate(outs):
-        out[...] = terms[lax.rem(place[0] + turn, count)]
-
-
-def exit_body(place, own, after, *refs):
-    outs, terms = refs[:-1], refs[-1]
-    count, share, width = terms.shape[:3]
-    for spot in range(count):
-        for item in range(share):
-            columns = pl.ds((spot * share + item) * width, width)
-            terms[spot, item] = tall_dot(own[:, columns], after[:, columns])
-    hand_out(place, terms, outs)
-
-
-def exit_sums(place, fields, exit_modes, count, share, width):
-    points, modes = fields.shape
+        out[...] = terms[lax.rem(lax.div(place[0], 2) + turn, pairs)]
+
+
+def inner_sums(place, own, arrived, pairs, width, ends=False):
+    points, items = own[0].shape[0], len(own) // 2
     whole = pl.BlockSpec(memory_space=pltpu.VMEM)
     return pl.pallas_call(
-        exit_body,
-        out_shape=[jax.ShapeDtypeStruct((share, width, width), jnp.float32)] * count,
-        in_specs=[pl.BlockSpec(memory_space=pltpu.SMEM), whole, whole],
-        out_specs=[whole] * count,
-        scratch_shapes=[pltpu.VMEM((count, share, width, width), jnp.float32)],
+        functools.partial(inner_body, pairs=pairs, ends=ends),
+        out_shape=[jax.ShapeDtypeStruct((items, width, width), jnp.float32)] * pairs,
+        in_specs=[pl.BlockSpec(memory_space=pltpu.SMEM)] + [whole] * (4 * items),
+        out_specs=[whole] * pairs,
+        scratch_shapes=[pltpu.VMEM((pairs, items, width, width), jnp.float32)],
         compiler_params=ROOM,
         cost_estimate=pl.CostEstimate(
-            flops=2 * points * modes * width, bytes_accessed=4 * points * modes, transcendentals=0
+            flops=4 * points * pairs * items * width**2,
+            bytes_accessed=8 * points * pairs * items * width,
+            transcendentals=0,
         ),
-    )(place, fields, exit_modes)
-
-
-def inner_body(place, fields, arrived, *refs):
-    outs, terms = refs[:-1], refs[-1]
-    count, share, width = terms.shape[:3]
-
-    def fill(left, right):
-        for order in range(count * share):
-            columns = pl.ds(order * width, width)
-            terms[order // share, order % share] = tall_dot(left[:, columns], right[:, columns])
-
-    even = lax.rem(place[0], 2) == 0
-
-    @pl.when(even)
-    def _():
-        fill(arrived, fields)
-
-    @pl.when(jnp.logical_not(even))
-    def _():
-        fill(fields, arrived)
-
-    hand_out(place, terms, outs)
-
-
-def inner_sums(place, fields, arrived, count, share, width):
-    points, modes = fields.shape
-    whole = pl.BlockSpec(memory_space=pltpu.VMEM)
-    return pl.pallas_call(
-        inner_body,
-        out_shape=[jax.ShapeDtypeStruct((share, width, width), jnp.float32)] * count,
-        in_specs=[pl.BlockSpec(memory_space=pltpu.SMEM), whole, whole],
-        out_specs=[whole] * count,
-        scratch_shapes=[pltpu.VMEM((count, share, width, width), jnp.float32)],
-        compiler_params=ROOM,
-        cost_estimate=pl.CostEstimate(
-            flops=2 * points * modes * width, bytes_accessed=4 * points * modes, transcendentals=0
-        ),
-    )(place, fields, arrived)
+    )(place, *own, *arrived)
 
 
 def body(modes, exit_modes, pattern, attenuation, reflection):
@@ -274,32 +278,43 @@
     def send(value, pairs):
         return lax.ppermute(value, AXES, [(s * count + g, t * count + h) for (s, g), (t, h) in pairs])
 
-    def gathered(parts, members):
+    grid, pairs = range(count), count // 2
+    everywhere = [(s, g) for s in range(sections) for g in grid]
+
+    def beside(columns):
+        got = [send(columns[2 * item + 1], [((s, g), (s, g ^ 1)) for s, g in everywhere]) for item in range(share)]
+        return [[columns[2 * item], got[item]] for item in range(share)]
+
+    def summed_over(parts, members):
         got = [parts[0]]
-        for turn in range(1, count):
-            got.append(send(parts[turn], [(row[g], row[(g + turn) % count]) for row in members for g in range(count)]))
+        for turn in range(1, pairs):
+            got.append(send(parts[turn], [((s, g), (s, (g + 2 * turn) % count)) for s, g in members]))
         return got
 
-    steps = [((s + g % 2, g), (s + 1 - g % 2, g)) for s in range(final) for g in range(count)]
-    arrived = send(fields, steps)
-
-    exit_parts = exit_sums(place, fields, exit_modes, count, share, width)
-    exits = sum(gathered(exit_parts, [[(final, g) for g in range(count)]]))
-    hop = send(exits, [((final, g), (0, g)) for g in range(0, count, 2)]) if small else exits
-
-    parts = inner_sums(place, fields, arrived, count, share, width)
-    parts = gathered(parts, [[(s + 1 - g % 2, g) for g in range(count)] for s in range(final)])
-    if not small:
-        own = sum(parts)
-        back = send(own, [((s + 1, g), (s, g)) for s in range(final) for g in range(0, count, 2)])
-        parts = [jnp.where(even == 1, back, own)]
-    own = own_terms(place, pattern, attenuation, reflection, parts, exits, hop)
-    terms = [own]
-    for turn in range(1, BLOCK):
-        ring = [(s, s - s % BLOCK + (s + turn) % BLOCK) for s in range(sections)]
-        terms.append(send(own, [((s, g), (t, g)) for s, t in ring for g in range(count)]))
-    merged = star_of_four(place, terms, width // sections if small else width)
-    return merged if small else later_levels(merged, sections, sec)
+    steps = [((s + g % 2, g), (s + 1 - g % 2, g)) for s in range(final) for g in grid]
+    own_fields = beside(packed(place, fields, pairs, share))
+    arrived = [[send(block, steps) for block in blocks] for blocks in own_fields]
+
+    ending = beside(packed(place, exit_modes, pairs, share))
+    exit_parts = inner_sums(place, sum(own_fields, []), sum(ending, []), pairs, width, True)
+    exits = sum(summed_over(exit_parts, [(final, g) for g in grid]))
+    hop = send(exits, [((final, g), (0, g)) for g in grid if g % 2 == 0]) if small else exits
+
+    done = []
+    for item in range(share):
+        parts = inner_sums(place, own_fields[item], arrived[item], pairs, width)
+        parts = summed_over(parts, everywhere)
+        if not small:
+            own = sum(parts)
+            back = send(own, [((s + 1, g), (s, g)) for s in range(final) for g in grid if g % 2 == 0])
+            parts = [jnp.where(even == 1, back, own)]
+        own = own_terms(place, pattern, attenuation, reflection, parts, exits, hop, item)
+        terms = [own]
+        for turn in range(1, BLOCK):
+            ring = [(s, s - s % BLOCK + (s + turn) % BLOCK) for s in range(sections)]
+            terms.append(send(own, [((s, g), (t, g)) for s, t in ring for g in grid]))
+        done = [star_of_four(place, terms, width // sections if small else width, done)]
+    return done[0] if small else later_levels(done[0], sections, sec)
 
 
 def pair_body(first, second, out):

time: 61.7 us -> 54.1 us (0.88); the launches traced: 60.6 us -> 53.9 us
  waiting for transfers between devices: 23.8 us -> 12.3 us
  Pallas kernels: 6.38 us -> 10.7 us
  starting transfers between devices: 26.8 us -> 28.9 us
  local copies, waits for them, and re-layouts: 3.28 us -> 1.69 us
    ppermute x11 -> x18, waiting for transfers between devices: 23.8 us -> 12.3 us  [send(): lax.ppermute(value, AXES, [(s * count + g, t * count + h) for (s, g), (t,...]
    pallas_call x3 -> x7, Pallas kernels: 3.89 us -> 6.94 us  [the longest x3 3.49 us: inner_sums(): pl.pallas_call(functools.partial(inner_body, pairs=pairs, ends=ends), out...]
    ppermute x11 -> x18, starting transfers between devices: 26.8 us -> 28.9 us  [send(): lax.ppermute(value, AXES, [(s * count + g, t * count + h) for (s, g), (t,...]
    unnamed x11, local copies, waits for them, and re-layouts: 3.28 us -> 1.69 us
    pallas_call x1 -> x2, Pallas kernels: 2.49 us -> 3.8 us  [star_of_four(): pl.pallas_call(functools.partial(star_body, orders=orders, rows=rows), ou...]
  transfers between devices with their start and end apart: 11 -> 18, of which waited for: 3 -> 4; matrix products, arithmetic and copies ran while one was open for 0% -> 0% of each run, Pallas kernels for 5% -> 14%
where the time goes in v6:
time: 54.1 us; the launch traced here: 53.9 us
  starting transfers between devices  28.9 us (53%)
  waiting for transfers between devices  12.3 us (23%)
  Pallas kernels  10.7 us (20%)
  local copies, waits for them, and re-layouts  1.69 us (3%)
    ppermute x18, starting transfers between devices, send(): lax.ppermute(value, AXES, [(s * count + g, t * count + h) for (s, g), (t,...  28.9 us
    ppermute x18, waiting for transfers between devices, send(): lax.ppermute(value, AXES, [(s * count + g, t * count + h) for (s, g), (t,...  12.3 us
    pallas_call x2, Pallas kernels, star_of_four(): pl.pallas_call(functools.partial(star_body, orders=orders, rows=rows), ou...  3.8 us
    pallas_call x3, Pallas kernels, inner_sums(): pl.pallas_call(functools.partial(inner_body, pairs=pairs, ends=ends), out...  3.49 us
    pallas_call x2, Pallas kernels, packed(): pl.pallas_call(functools.partial(pack_body, pairs=pairs), out_shape=[jax....  2.2 us
    unnamed x11, local copies, waits for them, and re-layouts  1.69 us
    pallas_call x2, Pallas kernels, own_terms(): pl.pallas_call(functools.partial(own_body, item=item), out_shape=jax.Shap...  1.24 us
  transfers between devices with their start and end apart: 18, of which 4 were waited for; matrix products, arithmetic and copies ran while one was open for 0% of the time, Pallas kernels for 14%

profile of v6, /device:TPU:0, one launch (start us, length us, event | category | flops | bytes accessed | tf_op | source)
XLA Modules:
  0.0 53.9 jit_solution(1962166196504904458)
XLA Ops:
  0.1 1.6 %copy-done = bf16[1,1024,1024]{2,1,0:T(8,128)(2,1)S(1)} copy-done((bf16[1,1024,1024]{2,1,0:T(8,128)(2,1)S(1)}, bf16[1,1024,1024]{2,1,0:T(8,128)(2,1)}, u32[]{:S(2)}) %copy-start) | copy-done | bytes 2097176
  1.7 1.1 %shard_map.55 = (bf16[1024,256]{1,0:T(8,128)(2,1)S(1)}, bf16[1024,256]{1,0:T(8,128)(2,1)S(1)}, bf16[1024,256]{1,0:T(8,128)(2,1)S(1)}, bf16[1024,256]{1,0:T(8,128)(2,1)S(1)}) custom-call(s32[4]{0:T(128)S(1)} %pad_add_fusion.place, bf16[1024,1024]{1,0:T(8,128)(2,1)S(1)} %bitcast.5), custom_call_target="tpu_custom_call" | custom-call | bytes 4194304 | tf_op jit(solution)/shard_map/pallas_call | solution.py:202
  3.4 1.1 %shard_map.57 = (bf16[1024,256]{1,0:T(8,128)(2,1)S(1)}, bf16[1024,256]{1,0:T(8,128)(2,1)S(1)}, bf16[1024,256]{1,0:T(8,128)(2,1)S(1)}, bf16[1024,256]{1,0:T(8,128)(2,1)S(1)}) custom-call(s32[4]{0:T(128)S(1)} %pad_add_fusion.place, bf16[1024,1024]{1,0:T(8,128)(2,1)S(1)} %copy-done.1), custom_call_target="tpu_custom_call" | custom-call | bytes 4194304 | tf_op jit(solution)/shard_map/pallas_call | solution.py:202
  5.1 4.9 %collective-permute-start.12 = (bf16[1024,256]{1,0:T(8,128)(2,1)S(1)}, bf16[1024,256]{1,0:T(8,128)(2,1)S(1)}, u32[]{:S(2)}, u32[]{:S(2)}) collective-permute-start(bf16[1024,256]{1,0:T(8,128)(2,1)S(1)} %get-tuple-element.23.refs_0_), channel_id=1, source_target_pairs={{0,4},{5,1},{2,6},{7,3},{4,8},{9,5},{6,10},{11,7},{8,12},{13,9},{1... | collective-permute-start | bytes 1572872 | tf_op jit(solution)/shard_map/ppermute | solution.py:279
  10.0 3.5 %collective-permute-start.13 = (bf16[1024,256]{1,0:T(8,128)(2,1)S(1)}, bf16[1024,256]{1,0:T(8,128)(2,1)S(1)}, u32[]{:S(2)}, u32[]{:S(2)}) collective-permute-start(bf16[1024,256]{1,0:T(8,128)(2,1)S(1)} %collective-permute-done.4.refs_1_), channel_id=1, source_target_pairs={{0,4},{5,1},{2,6},{7,3},{4,8},{9,5},{6,10},{11,7},{8,12},{13,9},{1... | collective-permute-start | bytes 1572872 | tf_op jit(solution)/shard_map/ppermute | solution.py:279
  13.5 3.5 %collective-permute-start.1 = (bf16[1024,256]{1,0:T(8,128)(2,1)S(1)}, bf16[1024,256]{1,0:T(8,128)(2,1)S(1)}, u32[]{:S(2)}, u32[]{:S(2)}) collective-permute-start(bf16[1024,256]{1,0:T(8,128)(2,1)S(1)} %get-tuple-element.19.refs_0_.refs_2_), channel_id=1, source_target_pairs={{0,4},{5,1},{2,6},{7,3},{4,8},{9,5},{6,10},{11,7},{8,12},{13,9},{1... | collective-permute-start | bytes 1572872 | tf_op jit(solution)/shard_map/ppermute | solution.py:279
  17.0 1.9 %collective-permute-start.2 = (bf16[1024,256]{1,0:T(8,128)(2,1)S(1)}, bf16[1024,256]{1,0:T(8,128)(2,1)S(1)}, u32[]{:S(2)}, u32[]{:S(2)}) collective-permute-start(bf16[1024,256]{1,0:T(8,128)(2,1)S(1)} %collective-permute-done.refs_1_.refs_3_), channel_id=1, source_target_pairs={{0,4},{5,1},{2,6},{7,3},{4,8},{9,5},{6,10},{11,7},{8,12},{13,9},{1... | collective-permute-start | bytes 1572872 | tf_op jit(solution)/shard_map/ppermute | solution.py:279
  18.9 1.4 %shard_map.58 = (f32[2,128,128]{2,1,0:T(8,128)S(1)}, f32[2,128,128]{2,1,0:T(8,128)S(1)}) custom-call(s32[4]{0:T(128)S(1)} %pad_add_fusion.place, bf16[1024,256]{1,0:T(8,128)(2,1)S(1)} %get-tuple-element.23.refs_0_, bf16[1024,256]{1,0:T(8,128)(2,1)S(1)} %collective-permute-done.4.refs_1_, bf16[1024,256]{1,0:T(8,128)(2,1)S(1)} %get-tuple-element.19.refs_0_.refs_2_, ...), custom_call_target="tpu_custom_call" | custom-call | flops 268435456 | bytes 4194304 | tf_op jit(solution)/shard_map/pallas_call | solution.py:245
  20.4 0.8 %collective-permute-start.7 = (f32[2,128,128]{2,1,0:T(8,128)S(1)}, f32[2,128,128]{2,1,0:T(8,128)S(1)}, u32[]{:S(2)}, u32[]{:S(2)}) collective-permute-start(f32[2,128,128]{2,1,0:T(8,128)S(1)} %get-tuple-element.30), channel_id=1, source_target_pairs={{12,14},{13,15},{14,12},{15,13},{28,30},{29,31},{30,28},{31,29}} | collective-permute-start | bytes 393224 | tf_op jit(solution)/shard_map/ppermute | solution.py:279
  21.2 1.3 %collective-permute-start.8 = (f32[2,128,128]{2,1,0:T(8,128)S(1)}, f32[2,128,128]{2,1,0:T(8,128)S(1)}, u32[]{:S(2)}, u32[]{:S(2)}) collective-permute-start(f32[2,128,128]{2,1,0:T(8,128)S(1)} %add.3.refs_2_), channel_id=1, source_target_pairs={{12,0},{14,2},{28,16},{30,18}} | collective-permute-start | bytes 393224 | tf_op jit(solution)/shard_map/ppermute | solution.py:279
  22.5 1.1 %shard_map.60 = (f32[1,128,128]{2,1,0:T(8,128)S(1)}, f32[1,128,128]{2,1,0:T(8,128)S(1)}) custom-call(s32[4]{0:T(128)S(1)} %pad_add_fusion.place, bf16[1024,256]{1,0:T(8,128)(2,1)S(1)} %get-tuple-element.23.refs_0_, bf16[1024,256]{1,0:T(8,128)(2,1)S(1)} %collective-permute-done.4.refs_1_, bf16[1024,256]{1,0:T(8,128)(2,1)S(1)} %collective-permute-done.12.refs_2_, ...), custom_call_target="tpu_custom_call" | custom-call | flops 134217728 | bytes 2097152 | tf_op jit(solution)/shard_map/pallas_call | solution.py:245
  23.6 1.6 %collective-permute-start.14 = (f32[1,128,128]{2,1,0:T(8,128)S(1)}, f32[1,128,128]{2,1,0:T(8,128)S(1)}, u32[]{:S(2)}, u32[]{:S(2)}) collective-permute-start(f32[1,128,128]{2,1,0:T(8,128)S(1)} %get-tuple-element.32), channel_id=1, source_target_pairs={{0,2},{1,3},{2,0},{3,1},{4,6},{5,7},{6,4},{7,5},{8,10},{9,11},{10,... | collective-permute-start | bytes 196616 | tf_op jit(solution)/shard_map/ppermute | solution.py:279
  25.2 6.1 %collective-permute-done.8.refs_3_ = f32[2,128,128]{2,1,0:T(8,128)S(1)} collective-permute-done((f32[2,128,128]{2,1,0:T(8,128)S(1)}, f32[2,128,128]{2,1,0:T(8,128)S(1)}, u32[]{:S(2)}, u32[]{:S(2)}) %collective-permute-start.8) | collective-permute-done | bytes 131104 | tf_op jit(solution)/shard_map/ppermute | solution.py:279
  32.1 2.2 %collective-permute-done.2.refs_3_ = bf16[1024,256]{1,0:T(8,128)(2,1)S(1)} collective-permute-done((bf16[1024,256]{1,0:T(8,128)(2,1)S(1)}, bf16[1024,256]{1,0:T(8,128)(2,1)S(1)}, u32[]{:S(2)}, u32[]{:S(2)}) %collective-permute-start.2) | collective-permute-done | bytes 524320 | tf_op jit(solution)/shard_map/ppermute | solution.py:279
  34.2 1.1 %shard_map.56 = (f32[1,128,128]{2,1,0:T(8,128)S(1)}, f32[1,128,128]{2,1,0:T(8,128)S(1)}) custom-call(s32[4]{0:T(128)S(1)} %pad_add_fusion.place, bf16[1024,256]{1,0:T(8,128)(2,1)S(1)} %get-tuple-element.19.refs_0_.refs_2_, bf16[1024,256]{1,0:T(8,128)(2,1)S(1)} %collective-permute-done.refs_1_.refs_3_, bf16[1024,256]{1,0:T(8,128)(2,1)S(1)} %collective-permute-done.1.refs_2_, ...), custom_call_target="tpu_custom_call" | custom-call | flops 134217728 | bytes 2097152 | tf_op jit(solution)/shard_map/pallas_call | solution.py:245
  35.3 1.6 %collective-permute-start.3 = (f32[1,128,128]{2,1,0:T(8,128)S(1)}, f32[1,128,128]{2,1,0:T(8,128)S(1)}, u32[]{:S(2)}, u32[]{:S(2)}) collective-permute-start(f32[1,128,128]{2,1,0:T(8,128)S(1)} %get-tuple-element.22), channel_id=1, source_target_pairs={{0,2},{1,3},{2,0},{3,1},{4,6},{5,7},{6,4},{7,5},{8,10},{9,11},{10,... | collective-permute-start | bytes 196616 | tf_op jit(solution)/shard_map/ppermute | solution.py:279
  36.9 3.5 %collective-permute-start.16 = (f32[1,136,128]{2,1,0:T(8,128)S(1)}, f32[1,136,128]{2,1,0:T(8,128)S(1)}, u32[]{:S(2)}, u32[]{:S(2)}) collective-permute-start(f32[1,136,128]{2,1,0:T(8,128)S(1)} %shard_map.61.refs_0_), channel_id=1, source_target_pairs={{0,8},{1,9},{2,10},{3,11},{4,12},{5,13},{6,14},{7,15},{8,0},{9,1},... | collective-permute-start | bytes 208904 | tf_op jit(solution)/shard_map/ppermute | solution.py:279
  40.3 1.3 %collective-permute-start.17 = (f32[1,136,128]{2,1,0:T(8,128)S(1)}, f32[1,136,128]{2,1,0:T(8,128)S(1)}, u32[]{:S(2)}, u32[]{:S(2)}) collective-permute-start(f32[1,136,128]{2,1,0:T(8,128)S(1)} %shard_map.61.refs_0_), channel_id=1, source_target_pairs={{0,12},{1,13},{2,14},{3,15},{4,0},{5,1},{6,2},{7,3},{8,4},{9,5},{1... | collective-permute-start | bytes 208904 | tf_op jit(solution)/shard_map/ppermute | solution.py:279
  42.3 1.8 %collective-permute-start.10 = (f32[1,136,128]{2,1,0:T(8,128)S(1)}, f32[1,136,128]{2,1,0:T(8,128)S(1)}, u32[]{:S(2)}, u32[]{:S(2)}) collective-permute-start(f32[1,136,128]{2,1,0:T(8,128)S(1)} %shard_map.59.refs_0_), channel_id=1, source_target_pairs={{0,8},{1,9},{2,10},{3,11},{4,12},{5,13},{6,14},{7,15},{8,0},{9,1},... | collective-permute-start | bytes 208904 | tf_op jit(solution)/shard_map/ppermute | solution.py:279
  44.1 1.3 %collective-permute-start.11 = (f32[1,136,128]{2,1,0:T(8,128)S(1)}, f32[1,136,128]{2,1,0:T(8,128)S(1)}, u32[]{:S(2)}, u32[]{:S(2)}) collective-permute-start(f32[1,136,128]{2,1,0:T(8,128)S(1)} %shard_map.59.refs_0_), channel_id=1, source_target_pairs={{0,12},{1,13},{2,14},{3,15},{4,0},{5,1},{6,2},{7,3},{8,4},{9,5},{1... | collective-permute-start | bytes 208904 | tf_op jit(solution)/shard_map/ppermute | solution.py:279
  46.1 1.6 %shard_map.62.refs_4_ = f32[3,1,32,128]{3,2,1,0:T(8,128)S(1)} custom-call(s32[4]{0:T(128)S(1)} %pad_add_fusion.place, f32[1,136,128]{2,1,0:T(8,128)S(1)} %shard_map.61.refs_0_, f32[1,136,128]{2,1,0:T(8,128)S(1)} %collective-permute-done.15.refs_1_, f32[1,136,128]{2,1,0:T(8,128)S(1)} %collective-permute-done.16.refs_2_, ...), custom_call_target="tpu_custom_call" | custom-call | flops 251658240 | bytes 524288 | tf_op jit(solution)/shard_map/pallas_call | solution.py:133
  47.7 2.4 %collective-permute-done.10.refs_2_ = f32[1,136,128]{2,1,0:T(8,128)S(1)} collective-permute-done((f32[1,136,128]{2,1,0:T(8,128)S(1)}, f32[1,136,128]{2,1,0:T(8,128)S(1)}, u32[]{:S(2)}, u32[]{:S(2)}) %collective-permute-start.10) | collective-permute-done | bytes 69664 | tf_op jit(solution)/shard_map/ppermute | solution.py:279
  50.1 1.5 %collective-permute-done.9.refs_1_ = f32[1,136,128]{2,1,0:T(8,128)S(1)} collective-permute-done((f32[1,136,128]{2,1,0:T(8,128)S(1)}, f32[1,136,128]{2,1,0:T(8,128)S(1)}, u32[]{:S(2)}, u32[]{:S(2)}) %collective-permute-start.9) | collective-permute-done | bytes 69664 | tf_op jit(solution)/shard_map/ppermute | solution.py:279
  51.6 2.2 %shard_map.63 = f32[3,2,32,128]{3,2,1,0:T(8,128)} custom-call(s32[4]{0:T(128)S(1)} %pad_add_fusion.place, f32[1,136,128]{2,1,0:T(8,128)S(1)} %shard_map.59.refs_0_, f32[1,136,128]{2,1,0:T(8,128)S(1)} %collective-permute-done.9.refs_1_, f32[1,136,128]{2,1,0:T(8,128)S(1)} %collective-permute-done.10.refs_2_, ...), custom_call_target="tpu_custom_call" | custom-call | flops 251658240 | bytes 524288 | tf_op jit(solution)/shard_map/pallas_call | solution.py:133
  (34 shorter events, 3.4 us)
Async XLA Ops:
  0.1 1.6 %copy-start = (bf16[1,1024,1024]{2,1,0:T(8,128)(2,1)S(1)}, bf16[1,1024,1024]{2,1,0:T(8,128)(2,1)}, u32[]{:S(2)}) copy-start(bf16[1,1024,1024]{2,1,0:T(8,128)(2,1)} %param.5) | copy-start | bytes 6291460
  1.7 1.7 %copy-start.1 = (bf16[1024,1024]{1,0:T(8,128)(2,1)S(1)}, bf16[1024,1024]{1,0:T(8,128)(2,1)}, u32[]{:S(2)}) copy-start(bf16[1024,1024]{1,0:T(8,128)(2,1)} %fields.1) | copy-start | bytes 6291460
  2.8 7.2 %collective-permute-start.4 = (bf16[1024,256]{1,0:T(8,128)(2,1)S(1)}, bf16[1024,256]{1,0:T(8,128)(2,1)S(1)}, u32[]{:S(2)}, u32[]{:S(2)}) collective-permute-start(bf16[1024,256]{1,0:T(8,128)(2,1)S(1)} %get-tuple-element.24), channel_id=1, source_target_pairs={{0,1},{1,0},{2,3},{3,2},{4,5},{5,4},{6,7},{7,6},{8,9},{9,8},{10,11... | collective-permute-start | bytes 1572872 | tf_op jit(solution)/shard_map/ppermute | solution.py:279
  3.3 10.2 %collective-permute-start = (bf16[1024,256]{1,0:T(8,128)(2,1)S(1)}, bf16[1024,256]{1,0:T(8,128)(2,1)S(1)}, u32[]{:S(2)}, u32[]{:S(2)}) collective-permute-start(bf16[1024,256]{1,0:T(8,128)(2,1)S(1)} %get-tuple-element.20), channel_id=1, source_target_pairs={{0,1},{1,0},{2,3},{3,2},{4,5},{5,4},{6,7},{7,6},{8,9},{9,8},{10,11... | collective-permute-start | bytes 1572872 | tf_op jit(solution)/shard_map/ppermute | solution.py:279
  4.5 12.5 %collective-permute-start.5 = (bf16[1024,256]{1,0:T(8,128)(2,1)S(1)}, bf16[1024,256]{1,0:T(8,128)(2,1)S(1)}, u32[]{:S(2)}, u32[]{:S(2)}) collective-permute-start(bf16[1024,256]{1,0:T(8,128)(2,1)S(1)} %get-tuple-element.26), channel_id=1, source_target_pairs={{0,1},{1,0},{2,3},{3,2},{4,5},{5,4},{6,7},{7,6},{8,9},{9,8},{10,11... | collective-permute-start | bytes 1572872 | tf_op jit(solution)/shard_map/ppermute | solution.py:279
  5.0 14.0 %collective-permute-start.6 = (bf16[1024,256]{1,0:T(8,128)(2,1)S(1)}, bf16[1024,256]{1,0:T(8,128)(2,1)S(1)}, u32[]{:S(2)}, u32[]{:S(2)}) collective-permute-start(bf16[1024,256]{1,0:T(8,128)(2,1)S(1)} %get-tuple-element.28), channel_id=1, source_target_pairs={{0,1},{1,0},{2,3},{3,2},{4,5},{5,4},{6,7},{7,6},{8,9},{9,8},{10,11... | collective-permute-start | bytes 1572872 | tf_op jit(solution)/shard_map/ppermute | solution.py:279
  5.1 17.4 %collective-permute-start.12 = (bf16[1024,256]{1,0:T(8,128)(2,1)S(1)}, bf16[1024,256]{1,0:T(8,128)(2,1)S(1)}, u32[]{:S(2)}, u32[]{:S(2)}) collective-permute-start(bf16[1024,256]{1,0:T(8,128)(2,1)S(1)} %get-tuple-element.23.refs_0_), channel_id=1, source_target_pairs={{0,4},{5,1},{2,6},{7,3},{4,8},{9,5},{6,10},{11,7},{8,12},{13,9},{1... | collective-permute-start | bytes 1572872 | tf_op jit(solution)/shard_map/ppermute | solution.py:279
  10.0 12.5 %collective-permute-start.13 = (bf16[1024,256]{1,0:T(8,128)(2,1)S(1)}, bf16[1024,256]{1,0:T(8,128)(2,1)S(1)}, u32[]{:S(2)}, u32[]{:S(2)}) collective-permute-start(bf16[1024,256]{1,0:T(8,128)(2,1)S(1)} %collective-permute-done.4.refs_1_), channel_id=1, source_target_pairs={{0,4},{5,1},{2,6},{7,3},{4,8},{9,5},{6,10},{11,7},{8,12},{13,9},{1... | collective-permute-start | bytes 1572872 | tf_op jit(solution)/shard_map/ppermute | solution.py:279
  13.5 18.5 %collective-permute-start.1 = (bf16[1024,256]{1,0:T(8,128)(2,1)S(1)}, bf16[1024,256]{1,0:T(8,128)(2,1)S(1)}, u32[]{:S(2)}, u32[]{:S(2)}) collective-permute-start(bf16[1024,256]{1,0:T(8,128)(2,1)S(1)} %get-tuple-element.19.refs_0_.refs_2_), channel_id=1, source_target_pairs={{0,4},{5,1},{2,6},{7,3},{4,8},{9,5},{6,10},{11,7},{8,12},{13,9},{1... | collective-permute-start | bytes 1572872 | tf_op jit(solution)/shard_map/ppermute | solution.py:279
  17.0 17.2 %collective-permute-start.2 = (bf16[1024,256]{1,0:T(8,128)(2,1)S(1)}, bf16[1024,256]{1,0:T(8,128)(2,1)S(1)}, u32[]{:S(2)}, u32[]{:S(2)}) collective-permute-start(bf16[1024,256]{1,0:T(8,128)(2,1)S(1)} %collective-permute-done.refs_1_.refs_3_), channel_id=1, source_target_pairs={{0,4},{5,1},{2,6},{7,3},{4,8},{9,5},{6,10},{11,7},{8,12},{13,9},{1... | collective-permute-start | bytes 1572872 | tf_op jit(solution)/shard_map/ppermute | solution.py:279
  20.3 4.8 %copy-start.4 = (s32[1,8,2]{1,2,0:T(2,128)S(1)}, s32[1,8,2]{1,2,0:T(2,128)}, u32[]{:S(2)}) copy-start(s32[1,8,2]{1,2,0:T(2,128)} %param.7) | copy-start | bytes 196
  20.3 11.0 %copy-start.2 = (f32[1,1024]{1,0:T(1,128)S(1)}, f32[1,1024]{1,0:T(1,128)}, u32[]{:S(2)}) copy-start(f32[1,1024]{1,0:T(1,128)} %decays.3) | copy-start | bytes 12292
  20.4 11.0 %copy-start.3 = (f32[1,1024]{1,0:T(1,128)S(1)}, f32[1,1024]{1,0:T(1,128)}, u32[]{:S(2)}) copy-start(f32[1,1024]{1,0:T(1,128)} %mirrors.3) | copy-start | bytes 12292
  20.4 0.8 %collective-permute-start.7 = (f32[2,128,128]{2,1,0:T(8,128)S(1)}, f32[2,128,128]{2,1,0:T(8,128)S(1)}, u32[]{:S(2)}, u32[]{:S(2)}) collective-permute-start(f32[2,128,128]{2,1,0:T(8,128)S(1)} %get-tuple-element.30), channel_id=1, source_target_pairs={{12,14},{13,15},{14,12},{15,13},{28,30},{29,31},{30,28},{31,29}} | collective-permute-start | bytes 393224 | tf_op jit(solution)/shard_map/ppermute | solution.py:279
  21.2 10.1 %collective-permute-start.8 = (f32[2,128,128]{2,1,0:T(8,128)S(1)}, f32[2,128,128]{2,1,0:T(8,128)S(1)}, u32[]{:S(2)}, u32[]{:S(2)}) collective-permute-start(f32[2,128,128]{2,1,0:T(8,128)S(1)} %add.3.refs_2_), channel_id=1, source_target_pairs={{12,0},{14,2},{28,16},{30,18}} | collective-permute-start | bytes 393224 | tf_op jit(solution)/shard_map/ppermute | solution.py:279
  23.6 7.8 %collective-permute-start.14 = (f32[1,128,128]{2,1,0:T(8,128)S(1)}, f32[1,128,128]{2,1,0:T(8,128)S(1)}, u32[]{:S(2)}, u32[]{:S(2)}) collective-permute-start(f32[1,128,128]{2,1,0:T(8,128)S(1)} %get-tuple-element.32), channel_id=1, source_target_pairs={{0,2},{1,3},{2,0},{3,1},{4,6},{5,7},{6,4},{7,5},{8,10},{9,11},{10,... | collective-permute-start | bytes 196616 | tf_op jit(solution)/shard_map/ppermute | solution.py:279
  32.0 13.4 %collective-permute-start.15 = (f32[1,136,128]{2,1,0:T(8,128)S(1)}, f32[1,136,128]{2,1,0:T(8,128)S(1)}, u32[]{:S(2)}, u32[]{:S(2)}) collective-permute-start(f32[1,136,128]{2,1,0:T(8,128)S(1)} %shard_map.61.refs_0_), channel_id=1, source_target_pairs={{0,4},{1,5},{2,6},{3,7},{4,8},{5,9},{6,10},{7,11},{8,12},{9,13},{1... | collective-permute-start | bytes 208904 | tf_op jit(solution)/shard_map/ppermute | solution.py:279
  35.3 6.4 %collective-permute-start.3 = (f32[1,128,128]{2,1,0:T(8,128)S(1)}, f32[1,128,128]{2,1,0:T(8,128)S(1)}, u32[]{:S(2)}, u32[]{:S(2)}) collective-permute-start(f32[1,128,128]{2,1,0:T(8,128)S(1)} %get-tuple-element.22), channel_id=1, source_target_pairs={{0,2},{1,3},{2,0},{3,1},{4,6},{5,7},{6,4},{7,5},{8,10},{9,11},{10,... | collective-permute-start | bytes 196616 | tf_op jit(solution)/shard_map/ppermute | solution.py:279
  36.9 9.3 %collective-permute-start.16 = (f32[1,136,128]{2,1,0:T(8,128)S(1)}, f32[1,136,128]{2,1,0:T(8,128)S(1)}, u32[]{:S(2)}, u32[]{:S(2)}) collective-permute-start(f32[1,136,128]{2,1,0:T(8,128)S(1)} %shard_map.61.refs_0_), channel_id=1, source_target_pairs={{0,8},{1,9},{2,10},{3,11},{4,12},{5,13},{6,14},{7,15},{8,0},{9,1},... | collective-permute-start | bytes 208904 | tf_op jit(solution)/shard_map/ppermute | solution.py:279
  40.3 5.8 %collective-permute-start.17 = (f32[1,136,128]{2,1,0:T(8,128)S(1)}, f32[1,136,128]{2,1,0:T(8,128)S(1)}, u32[]{:S(2)}, u32[]{:S(2)}) collective-permute-start(f32[1,136,128]{2,1,0:T(8,128)S(1)} %shard_map.61.refs_0_), channel_id=1, source_target_pairs={{0,12},{1,13},{2,14},{3,15},{4,0},{5,1},{6,2},{7,3},{8,4},{9,5},{1... | collective-permute-start | bytes 208904 | tf_op jit(solution)/shard_map/ppermute | solution.py:279
  42.3 7.8 %collective-permute-start.10 = (f32[1,136,128]{2,1,0:T(8,128)S(1)}, f32[1,136,128]{2,1,0:T(8,128)S(1)}, u32[]{:S(2)}, u32[]{:S(2)}) collective-permute-start(f32[1,136,128]{2,1,0:T(8,128)S(1)} %shard_map.59.refs_0_), channel_id=1, source_target_pairs={{0,8},{1,9},{2,10},{3,11},{4,12},{5,13},{6,14},{7,15},{8,0},{9,1},... | collective-permute-start | bytes 208904 | tf_op jit(solution)/shard_map/ppermute | solution.py:279
  44.1 6.1 %collective-permute-start.11 = (f32[1,136,128]{2,1,0:T(8,128)S(1)}, f32[1,136,128]{2,1,0:T(8,128)S(1)}, u32[]{:S(2)}, u32[]{:S(2)}) collective-permute-start(f32[1,136,128]{2,1,0:T(8,128)S(1)} %shard_map.59.refs_0_), channel_id=1, source_target_pairs={{0,12},{1,13},{2,14},{3,15},{4,0},{5,1},{6,2},{7,3},{8,4},{9,5},{1... | collective-permute-start | bytes 208904 | tf_op jit(solution)/shard_map/ppermute | solution.py:279
  45.4 6.2 %collective-permute-start.9 = (f32[1,136,128]{2,1,0:T(8,128)S(1)}, f32[1,136,128]{2,1,0:T(8,128)S(1)}, u32[]{:S(2)}, u32[]{:S(2)}) collective-permute-start(f32[1,136,128]{2,1,0:T(8,128)S(1)} %shard_map.59.refs_0_), channel_id=1, source_target_pairs={{0,4},{1,5},{2,6},{3,7},{4,8},{5,9},{6,10},{7,11},{8,12},{9,13},{1... | collective-permute-start | bytes 208904 | tf_op jit(solution)/shard_map/ppermute | solution.py:279
